TPU v7x, 32 devices: a whole 2x2x4 slice. The times are simulated.
32 devices in a mesh: pb: 8 (over y, x, core), mem: 4 (over z).
Axes of the slice: x: 2, y: 2, z: 4, core: 2. Of those that a mesh axis runs over, the one named last changes fastest.
Arguments:
- hidden_in: bfloat16 [16, 1024, 1024], P('pb', 'mem'), may hold values from -6 to 6
- encoder_rows: bfloat16 [8, 12, 256, 1024], P('pb', 'mem'), may hold values from -6 to 6
- passage_map: int32 [16, 8], P('pb'), may hold values from 0 to 11, as said below
- self_qkv: bfloat16 [3, 1024, 1024], P(None, 'mem'), may hold values from -0.1875 to 0.1875
- self_out: bfloat16 [1024, 1024], P('mem'), may hold values from -0.75 to 0.75
- cross_qkv: bfloat16 [3, 1024, 1024], P(None, 'mem'), may hold values from -0.1875 to 0.1875
- cross_out: bfloat16 [1024, 1024], P('mem'), may hold values from -0.75 to 0.75
- ffn_in: bfloat16 [1024, 4096], P('mem'), may hold values from -0.1875 to 0.1875
- ffn_out: bfloat16 [4096, 1024], P('mem'), may hold values from -0.09375 to 0.09375
- ffn_in_bias: bfloat16 [4096], P('mem'), may hold values from -3 to 3
- biases: bfloat16 [10, 1024], P(None, 'mem'), may hold values from -3 to 3
- gains: bfloat16 [3, 1024], P(None, 'mem'), may hold values from 0.5 to 1.5
- cotangent: bfloat16 [16, 1024, 1024], P('pb', 'mem'), may hold values from -6 to 6
Outputs:
- layer_out: bfloat16 [16, 1024, 1024], P('pb', 'mem')
- grad_in: float32 [16, 1024, 1024], P('pb', 'mem')
- grad_encoder: float32 [8, 12, 256, 1024], P('pb', 'mem')
- grad_self_qkv: float32 [3, 1024, 1024], P(None, 'mem')
- grad_self_out: float32 [1024, 1024], P('mem')
- grad_cross_qkv: float32 [3, 1024, 1024], P(None, 'mem')
- grad_cross_out: float32 [1024, 1024], P('mem')
- grad_ffn_in: float32 [1024, 4096], P('mem')
- grad_ffn_out: float32 [4096, 1024], P('mem')
- grad_ffn_in_bias: float32 [4096], P('mem')
- grad_biases: float32 [10, 1024], P(None, 'mem')
- grad_gains: float32 [3, 1024], P(None, 'mem')
Inputs may be any that keep to these rules, and one draw needn't show every extreme that they name: `passage_map`: each question names 8 different passages of its own pb index, numbered within that index; every passage of an index is named by some question.
All inputs are finite; a program needn't handle non-finite values.
Results may differ from a plain program's by a relative error of at most 0.025.
Values may be sent and summed in bfloat16 or wider, within the bound.
A program may use at most 320 MiB of HBM per device.

v0:
```python
import jax
import jax.numpy as jnp
from jax import lax
from jax.sharding import PartitionSpec as P

HD = 64
PLEN = 256


def layer_norm(values, gain, shift):
    centre = values - jnp.mean(values, axis=-1, keepdims=True)
    spread = jnp.mean(centre * centre, axis=-1, keepdims=True)
    return centre * lax.rsqrt(spread + 1e-05) * gain + shift


def gelu_exact(values):
    return jax.nn.gelu(values, approximate=False)


def head_slices(queries4, keys4, values4, first):
    query_part = lax.dynamic_slice_in_dim(queries4, first, 4, 2)
    key_part = lax.dynamic_slice_in_dim(keys4, first, 4, keys4.ndim - 2)
    value_part = lax.dynamic_slice_in_dim(values4, first, 4, values4.ndim - 2)
    return (query_part, key_part, value_part)


def block_scores(query_part, key_part, allowed, shared):
    if shared:
        scores = jnp.einsum(
            "bqhe,khe->bhqk", query_part, key_part, preferred_element_type=jnp.float32
        )
    else:
        scores = jnp.einsum(
            "bqhe,bkhe->bhqk", query_part, key_part, preferred_element_type=jnp.float32
        )
    return jnp.where(allowed[:, None], scores, -1000000000.0)


def attend_forward(queries4, keys4, values4, allowed, shared):
    groups = queries4.shape[2] // 4

    def one_block(block_index):
        query_part, key_part, value_part = head_slices(queries4, keys4, values4, block_index * 4)
        scores = block_scores(query_part, key_part, allowed, shared)
        largest = jnp.max(scores, axis=-1, keepdims=True)
        expo = jnp.exp(scores - largest)
        total = jnp.sum(expo, axis=-1, keepdims=True)
        probs_low = (expo / total).astype(jnp.bfloat16)
        log_total = (largest + jnp.log(total))[..., 0]
        if shared:
            mixed = jnp.einsum(
                "bhqk,khe->bqhe", probs_low, value_part, preferred_element_type=jnp.float32
            )
        else:
            mixed = jnp.einsum(
                "bhqk,bkhe->bqhe", probs_low, value_part, preferred_element_type=jnp.float32
            )
        return (mixed, log_total)

    mixed, log_total = lax.map(one_block, jnp.arange(groups))
    batch, rows = (queries4.shape[0], queries4.shape[1])
    return (mixed.transpose(1, 2, 0, 3, 4).reshape(batch * rows, -1), log_total)


def attend_backward(queries4, keys4, values4, allowed, log_total, grad_mixed4, shared):
    groups = queries4.shape[2] // 4

    def one_block(block_index):
        first = block_index * 4
        query_part, key_part, value_part = head_slices(queries4, keys4, values4, first)
        grad_part = lax.dynamic_slice_in_dim(grad_mixed4, first, 4, 2)
        scores = block_scores(query_part, key_part, allowed, shared)
        probs = jnp.exp(scores - log_total[block_index][..., None])
        probs_low = probs.astype(jnp.bfloat16)
        if shared:
            grad_values = jnp.einsum(
                "bhqk,bqhe->khe", probs_low, grad_part, preferred_element_type=jnp.float32
            )
            grad_probs = jnp.einsum(
                "bqhe,khe->bhqk", grad_part, value_part, preferred_element_type=jnp.float32
            )
        else:
            grad_values = jnp.einsum(
                "bhqk,bqhe->bkhe", probs_low, grad_part, preferred_element_type=jnp.float32
            )
            grad_probs = jnp.einsum(
                "bqhe,bkhe->bhqk", grad_part, value_part, preferred_element_type=jnp.float32
            )
        grad_scores = probs * (grad_probs - jnp.sum(probs * grad_probs, axis=-1, keepdims=True))
        grad_low = grad_scores.astype(jnp.bfloat16)
        if shared:
            grad_queries = jnp.einsum(
                "bhqk,khe->bqhe", grad_low, key_part, preferred_element_type=jnp.float32
            )
            grad_keys = jnp.einsum(
                "bhqk,bqhe->khe", grad_low, query_part, preferred_element_type=jnp.float32
            )
        else:
            grad_queries = jnp.einsum(
                "bhqk,bkhe->bqhe", grad_low, key_part, preferred_element_type=jnp.float32
            )
            grad_keys = jnp.einsum(
                "bhqk,bqhe->bkhe", grad_low, query_part, preferred_element_type=jnp.float32
            )
        return (grad_queries, grad_keys, grad_values)

    grad_queries, grad_keys, grad_values = lax.map(one_block, jnp.arange(groups))
    batch, rows = (queries4.shape[0], queries4.shape[1])
    grad_queries = grad_queries.transpose(1, 2, 0, 3, 4).reshape(batch * rows, -1)
    if shared:
        grad_keys = grad_keys.transpose(1, 0, 2, 3).reshape(grad_keys.shape[1], -1)
        grad_values = grad_values.transpose(1, 0, 2, 3).reshape(grad_values.shape[1], -1)
    else:
        grad_keys = grad_keys.transpose(1, 2, 0, 3, 4).reshape(batch, grad_keys.shape[2], -1)
        grad_values = grad_values.transpose(1, 2, 0, 3, 4).reshape(batch, grad_values.shape[2], -1)
    return (grad_queries, grad_keys, grad_values)


def body(
    hidden_in,
    encoder_rows,
    passage_map,
    self_qkv,
    self_out,
    cross_qkv,
    cross_out,
    ffn_in,
    ffn_out,
    ffn_in_bias,
    biases,
    gains,
    cotangent,
):
    group_size = lax.axis_size("mem")
    member_index = lax.axis_index("mem")
    (
        w_self,
        w_self_out,
        w_cross,
        w_cross_out,
        w_ffn_in,
        w_ffn_out,
        ffn_bias_full,
        bias_rows,
        gain_rows,
    ) = (
        lax.all_gather(self_qkv, "mem", axis=1, tiled=True),
        lax.all_gather(self_out, "mem", axis=0, tiled=True),
        lax.all_gather(cross_qkv, "mem", axis=1, tiled=True),
        lax.all_gather(cross_out, "mem", axis=0, tiled=True),
        lax.all_gather(ffn_in, "mem", axis=0, tiled=True),
        lax.all_gather(ffn_out, "mem", axis=0, tiled=True),
        lax.all_gather(ffn_in_bias, "mem", axis=0, tiled=True),
        lax.all_gather(biases, "mem", axis=1, tiled=True),
        lax.all_gather(gains, "mem", axis=1, tiled=True),
    )
    bias_float = bias_rows.astype(jnp.float32)
    gain_float = gain_rows.astype(jnp.float32)
    questions, seg_rows, width = hidden_in.shape
    heads = width // HD
    tok_rows = questions * seg_rows
    flat_in = hidden_in.reshape(tok_rows, width)
    projected = jnp.einsum("te,ieo->tio", flat_in, w_self, preferred_element_type=jnp.float32)
    self_queries = ((projected[:, 0] + bias_float[0]) * 0.125).astype(jnp.bfloat16)
    self_keys_low = projected[:, 1].astype(jnp.bfloat16)
    self_values_low = (projected[:, 2] + bias_float[1]).astype(jnp.bfloat16)
    keys_all, values_all = (
        lax.all_gather(
            self_keys_low.reshape(questions, seg_rows, width), "mem", axis=1, tiled=True
        ),
        lax.all_gather(
            self_values_low.reshape(questions, seg_rows, width), "mem", axis=1, tiled=True
        ),
    )
    full_len = keys_all.shape[1]
    query_pos = member_index * seg_rows + jnp.arange(seg_rows, dtype=jnp.int32)
    key_pos = jnp.arange(full_len, dtype=jnp.int32)
    self_mask = (key_pos[None, :] <= query_pos[:, None])[None]
    self_q4 = self_queries.reshape(questions, seg_rows, heads, HD)
    self_k4 = keys_all.reshape(questions, full_len, heads, HD)
    self_v4 = values_all.reshape(questions, full_len, heads, HD)
    self_mixed, self_lse = attend_forward(self_q4, self_k4, self_v4, self_mask, False)
    self_attended = self_mixed.astype(jnp.bfloat16)
    self_branch = (
        jnp.dot(self_attended, w_self_out, preferred_element_type=jnp.float32) + bias_float[2]
    )
    first_norm, first_back = jax.vjp(
        layer_norm, flat_in.astype(jnp.float32) + self_branch, gain_float[0], bias_float[6]
    )
    first_low = first_norm.astype(jnp.bfloat16)
    cross_queries = (
        (jnp.dot(first_low, w_cross[0], preferred_element_type=jnp.float32) + bias_float[3]) * 0.125
    ).astype(jnp.bfloat16)
    enc_local = encoder_rows.reshape(-1, width)
    memory_proj = jnp.einsum(
        "te,ieo->tio", enc_local, w_cross[1:3], preferred_element_type=jnp.float32
    )
    memory_keys_low = memory_proj[:, 0].astype(jnp.bfloat16)
    memory_values_low = (memory_proj[:, 1] + bias_float[4]).astype(jnp.bfloat16)
    memory_keys_all, memory_values_all = (
        lax.all_gather(memory_keys_low, "mem", axis=0, tiled=True),
        lax.all_gather(memory_values_low, "mem", axis=0, tiled=True),
    )
    units = encoder_rows.shape[1] * group_size
    member = jnp.any(
        passage_map[:, :, None] == jnp.arange(units, dtype=jnp.int32)[None, None, :], axis=1
    )
    key_mask = jnp.repeat(member, PLEN, axis=1)[:, None, :]
    memory_rows = memory_keys_all.shape[0]
    cross_q4 = cross_queries.reshape(questions, seg_rows, heads, HD)
    cross_k4 = memory_keys_all.reshape(memory_rows, heads, HD)
    cross_v4 = memory_values_all.reshape(memory_rows, heads, HD)
    cross_mixed, cross_lse = attend_forward(cross_q4, cross_k4, cross_v4, key_mask, True)
    cross_attended = cross_mixed.astype(jnp.bfloat16)
    cross_branch = (
        jnp.dot(cross_attended, w_cross_out, preferred_element_type=jnp.float32) + bias_float[5]
    )
    second_norm, second_back = jax.vjp(
        layer_norm, first_norm + cross_branch, gain_float[1], bias_float[7]
    )
    second_low = second_norm.astype(jnp.bfloat16)
    hidden_pre = jnp.dot(
        second_low, w_ffn_in, preferred_element_type=jnp.float32
    ) + ffn_bias_full.astype(jnp.float32)
    activated, gelu_back = jax.vjp(gelu_exact, hidden_pre)
    activated_low = activated.astype(jnp.bfloat16)
    ffn_branch = (
        jnp.dot(activated_low, w_ffn_out, preferred_element_type=jnp.float32) + bias_float[9]
    )
    final_norm, final_back = jax.vjp(
        layer_norm, second_norm + ffn_branch, gain_float[2], bias_float[8]
    )
    layer_out = final_norm.astype(jnp.bfloat16).reshape(questions, seg_rows, width)
    grad_out = cotangent.reshape(tok_rows, width).astype(jnp.float32)
    grad_third, grad_gain_third, grad_shift_third = final_back(grad_out)
    grad_ffn_branch = grad_third.astype(jnp.bfloat16)
    grad_bias_ffn_out = jnp.sum(grad_ffn_branch.astype(jnp.float32), axis=0)
    grad_activated = jnp.einsum(
        "td,fd->tf", grad_ffn_branch, w_ffn_out, preferred_element_type=jnp.float32
    )
    (grad_hidden,) = gelu_back(grad_activated)
    grad_hidden_low = grad_hidden.astype(jnp.bfloat16)
    grad_w_ffn_in = jnp.einsum(
        "te,tf->ef", second_low, grad_hidden_low, preferred_element_type=jnp.float32
    )
    grad_ffn_bias = jnp.sum(grad_hidden_low.astype(jnp.float32), axis=0)
    grad_second = grad_third + jnp.einsum(
        "tf,ef->te", grad_hidden_low, w_ffn_in, preferred_element_type=jnp.float32
    )
    grad_mid, grad_gain_mid, grad_shift_mid = second_back(grad_second)
    grad_cross_branch = grad_mid.astype(jnp.bfloat16)
    grad_w_cross_out = jnp.einsum(
        "td,te->de", cross_attended, grad_cross_branch, preferred_element_type=jnp.float32
    )
    grad_bias_cross_out = jnp.sum(grad_cross_branch.astype(jnp.float32), axis=0)
    grad_cross_attended = jnp.einsum(
        "te,de->td", grad_cross_branch, w_cross_out, preferred_element_type=jnp.float32
    ).astype(jnp.bfloat16)
    grad_cross_q, grad_memory_keys, grad_memory_values = attend_backward(
        cross_q4,
        cross_k4,
        cross_v4,
        key_mask,
        cross_lse,
        grad_cross_attended.reshape(questions, seg_rows, heads, HD),
        True,
    )
    own_memory_keys, own_memory_values = (
        lax.psum_scatter(
            grad_memory_keys.astype(jnp.bfloat16), "mem", scatter_dimension=0, tiled=True
        ).astype(jnp.float32),
        lax.psum_scatter(
            grad_memory_values.astype(jnp.bfloat16), "mem", scatter_dimension=0, tiled=True
        ).astype(jnp.float32),
    )
    memory_grads = jnp.stack(
        [own_memory_keys.astype(jnp.bfloat16), own_memory_values.astype(jnp.bfloat16)], axis=1
    )
    grad_cross_q_low = grad_cross_q.astype(jnp.bfloat16) * jnp.bfloat16(0.125)
    grad_w_cross_q = jnp.einsum(
        "te,to->eo", first_low, grad_cross_q_low, preferred_element_type=jnp.float32
    )
    grad_w_cross_kv = jnp.einsum(
        "te,tio->ieo", enc_local, memory_grads, preferred_element_type=jnp.float32
    )
    grad_w_cross = jnp.concatenate([grad_w_cross_q[None], grad_w_cross_kv], axis=0)
    grad_bias_cross_q = jnp.sum(grad_cross_q_low.astype(jnp.float32), axis=0)
    grad_bias_cross_v = jnp.sum(memory_grads[:, 1].astype(jnp.float32), axis=0)
    grad_encoder = jnp.einsum(
        "tio,ieo->te", memory_grads, w_cross[1:3], preferred_element_type=jnp.float32
    ).reshape(encoder_rows.shape)
    grad_first = grad_mid + jnp.einsum(
        "to,eo->te", grad_cross_q_low, w_cross[0], preferred_element_type=jnp.float32
    )
    grad_low_first, grad_gain_first, grad_shift_first = first_back(grad_first)
    grad_self_branch = grad_low_first.astype(jnp.bfloat16)
    grad_w_self_out = jnp.einsum(
        "td,te->de", self_attended, grad_self_branch, preferred_element_type=jnp.float32
    )
    grad_bias_self_out = jnp.sum(grad_self_branch.astype(jnp.float32), axis=0)
    grad_self_attended = jnp.einsum(
        "te,de->td", grad_self_branch, w_self_out, preferred_element_type=jnp.float32
    ).astype(jnp.bfloat16)
    grad_self_q, grad_self_keys, grad_self_values = attend_backward(
        self_q4,
        self_k4,
        self_v4,
        self_mask,
        self_lse,
        grad_self_attended.reshape(questions, seg_rows, heads, HD),
        False,
    )
    own_self_keys, own_self_values = (
        lax.psum_scatter(
            grad_self_keys.astype(jnp.bfloat16), "mem", scatter_dimension=1, tiled=True
        ).astype(jnp.float32),
        lax.psum_scatter(
            grad_self_values.astype(jnp.bfloat16), "mem", scatter_dimension=1, tiled=True
        ).astype(jnp.float32),
    )
    grad_self_q_low = grad_self_q.astype(jnp.bfloat16) * jnp.bfloat16(0.125)
    self_grads = jnp.stack(
        [
            grad_self_q_low,
            own_self_keys.reshape(tok_rows, width).astype(jnp.bfloat16),
            own_self_values.reshape(tok_rows, width).astype(jnp.bfloat16),
        ],
        axis=1,
    )
    grad_in = (
        grad_low_first
        + jnp.einsum("tio,ieo->te", self_grads, w_self, preferred_element_type=jnp.float32)
    ).reshape(questions, seg_rows, width)
    grad_bias_self_q = jnp.sum(self_grads[:, 0].astype(jnp.float32), axis=0)
    grad_bias_self_v = jnp.sum(self_grads[:, 2].astype(jnp.float32), axis=0)
    grad_w_ffn_out = jnp.einsum(
        "tf,td->fd", activated_low, grad_ffn_branch, preferred_element_type=jnp.float32
    )
    grad_w_self = jnp.einsum("te,tio->ieo", flat_in, self_grads, preferred_element_type=jnp.float32)
    grad_bias_rows = jnp.stack(
        [
            grad_bias_self_q,
            grad_bias_self_v,
            grad_bias_self_out,
            grad_bias_cross_q,
            grad_bias_cross_v,
            grad_bias_cross_out,
            grad_shift_first,
            grad_shift_mid,
            grad_shift_third,
            grad_bias_ffn_out,
        ],
        axis=0,
    )
    grad_gain_rows = jnp.stack([grad_gain_first, grad_gain_mid, grad_gain_third], axis=0)
    local_sums = (
        lax.psum_scatter(
            grad_w_self.astype(jnp.bfloat16), "mem", scatter_dimension=1, tiled=True
        ).astype(jnp.float32),
        lax.psum_scatter(
            grad_w_self_out.astype(jnp.bfloat16), "mem", scatter_dimension=0, tiled=True
        ).astype(jnp.float32),
        lax.psum_scatter(
            grad_w_cross.astype(jnp.bfloat16), "mem", scatter_dimension=1, tiled=True
        ).astype(jnp.float32),
        lax.psum_scatter(
            grad_w_cross_out.astype(jnp.bfloat16), "mem", scatter_dimension=0, tiled=True
        ).astype(jnp.float32),
        lax.psum_scatter(
            grad_w_ffn_in.astype(jnp.bfloat16), "mem", scatter_dimension=0, tiled=True
        ).astype(jnp.float32),
        lax.psum_scatter(
            grad_w_ffn_out.astype(jnp.bfloat16), "mem", scatter_dimension=0, tiled=True
        ).astype(jnp.float32),
        lax.psum_scatter(
            grad_ffn_bias.astype(jnp.bfloat16), "mem", scatter_dimension=0, tiled=True
        ).astype(jnp.float32),
        lax.psum_scatter(
            grad_bias_rows.astype(jnp.bfloat16), "mem", scatter_dimension=1, tiled=True
        ).astype(jnp.float32),
        lax.psum_scatter(
            grad_gain_rows.astype(jnp.bfloat16), "mem", scatter_dimension=1, tiled=True
        ).astype(jnp.float32),
    )
    totals = lax.psum(
        (
            local_sums[0],
            local_sums[1],
            local_sums[2],
            local_sums[3],
            local_sums[4],
            local_sums[5],
            local_sums[6],
            local_sums[7],
            local_sums[8],
        ),
        "pb",
    )
    return (
        layer_out,
        grad_in,
        grad_encoder,
        totals[0],
        totals[1],
        totals[2],
        totals[3],
        totals[4],
        totals[5],
        totals[6],
        totals[7],
        totals[8],
    )


def solution(mesh):
    placed = (
        P("pb", "mem", None),
        P("pb", "mem", None, None),
        P("pb", None),
        P(None, "mem", None),
        P("mem", None),
        P(None, "mem", None),
        P("mem", None),
        P("mem", None),
        P("mem", None),
        P("mem"),
        P(None, "mem"),
        P(None, "mem"),
        P("pb", "mem", None),
    )
    return jax.shard_map(
        body,
        mesh=mesh,
        in_specs=placed,
        out_specs=(
            P("pb", "mem", None),
            P("pb", "mem", None),
            P("pb", "mem", None, None),
            P(None, "mem", None),
            P("mem", None),
            P(None, "mem", None),
            P("mem", None),
            P("mem", None),
            P("mem", None),
            P("mem"),
            P(None, "mem"),
            P(None, "mem"),
        ),
        check_vma=False,
    )
```

profile of v0, /device:TPU:0, one launch (start us, length us, event | category | flops | bytes accessed | tf_op | source)
XLA Modules:
  0.0 2936.5 jit_solution(5343339522504366061)
XLA Ops:
  8.7 15.0 all_gather.40
  24.4 103.3 %all-gather.12.cloned.1.call-done = bf16[3,1024,1024]{2,1,0:T(8,128)(2,1)} async-done(((bf16[3,256,1024]{2,1,0:T(8,128)(2,1)}), bf16[3,1024,1024]{2,1,0:T(8,128)(2,1)}) %all-gather.12.cloned.1.call-update) | async-done | bytes 6291472 | tf_op jit(solution)/shard_map/all_gather | solution.py:147
  142.0 100.8 %all-gather.20.cloned.1.call-done = bf16[3,1024,1024]{2,1,0:T(8,128)(2,1)} async-done(((bf16[3,256,1024]{2,1,0:T(8,128)(2,1)}), bf16[3,1024,1024]{2,1,0:T(8,128)(2,1)}) %all-gather.20.cloned.1.call-update) | async-done | bytes 6291472 | tf_op jit(solution)/shard_map/all_gather | solution.py:149
  258.2 12.0 all_gather.44
  271.5 12.2 all_gather.50
  293.6 30.7 %all-gather.14.cloned.1.call-done = bf16[2,1024,1024]{2,1,0:T(8,128)(2,1)} async-done(((bf16[2,256,1024]{2,1,0:T(8,128)(2,1)}), bf16[2,1024,1024]{2,1,0:T(8,128)(2,1)}) %all-gather.14.cloned.1.call-update) | async-done | bytes 4194320 | tf_op jit(solution)/shard_map/all_gather | solution.py:171
  330.4 75.1 %all-gather.16.cloned.1.call-done = bf16[2,1024,1024]{2,1,0:T(8,128)(2,1)} async-done(((bf16[2,256,1024]{2,1,0:T(8,128)(2,1)}), bf16[2,1024,1024]{2,1,0:T(8,128)(2,1)}) %all-gather.16.cloned.1.call-update) | async-done | bytes 4194320 | tf_op jit(solution)/shard_map/all_gather | solution.py:168
  412.8 45.2 %while.56 = (s32[]{:T(128)}, bf16[4,2,256,4,64]{2,4,3,1,0:T(8,128)(2,1)}, f32[4,2,4,256]{3,2,1,0:T(4,128)}, s32[4]{0:T(128)S(1)}, bf16[2,1024,16,64]{1,3,2,0:T(8...) while((s32[]{:T(128)}, ...), condition=%wide.region_3.4_spmd.clone, body=%wide.region_0.3_spmd.clone.sunk | while | flops 556005376 | bytes 29166772 | solution.py:60
  475.1 92.5 %all-gather.22.cloned.1.call-done = bf16[3072,1024]{1,0:T(8,128)(2,1)} async-done(((bf16[768,1024]{1,0:T(8,128)(2,1)}), bf16[3072,1024]{1,0:T(8,128)(2,1)}) %all-gather.22.cloned.1.call-update) | async-done | bytes 6291472 | tf_op jit(solution)/shard_map/all_gather | solution.py:202
  576.3 107.0 %all-gather.30.cloned.1.call-done = bf16[3072,1,1024]{2,0,1:T(8,128)(2,1)} async-done(((bf16[768,1,1024]{2,0,1:T(8,128)(2,1)}), bf16[3072,1,1024]{2,0,1:T(8,128)(2,1)}) %all-gather.30.cloned.1.call-update) | async-done | bytes 6291472 | tf_op jit(solution)/shard_map/all_gather | solution.py:201
  692.1 152.0 %while.57 = (s32[]{:T(128)}, bf16[4,2,256,4,64]{2,4,1,3,0:T(8,128)(2,1)}, f32[4,2,4,256]{3,1,2,0:T(2,128)}, s32[4]{0:T(128)S(1)}, bf16[3072,16,64]{0,2,1:T(8,128...) while((s32[]{:T(128)}, ...), condition=%wide.region_10.11_spmd.clone, body=%wide.region_7.10_spmd.clone.sunk | while | flops 1667233792 | bytes 180203760 | solution.py:60
  694.3 12.1 fusion.221
  731.8 13.6 fusion.221
  770.9 12.2 fusion.221
  808.5 12.1 fusion.221
  853.5 25.6 all-gather.26.cloned.1.call-done
  879.1 28.4 multiply_convert_fusion.1
  907.5 120.9 %all-gather.28.cloned.1.call-done = bf16[4096,1024]{1,0:T(8,128)(2,1)} async-done(((bf16[1024,1024]{1,0:T(8,128)(2,1)}), bf16[4096,1024]{1,0:T(8,128)(2,1)}) %all-gather.28.cloned.1.call-update) | async-done | bytes 8388624 | tf_op jit(solution)/shard_map/all_gather | solution.py:152
  1042.9 15.9 fusion.140
  1082.9 338.5 %while.58 = (s32[]{:T(128)}, bf16[4,2,256,4,64]{2,4,3,1,0:T(8,128)(2,1)}, bf16[4,3072,4,64]{1,3,2,0:T(8,128)(2,1)}, bf16[4,3072,4,64]{1,3,2,0:T(8,128)(2,1)}, s3...) while((s32[]{:T(128)}, ...), condition=%wide.region_21.22_spmd.clone, body=%wide.region_19.21_spmd.clone.sunk | while | flops 4102027264 | bytes 201686800 | solution.py:107
  1084.4 11.6 fusion.232
  1099.4 16.9 fusion.233
  1116.3 21.6 fusion.234
  1155.5 12.1 fusion.237
  1168.8 11.6 fusion.232
  1183.8 16.8 fusion.233
  1200.7 21.6 fusion.234
  1239.9 12.1 fusion.237
  1253.3 11.6 fusion.232
  1268.3 16.9 fusion.233
  1285.2 21.6 fusion.234
  1324.6 12.1 fusion.237
  1352.9 16.8 fusion.233
  1369.8 21.6 fusion.234
  1409.0 12.0 fusion.237
  1442.3 114.2 %while.59 = (s32[]{:T(128)}, bf16[4,2,256,4,64]{2,4,3,1,0:T(8,128)(2,1)}, bf16[4,2,1024,4,64]{2,4,3,0,1:T(8,128)(2,1)}, bf16[4,2,1024,4,64]{2,4,3,0,1:T(8,128)(2...) while((s32[]{:T(128)}, ...), condition=%wide.region_26.27_spmd.clone, body=%wide.region_24.26_spmd.clone.sunk | while | flops 1367603200 | bytes 106492768 | solution.py:107
  1587.0 44.7 %reduce-scatter.17.cloned.1.call-done = bf16[2,256,1024]{1,2,0:T(8,128)(2,1)} async-done(((bf16[2,1024,1024]{1,2,0:T(8,128)(2,1)}), bf16[2,256,1024]{1,2,0:T(8,128)(2,1)}) %reduce-scatter.17.cloned.1.call-update) | async-done | bytes 1048592 | tf_op jit(solution)/shard_map/reduce_scatter | solution.py:317
  1633.2 112.1 %reduce-scatter.21.cloned.1.call-done = bf16[768,1024]{1,0:T(8,128)(2,1)} async-done(((bf16[3072,1024]{1,0:T(8,128)(2,1)}), bf16[768,1024]{1,0:T(8,128)(2,1)}) %reduce-scatter.21.cloned.1.call-update) | async-done | bytes 1572880 | tf_op jit(solution)/shard_map/reduce_scatter | solution.py:272
  1779.5 45.5 %reduce-scatter.15.cloned.1.call-done = bf16[2,256,1024]{1,2,0:T(8,128)(2,1)} async-done(((bf16[2,1024,1024]{1,2,0:T(8,128)(2,1)}), bf16[2,256,1024]{1,2,0:T(8,128)(2,1)}) %reduce-scatter.15.cloned.1.call-update) | async-done | bytes 1048592 | tf_op jit(solution)/shard_map/reduce_scatter | solution.py:314
  1845.1 93.3 %reduce-scatter.19.cloned.1.call-done = bf16[768,1024]{1,0:T(8,128)(2,1)} async-done(((bf16[3072,1024]{1,0:T(8,128)(2,1)}), bf16[768,1024]{1,0:T(8,128)(2,1)}) %reduce-scatter.19.cloned.1.call-update) | async-done | bytes 1572880 | tf_op jit(solution)/shard_map/reduce_scatter | solution.py:269
  1948.8 11.6 all-reduce
  1961.9 44.2 %reduce-scatter.25.cloned.1.call-done = bf16[256,1024]{1,0:T(8,128)(2,1)} async-done(((bf16[1024,1024]{1,0:T(8,128)(2,1)}), bf16[256,1024]{1,0:T(8,128)(2,1)}) %reduce-scatter.25.cloned.1.call-update) | async-done | bytes 524304 | tf_op jit(solution)/shard_map/reduce_scatter | solution.py:360
  2006.1 46.0 %reduce-scatter.29.cloned.1.call-done = bf16[256,1024]{1,0:T(8,128)(2,1)} async-done(((bf16[1024,1024]{1,0:T(8,128)(2,1)}), bf16[256,1024]{1,0:T(8,128)(2,1)}) %reduce-scatter.29.cloned.1.call-update) | async-done | bytes 524304 | tf_op jit(solution)/shard_map/reduce_scatter | solution.py:366
  2072.5 145.0 %reduce-scatter.31.cloned.1.call-done = bf16[256,4096]{1,0:T(8,128)(2,1)} async-done(((bf16[1024,4096]{1,0:T(8,128)(2,1)}), bf16[256,4096]{1,0:T(8,128)(2,1)}) %reduce-scatter.31.cloned.1.call-update) | async-done | bytes 2097168 | tf_op jit(solution)/shard_map/reduce_scatter | solution.py:369
  2217.5 147.4 %reduce-scatter.33.cloned.1.call-done = bf16[1024,1024]{1,0:T(8,128)(2,1)} async-done(((bf16[4096,1024]{1,0:T(8,128)(2,1)}), bf16[1024,1024]{1,0:T(8,128)(2,1)}) %reduce-scatter.33.cloned.1.call-update) | async-done | bytes 2097168 | tf_op jit(solution)/shard_map/reduce_scatter | solution.py:372
  2365.0 113.8 %reduce-scatter.23.cloned.1.call-done = bf16[3,256,1024]{1,2,0:T(8,128)(2,1)} async-done(((bf16[3,1024,1024]{1,2,0:T(8,128)(2,1)}), bf16[3,256,1024]{1,2,0:T(8,128)(2,1)}) %reduce-scatter.23.cloned.1.call-update) | async-done | bytes 1572880 | tf_op jit(solution)/shard_map/reduce_scatter | solution.py:357
  2478.8 113.6 %reduce-scatter.27.cloned.1.call-done = bf16[3,256,1024]{1,2,0:T(8,128)(2,1)} async-done(((bf16[3,1024,1024]{1,2,0:T(8,128)(2,1)}), bf16[3,256,1024]{1,2,0:T(8,128)(2,1)}) %reduce-scatter.27.cloned.1.call-update) | async-done | bytes 1572880 | tf_op jit(solution)/shard_map/reduce_scatter | solution.py:363
  2592.4 330.0 %all-reduce.3 = (f32[3,256,1024]{1,2,0:T(8,128)}, f32[256,1024]{1,0:T(8,128)}, f32[3,256,1024]{1,2,0:T(8,128)}, f32[256,1024]{1,0:T(8,128)}, f32[256,4096]{1,0:T...) all-reduce(bf16[3,256,1024]{1,2,0:T(8,128)(2,1)} %reduce-scatter.23, ...), channel_id=1, replica_groups=mesh['pb'=8,'mem'=4] {'pb'}, use_global_device_ids=true, to_apply=%region_32.33 | all-reduce | flops 4198656 | bytes 25193984 | tf_op jit(solution)/shard_map/psum | solution.py:385
  (469 shorter events, 619.6 us)
Async XLA Ops:
  7.2 235.7 %copy-start = (bf16[1,3,256,1024]{3,2,1,0:T(8,128)(2,1)S(1)}, bf16[1,3,256,1024]{3,2,1,0:T(8,128)(2,1)}, u32[]{:S(2)}) copy-start(bf16[1,3,256,1024]{3,2,1,0:T(8,128)(2,1)} %param.22) | copy-start | bytes 4718596
  7.2 120.5 %all-gather.12.cloned.1.call-start = ((), (), s32[]{:S(2)}) async-start(), calls=%async_computation.12 | async-start | bytes 7864320 | tf_op jit(solution)/shard_map/all_gather | solution.py:147
  7.9 234.9 %all-gather.20.cloned.1.call-start = ((), (), s32[]{:S(2)}) async-start(), calls=%async_computation.16 | async-start | bytes 7864320 | tf_op jit(solution)/shard_map/all_gather | solution.py:149
  8.7 315.6 %all-gather.14.cloned.1.call-start = ((), (), s32[]{:S(2)}) async-start(), calls=%async_computation.13 | async-start | bytes 5242880 | tf_op jit(solution)/shard_map/all_gather | solution.py:171
  24.4 442.9 %copy-start.59 = (f32[1,1024]{1,0:T(1,128)}, f32[1,1024]{1,0:T(1,128)S(1)}, u32[]{:S(2)}) copy-start(f32[1,1024]{1,0:T(1,128)S(1)} %get-tuple-element.642) | copy-start | bytes 12292
  138.4 267.2 %all-gather.16.cloned.1.call-start = ((), (), s32[]{:S(2)}) async-start(), calls=%async_computation.14 | async-start | bytes 5242880 | tf_op jit(solution)/shard_map/all_gather | solution.py:168
  141.3 320.7 %all-gather.18.cloned.1.call-start = ((), (), s32[]{:S(2)}) async-start(), calls=%async_computation.15 | async-start | bytes 2621440 | tf_op jit(solution)/shard_map/all_gather | solution.py:148
  141.9 425.6 %all-gather.22.cloned.1.call-start = ((), (), s32[]{:S(2)}) async-start(), calls=%async_computation.17 | async-start | bytes 7864320 | tf_op jit(solution)/shard_map/all_gather | solution.py:202
  252.3 18.5 copy-start.72
  252.3 19.2 copy-start.67
  252.3 431.0 %all-gather.30.cloned.1.call-start = ((), (), s32[]{:S(2)}) async-start(), calls=%async_computation.32 | async-start | bytes 7864320 | tf_op jit(solution)/shard_map/all_gather | solution.py:201
  255.9 591.7 %all-gather.24.cloned.1.call-start = ((), (), s32[]{:S(2)}) async-start(), calls=%async_computation.18 | async-start | bytes 2621440 | tf_op jit(solution)/shard_map/all_gather | solution.py:150
  256.7 622.4 %all-gather.26.cloned.1.call-start = ((), (), s32[]{:S(2)}) async-start(), calls=%async_computation.19 | async-start | bytes 10485760 | tf_op jit(solution)/shard_map/all_gather | solution.py:151
  257.4 771.0 %all-gather.28.cloned.1.call-start = ((), (), s32[]{:S(2)}) async-start(), calls=%async_computation.20 | async-start | bytes 10485760 | tf_op jit(solution)/shard_map/all_gather | solution.py:152
  258.0 1373.7 %reduce-scatter.17.cloned.1.call-start = ((), (), s32[]{:S(2)}) async-start(), calls=%async_computation.22 | async-start | bytes 5242880 | tf_op jit(solution)/shard_map/reduce_scatter | solution.py:317
  270.8 196.5 %copy-start.39 = (f32[1,1024]{1,0:T(1,128)}, f32[1,1024]{1,0:T(1,128)S(1)}, u32[]{:S(2)}) copy-start(f32[1,1024]{1,0:T(1,128)S(1)} %get-tuple-element.649) | copy-start | bytes 12292
  706.4 15.6 copy-start.1
  745.4 15.6 copy-start.1
  783.0 15.6 copy-start.1
  820.6 15.6 copy-start.1
  847.7 31.4 %copy-start.38 = (f32[4096]{0:T(1024)S(1)}, f32[4096]{0:T(1024)}, u32[]{:S(2)}) copy-start(f32[4096]{0:T(1024)} %convert_element_type.289) | copy-start | bytes 49156
  847.7 31.4 %copy-start.43 = (f32[1,1024]{1,0:T(1,128)S(1)}, f32[1,1024]{1,0:T(1,128)}, u32[]{:S(2)}) copy-start(f32[1,1024]{1,0:T(1,128)} %get-tuple-element.648) | copy-start | bytes 12292
  847.7 31.4 %copy-start.62 = (f32[1,1024]{1,0:T(1,128)S(1)}, f32[1,1024]{1,0:T(1,128)}, u32[]{:S(2)}) copy-start(f32[1,1024]{1,0:T(1,128)} %get-tuple-element.640) | copy-start | bytes 12292
  851.8 216.5 %copy-start.33 = (f32[512]{0:T(512)}, f32[512]{0:T(512)S(1)}, u32[]{:S(2)}) copy-start(f32[512]{0:T(512)S(1)} %broadcast_multiply_fusion.1) | copy-start | bytes 6148
  853.5 214.9 %copy-start.52 = (f32[512]{0:T(512)}, f32[512]{0:T(512)S(1)}, u32[]{:S(2)}) copy-start(f32[512]{0:T(512)S(1)} %fusion.125) | copy-start | bytes 6148
  879.1 149.3 %copy-start.64 = (f32[1,1024]{1,0:T(1,128)S(1)}, f32[1,1024]{1,0:T(1,128)}, u32[]{:S(2)}) copy-start(f32[1,1024]{1,0:T(1,128)} %get-tuple-element.639) | copy-start | bytes 12292
  1028.4 10.3 copy-start.6
  1028.4 10.4 copy-start.28
  1042.9 15.9 copy-start.22
  1042.9 15.9 copy-start.9
  1556.6 188.7 %reduce-scatter.21.cloned.1.call-start = ((), (), s32[]{:S(2)}) async-start(), calls=%async_computation.24 | async-start | bytes 7864320 | tf_op jit(solution)/shard_map/reduce_scatter | solution.py:272
  1565.4 259.6 %reduce-scatter.15.cloned.1.call-start = ((), (), s32[]{:S(2)}) async-start(), calls=%async_computation.21 | async-start | bytes 5242880 | tf_op jit(solution)/shard_map/reduce_scatter | solution.py:314
  1566.1 372.3 %reduce-scatter.19.cloned.1.call-start = ((), (), s32[]{:S(2)}) async-start(), calls=%async_computation.23 | async-start | bytes 7864320 | tf_op jit(solution)/shard_map/reduce_scatter | solution.py:269
  1574.9 386.2 %reduce-scatter.37.cloned.1.call-start = ((), (), s32[]{:S(2)}) async-start(), calls=%async_computation.33 | async-start | bytes 327680
  1576.5 429.6 %reduce-scatter.25.cloned.1.call-start = ((), (), s32[]{:S(2)}) async-start(), calls=%async_computation.26 | async-start | bytes 2621440 | tf_op jit(solution)/shard_map/reduce_scatter | solution.py:360
  1580.4 471.7 %reduce-scatter.29.cloned.1.call-start = ((), (), s32[]{:S(2)}) async-start(), calls=%async_computation.28 | async-start | bytes 2621440 | tf_op jit(solution)/shard_map/reduce_scatter | solution.py:366
  1584.7 163.6 %copy-start.34 = (f32[512]{0:T(512)S(1)}, f32[512]{0:T(512)}, u32[]{:S(2)}) copy-start(f32[512]{0:T(512)} %copy-done.33) | copy-start | bytes 6148
  1584.7 163.6 %copy-start.44 = (f32[1,1024]{1,0:T(1,128)S(1)}, f32[1,1024]{1,0:T(1,128)}, u32[]{:S(2)}) copy-start(f32[1,1024]{1,0:T(1,128)} %get-tuple-element.648) | copy-start | bytes 12292
  1584.7 163.6 %copy-start.53 = (f32[512]{0:T(512)S(1)}, f32[512]{0:T(512)}, u32[]{:S(2)}) copy-start(f32[512]{0:T(512)} %copy-done.52) | copy-start | bytes 6148
  1584.7 163.6 %copy-start.63 = (f32[1,1024]{1,0:T(1,128)S(1)}, f32[1,1024]{1,0:T(1,128)}, u32[]{:S(2)}) copy-start(f32[1,1024]{1,0:T(1,128)} %get-tuple-element.640) | copy-start | bytes 12292
  1584.7 487.8 %reduce-scatter.35.cloned.1.call-start = ((), (), s32[]{:S(2)}) async-start(), calls=%async_computation.31 | async-start | bytes 40960 | tf_op jit(solution)/shard_map/reduce_scatter | solution.py:378
  1748.2 469.3 %reduce-scatter.31.cloned.1.call-start = ((), (), s32[]{:S(2)}) async-start(), calls=%async_computation.29 | async-start | bytes 10485760 | tf_op jit(solution)/shard_map/reduce_scatter | solution.py:369
  1759.2 605.8 %reduce-scatter.33.cloned.1.call-start = ((), (), s32[]{:S(2)}) async-start(), calls=%async_computation.30 | async-start | bytes 10485760 | tf_op jit(solution)/shard_map/reduce_scatter | solution.py:372
  1769.6 709.2 %reduce-scatter.23.cloned.1.call-start = ((), (), s32[]{:S(2)}) async-start(), calls=%async_computation.25 | async-start | bytes 7864320 | tf_op jit(solution)/shard_map/reduce_scatter | solution.py:357
  1776.8 59.0 %copy-start.21 = (bf16[512,1,1024]{2,0,1:T(8,128)(2,1)}, bf16[512,1,1024]{2,0,1:T(8,128)(2,1)S(1)}, u32[]{:S(2)}) copy-start(bf16[512,1,1024]{2,0,1:T(8,128)(2,1)S(1)} %reshape.342) | copy-start | bytes 3145732
  1835.9 102.5 %copy-start.20 = (bf16[768,1024]{1,0:T(8,128)(2,1)S(1)}, bf16[768,1024]{1,0:T(8,128)(2,1)}, u32[]{:S(2)}) copy-start(bf16[768,1024]{1,0:T(8,128)(2,1)} %reduce-scatter.21.cloned.1.call-done) | copy-start | bytes 4718596
  1835.9 756.5 %reduce-scatter.27.cloned.1.call-start = ((), (), s32[]{:S(2)}) async-start(), calls=%async_computation.27 | async-start | bytes 7864320 | tf_op jit(solution)/shard_map/reduce_scatter | solution.py:363
  1946.9 105.2 %copy-start.55 = (f32[512]{0:T(512)S(1)}, f32[512]{0:T(512)}, u32[]{:S(2)}) copy-start(f32[512]{0:T(512)} %copy-done.54) | copy-start | bytes 6148
  (65 other events, 219.7 us)
Sparse Core Ops, SparseCore 0:
  9.6 118.0 all-gather.11
  129.2 113.5 all-gather.19
  245.0 79.2 all-gather.13
  326.2 79.2 all-gather.15
  407.0 44.5 all-gather.17
  453.5 113.9 all-gather.21
  569.7 113.5 all-gather.29
  684.9 44.1 all-gather.23
  730.7 148.3 all-gather.25
  880.5 147.8 all-gather.27
  1556.7 74.9 reduce-scatter.16
  1634.0 111.2 reduce-scatter.20
  1747.6 77.2 reduce-scatter.14
  1827.1 111.2 reduce-scatter.18
  1940.5 20.4 reduce-scatter.36
  1963.8 42.2 reduce-scatter.24
  2008.8 43.1 reduce-scatter.28
  2054.2 18.2 reduce-scatter.34
  2074.9 142.6 reduce-scatter.30
  2219.7 145.1 reduce-scatter.32
  2367.3 111.4 reduce-scatter.22
  2481.1 111.2 reduce-scatter.26
where the time goes:
time: 2940 us
  waiting for transfers between devices  1570 us (53%)
  matrix products  584 us (20%)
  blocking collectives  381 us (13%)
  local copies, waits for them, and re-layouts  178 us (6%)
  other arithmetic  178 us (6%)
    psum x1, blocking collectives, body(): lax.psum((local_sums[0], local_sums[1], local_sums[2], local_sums[3], loc...  330 us
    reduce_scatter x1, waiting for transfers between devices, body(): lax.psum_scatter(grad_w_ffn_out.astype(jnp.bfloat16), 'mem', scatter_dime...  147 us
    reduce_scatter x1, waiting for transfers between devices, body(): lax.psum_scatter(grad_w_ffn_in.astype(jnp.bfloat16), 'mem', scatter_dimen...  145 us
    all_gather x1, waiting for transfers between devices, body(): lax.all_gather(ffn_out, 'mem', axis=0, tiled=True)  121 us
    reduce_scatter x1, waiting for transfers between devices, body(): lax.psum_scatter(grad_w_self.astype(jnp.bfloat16), 'mem', scatter_dimensi...  114 us
    reduce_scatter x1, waiting for transfers between devices, body(): lax.psum_scatter(grad_w_cross.astype(jnp.bfloat16), 'mem', scatter_dimens...  114 us
    reduce_scatter x1, waiting for transfers between devices, body(): lax.psum_scatter(grad_memory_values.astype(jnp.bfloat16), 'mem', scatter_...  112 us
    all_gather x1, waiting for transfers between devices, body(): lax.all_gather(memory_keys_low, 'mem', axis=0, tiled=True)  107 us
  transfers between devices with their start and end apart: 22, of which 20 were waited for; matrix products, arithmetic and copies ran while one was open for 14% of the time, Pallas kernels for 0%

commit v1 on v0

v1 whole, which is shorter than its diff:
```python
import functools

import jax
import jax.numpy as jnp
from jax import lax
from jax.experimental import pallas as pl
from jax.experimental.pallas import tpu as pltpu
from jax.sharding import PartitionSpec as P

HD = 64
PLEN = 256
BLK = 256
F32 = jnp.float32
BF16 = jnp.bfloat16

NN = (((1,), (0,)), ((), ()))
NT = (((1,), (1,)), ((), ()))


def mm(a, b, dims=NN):
    return lax.dot_general(a, b, dims, preferred_element_type=F32)


def head_mask_rows(block, head):
    rows = lax.broadcasted_iota(jnp.int32, block.shape, 0)
    return jnp.where((rows // HD) == head, block, jnp.zeros_like(block))


def head_rows(block, head, extra=None):
    block = block.astype(F32)
    rows = lax.broadcasted_iota(jnp.int32, block.shape, 0)
    out = jnp.where((rows // HD) == head, block, 0.0)
    if extra is not None:
        rest = -extra
        for i in range(3):
            term = rest.astype(BF16).astype(F32)
            rest = rest - term
            out = jnp.where(rows == (1 - head) * HD + i, term, out)
    return out.astype(BF16)


def ones_in(block, head):
    lanes = lax.broadcasted_iota(jnp.int32, block.shape, 1)
    first = (1 - head) * HD
    return jnp.where((lanes >= first) & (lanes < first + 3), jnp.ones_like(block), block)


def pick_heads(first, second):
    lanes = lax.broadcasted_iota(jnp.int32, first.shape, 1)
    return jnp.where(lanes < HD, first, second)


MESH = pl.DeviceIdType.MESH
ANY = pl.BlockSpec(memory_space=pl.ANY)
VMEM = pl.BlockSpec(memory_space=pltpu.VMEM)
PLANE = 4


def flip(index, bits):
    bit = 1
    while bit <= bits:
        if bits & bit:
            unit = jnp.int32(bit)
            index = index + unit - 2 * unit * lax.rem(lax.div(index, unit), jnp.int32(2))
        bit *= 2
    return index


class Place:
    def __init__(self, plane, planes=1):
        self.pb = lax.axis_index("pb")
        self.mem = lax.axis_index("mem")
        two = jnp.int32(2)
        self.core = lax.rem(self.pb, two)
        self.quarter = lax.rem(lax.div(self.pb, two), jnp.int32(plane))
        self.parity = lax.rem(self.mem, two)
        self.half = lax.div(self.mem, two)
        self.plane = plane
        self.planes = planes

    def near(self, t):
        return (flip(self.pb, 2 * t), self.mem)

    def far(self, r):
        return (flip(self.pb, 2 * self.plane * r), self.mem)

    def line(self, s):
        return (self.pb, flip(self.mem, s))

    def twin(self):
        return (flip(self.pb, 1), self.mem)

    def pair(self):
        return (self.pb, flip(self.mem, 1))

    def worker(self, k):
        return (self.pb - self.core + self.half, 2 * self.core + flip(self.parity, k))

    def at_home(self):
        return self.half == self.core

    def meet(self, peers):
        barrier = pltpu.get_barrier_semaphore()
        for pb_bits, mem_bits in peers:
            pl.semaphore_signal(
                barrier,
                inc=1,
                device_id=(flip(self.pb, pb_bits), flip(self.mem, mem_bits)),
                device_id_type=MESH,
            )
        pl.semaphore_wait(barrier, len(peers))


def column_peers(n_mem):
    return [(a, b) for a in range(2) for b in range(n_mem) if (a, b) != (0, 0)]


def plane_peers(plane):
    return [(2 * t, 0) for t in range(1, plane)]


class Sems:
    def __init__(self, ref):
        self.ref = ref
        self.used = 0

    def take(self, count):
        first = self.used
        self.used += count
        return [self.ref.at[first + i] for i in range(count)]


def remote(src, dst, send_sem, recv_sem, device):
    return pltpu.make_async_remote_copy(
        src_ref=src,
        dst_ref=dst,
        send_sem=send_sem,
        recv_sem=recv_sem,
        device_id=device,
        device_id_type=MESH,
    )


class Spread:
    def __init__(self, place, sems, src, dst, kinds=(0, 1)):
        self.place, self.src, self.dst, self.kinds = place, src, dst, kinds
        self.send = sems.take(2)
        self.recv = sems.take(2)

    def copy(self, k):
        return remote(self.src(k), self.dst(k), self.send[k], self.recv[k], self.place.worker(k))

    def start(self):
        for k in self.kinds:
            if k == 0:
                home = self.place.at_home()

                @pl.when(home)
                def _():
                    pltpu.make_async_copy(self.src(0), self.dst(0), self.recv[0]).start()

                @pl.when(jnp.logical_not(home))
                def _():
                    self.copy(0).start()
            else:
                self.copy(k).start()

    def wait_recv(self, k):
        if k == 0:
            home = self.place.at_home()

            @pl.when(home)
            def _():
                pltpu.make_async_copy(self.src(0), self.dst(0), self.recv[0]).wait()

            @pl.when(jnp.logical_not(home))
            def _():
                self.copy(0).wait_recv()
        else:
            self.copy(k).wait_recv()

    def wait_send(self):
        for k in self.kinds:
            if k == 0:

                @pl.when(jnp.logical_not(self.place.at_home()))
                def _():
                    self.copy(0).wait_send()
            else:
                self.copy(k).wait_send()


class Own:
    def __init__(self, place, sems, shard, full, columns, n_mem):
        self.copies = []
        mem, core = place.mem, place.core
        if columns:
            unit = full.shape[-1] // n_mem
            for b, sem in zip(range(n_mem), sems.take(n_mem)):
                start = pl.multiple_of(2 * unit * b + unit * core, unit)
                src = shard.at[:, :, :, pl.ds(start, unit)]
                dst = full.at[:, mem, :, :, pl.ds(unit * b, unit)]
                self.copies.append(pltpu.make_async_copy(src, dst, sem))
        else:
            (sem,) = sems.take(1)
            self.copies.append(pltpu.make_async_copy(shard.at[core], full.at[0, mem], sem))

    def start(self):
        for copy in self.copies:
            copy.start()

    def wait(self):
        for copy in self.copies:
            copy.wait()


class Line:
    def __init__(self, place, sems, src, dst, n_mem):
        send, recv = sems.take(n_mem - 1), sems.take(n_mem - 1)
        self.copies = [
            remote(src(s), dst(s), send[s - 1], recv[s - 1], place.line(s)) for s in range(1, n_mem)
        ]

    def start(self):
        for copy in self.copies:
            copy.start()

    def wait_recv(self, s):
        self.copies[s - 1].wait_recv()

    def wait_send(self):
        for copy in self.copies:
            copy.wait_send()


class Share:
    def __init__(self, place, sems, src, block):
        send, recv = sems.take(4), sems.take(4)
        rows = src.shape[-2]
        half = rows // 2

        def part(ref, i):
            return ref.at[:, pl.ds(i * half, half)]

        self.first = [
            remote(src, block(0), send[t - 1], recv[t - 1], place.near(t)) for t in (1, 2)
        ]
        self.second = [
            remote(part(block(t), t - 1), part(block(t), t - 1), send[t + 1], recv[t + 1], place.near(3 - t))
            for t in (1, 2)
        ]

    def start(self):
        for copy in self.first:
            copy.start()

    def forward(self):
        for direct, onward in zip(self.first, self.second):
            direct.wait_recv()
            onward.start()

    def wait(self):
        for copy in self.first:
            copy.wait_send()
        for copy in self.second:
            copy.wait()


class Chain:
    def __init__(self, place, sems, block, n_mem):
        self.place, self.block, self.n = place, block, n_mem
        self.sems = {way: (sems.take(n_mem - 1), sems.take(n_mem - 1)) for way in (1, -1)}

    def copy(self, way, hops):
        mem = self.place.mem
        source = lax.rem(mem + jnp.int32(self.n - way * hops), jnp.int32(self.n))
        target = lax.rem(mem + jnp.int32(self.n + way), jnp.int32(self.n))
        send, recv = self.sems[way]
        piece = self.block(source)
        return remote(piece, piece, send[hops], recv[hops], (self.place.pb, target))

    def comes(self, way, hops):
        mem = self.place.mem
        return mem >= hops if way == 1 else mem + hops < self.n

    def goes(self, way, hops):
        mem = self.place.mem
        ahead = mem + 1 < self.n if way == 1 else mem >= 1
        return jnp.logical_and(ahead, self.comes(way, hops))

    def start(self):
        for way in (1, -1):

            @pl.when(self.goes(way, 0))
            def _():
                self.copy(way, 0).start()

    def relay(self, hops, arrived):
        for way in (1, -1):

            @pl.when(self.comes(way, hops))
            def _():
                self.copy(way, hops - 1).wait_recv()
                if hops < self.n - 1:

                    @pl.when(self.goes(way, hops))
                    def _():
                        self.copy(way, hops).start()

                arrived(hops if way == 1 else self.n - hops)

    def wait_send(self):
        for hops in range(self.n - 1):
            for way in (1, -1):

                @pl.when(self.goes(way, hops))
                def _():
                    self.copy(way, hops).wait_send()


class Gather:
    def __init__(self, place, sems, shard, full, columns, n_mem, in_plane=True):
        mem, quarter = place.mem, place.quarter
        self.n_mem = n_mem
        self.in_plane = in_plane
        self.own = Own(place, sems, shard, full, columns, n_mem)
        self.chain = Chain(place, sems, lambda i: full.at[:, i, quarter], n_mem)
        self.shares = {}
        for d in range(1, n_mem if in_plane else 1):
            source = lax.rem(mem + jnp.int32(n_mem - d), jnp.int32(n_mem))

            def block(t, source=source):
                return full.at[:, source, flip(quarter, t)]

            self.shares[d] = Share(place, sems, block(0), block)

    def begin(self):
        self.own.wait()
        self.chain.start()

    def share(self, hops):
        self.chain.relay(hops, lambda d: self.shares[d].start() if self.in_plane else None)

    def forward(self, hops):
        for way, d in ((1, hops), (-1, self.n_mem - hops)):

            @pl.when(self.chain.comes(way, hops))
            def _():
                self.shares[d].forward()

    def finish(self):
        self.chain.wait_send()
        for share in self.shares.values():
            share.wait()


GATHER_SEMS = 44


def half_views(shard, columns, n_mem, plane):
    if columns:
        lead, depth, hidden = shard.shape
        part = depth // plane
        return shard.reshape(lead, plane, part, hidden), (lead, n_mem, plane, part, hidden // 2)
    depth, width = shard.shape
    part = depth // 2 // plane
    return shard.reshape(2, plane, part, width), (1, n_mem, plane, part, width)


class Walk:
    def __init__(self, refs):
        self.refs = list(refs)

    def take(self, count):
        out, self.refs = self.refs[:count], self.refs[count:]
        return out

    def one(self):
        return self.take(1)[0]


def softmax_units(units, finish, serve=None):
    def scores_of(unit, j):
        return unit[0][j]()

    ready = [scores_of(units[0], j) for j in range(len(units[0][0]))]
    for n, (_, values, tag) in enumerate(units):
        if serve is not None:
            serve(n)
        coming = list(range(len(units[n + 1][0]))) if n + 1 < len(units) else []
        following = []
        top = functools.reduce(
            jnp.maximum, [jnp.max(tile, axis=0, keepdims=True) for tile in ready]
        )
        total = jnp.zeros_like(top)
        acc = None
        share = -(-len(coming) // len(ready))
        for j, tile in enumerate(ready):
            for i in coming[j * share : (j + 1) * share]:
                following.append(scores_of(units[n + 1], i))
            probs = jnp.exp(tile - top)
            total += jnp.sum(probs, axis=0, keepdims=True)
            part = mm(values[j](), probs.astype(BF16))
            acc = part if acc is None else acc + part
        finish(tag, acc / total, top + jnp.log(total))
        ready = following


def self_attend(place, pair, q_vm, k_vm, v_vm, o_vm, lse_vm, v_t, o_t):
    base = 2 * place.core + place.parity
    count = q_vm.shape[0] // BLK
    lanes = pl.ds(pl.multiple_of(pair * 2 * HD, 2 * HD), 2 * HD)

    def rows(i):
        return pl.ds(pl.multiple_of(flip(base, i) * BLK, BLK), BLK)

    for j in range(count):
        v_t[:, j * BLK : (j + 1) * BLK] = v_vm[rows(j), lanes].T
    key_pos = lax.broadcasted_iota(jnp.int32, (BLK, BLK), 0)
    query_pos = lax.broadcasted_iota(jnp.int32, (BLK, BLK), 1)
    units = []
    for i in range(count):
        q_t = q_vm[rows(i), lanes].T
        for head in range(2):
            q_head = head_rows(q_t, head)

            def score(j, i=i, q_head=q_head):
                tile = mm(k_vm[rows(j), lanes], q_head)
                return jnp.where(key_pos <= query_pos, tile, -1000000000.0) if j == i else tile

            def value(j, head=head):
                return v_t[head * HD : (head + 1) * HD, j * BLK : (j + 1) * BLK]

            units.append(
                (
                    [functools.partial(score, j) for j in range(i + 1)],
                    [functools.partial(value, j) for j in range(i + 1)],
                    (i, head),
                )
            )

    def finish(tag, mixed, lse):
        i, head = tag
        span = slice(i * BLK, (i + 1) * BLK)
        o_t[head * HD : (head + 1) * HD, span] = mixed
        lse_vm[pair, head : head + 1, span] = lse

    softmax_units(units, finish)
    for i in range(count):
        o_vm[rows(i), lanes] = o_t[:, i * BLK : (i + 1) * BLK].T.astype(BF16)


def tiles(rows, step):
    def run(i, carry):
        step(pl.ds(pl.multiple_of(i * BLK, BLK), BLK))
        return carry

    lax.fori_loop(0, rows // BLK, run, 0)


def front_kernel(n_mem, plane, kinds, places, x_ref, enc_ref, map_ref, small_ref, *refs):
    refs = Walk(refs)
    count = len(kinds)
    shards = refs.take(count)
    x_out, enc_out, index_out, small_out = refs.take(4)
    halves = refs.take(count)
    kept = refs.take(11)
    x_vm, w_vm, so_vm, cq_w, small_vm = refs.take(5)
    q_vm, k_vm, v_vm, sa_vm, lse_vm, h1_vm, unit_vm, scale_vm, cq_vm = refs.take(9)
    k_all, v_all, v_t, o_t, part_vm, twin_vm, kv_w, enc_vm, map_in = refs.take(9)
    sems = Sems(refs.one())
    place = Place(plane)
    n_bias, n_gain = places
    rows = x_ref.shape[1]
    gathers = [
        Gather(place, sems, shard, half, columns, n_mem)
        for shard, half, columns in zip(shards, halves, kinds)
    ]
    spread = Spread(
        place,
        sems,
        lambda k: x_ref.at[flip(place.parity, k)],
        lambda k: x_out.at[pl.ds(rows * k, rows)],
    )
    twin_send, twin_recv = sems.take(2), sems.take(2)
    twin = [
        remote(
            x_out.at[pl.ds(rows * k, rows)],
            x_out.at[pl.ds(rows * (k + 2), rows)],
            twin_send[k],
            twin_recv[k],
            place.twin(),
        )
        for k in range(2)
    ]
    map_sems = sems.take(2)
    map_copy = remote(map_ref, map_in, map_sems[0], map_sems[1], place.twin())
    (small_sem,) = sems.take(1)
    small_own = pltpu.make_async_copy(small_ref, small_out.at[place.mem], small_sem)
    small_line = Line(
        place, sems, lambda s: small_ref, lambda s: small_out.at[place.mem], n_mem
    )
    units = enc_vm.shape[1]
    encs, enc_twins, enc_pairs, enc_onwards, enc_ends = [], [], [], [], []
    for u in range(units):
        encs.append(
            Spread(
                place, sems, lambda k, u=u: enc_ref.at[u], lambda k, u=u: enc_vm.at[0, u], kinds=(0,)
            )
        )
        pair_sems, twin_sems, end_sems = sems.take(2), sems.take(2), sems.take(2)
        enc_pairs.append(remote(enc_ref.at[u], enc_vm.at[1, u], *pair_sems, place.pair()))
        enc_onwards.append(remote(enc_vm.at[0, u], enc_vm.at[1, u], *pair_sems, place.pair()))
        enc_twins.append(remote(enc_vm.at[0, u], enc_vm.at[2, u], *twin_sems, place.twin()))
        enc_ends.append(remote(enc_vm.at[1, u], enc_vm.at[3, u], *end_sems, place.twin()))
    enc_keeps = [
        pltpu.make_async_copy(enc_vm.at[i], enc_out.at[i], sem) for i, sem in enumerate(sems.take(4))
    ]
    home = place.at_home()
    away = jnp.logical_not(home)
    loads = [
        pltpu.make_async_copy(src, dst, sem)
        for src, dst, sem in zip(
            (x_out, halves[0], halves[1], halves[2].at[0], small_out, halves[2].at[pl.ds(1, 2)]),
            (x_vm, w_vm, so_vm, cq_w, small_vm, kv_w),
            sems.take(6),
        )
    ]
    keeps = [
        pltpu.make_async_copy(src, dst, sem)
        for src, dst, sem in zip(
            (q_vm, k_vm, v_vm, sa_vm, lse_vm, h1_vm, unit_vm, scale_vm, cq_vm, k_all, v_all),
            kept,
            sems.take(11),
        )
    ]
    swap_sems = sems.take(4)
    own = 2 * rows
    swap_part = remote(part_vm, twin_vm, swap_sems[0], swap_sems[1], place.twin())
    swap_h1 = remote(
        h1_vm.at[pl.ds(0, own)], h1_vm.at[pl.ds(own, own)], swap_sems[2], swap_sems[3], place.twin()
    )

    for gather in gathers:
        gather.own.start()
    small_own.start()
    place.meet(column_peers(n_mem) + plane_peers(plane))
    for gather in gathers:
        gather.begin()
    small_line.start()
    map_copy.start()
    spread.start()
    for gather in gathers:
        gather.share(1)
    for gather in gathers:
        gather.share(2)
    gathers[0].forward(1)
    for k in range(2):
        spread.wait_recv(k)
        twin[k].start()
    for gather in gathers:
        gather.share(3)
    for u in range(units):
        encs[u].start()

        @pl.when(home)
        def _():
            enc_pairs[u].start()

    def first_arrival(u):
        encs[u].wait_recv(0)

        @pl.when(away)
        def _():
            enc_onwards[u].start()

        enc_twins[u].start()

    def second_arrival(u):
        @pl.when(home)
        def _():
            enc_pairs[u].wait()

        @pl.when(away)
        def _():
            enc_onwards[u].wait()

        enc_ends[u].start()

    for hops in (2, 3):
        gathers[0].forward(hops)
    for hops in (1, 2, 3):
        for gather in gathers[1:]:
            gather.forward(hops)
    for copy in twin:
        copy.wait_recv()
    small_own.wait()
    for s in range(1, n_mem):
        small_line.wait_recv(s)
    gathers[0].finish()
    for copy in (loads[0], loads[1], loads[4]):
        copy.start()
    for copy in (loads[0], loads[1], loads[4]):
        copy.wait()

    def half_row(row):
        lanes = pl.ds(pl.multiple_of(place.core * 2 * HD, 2 * HD), 2 * HD)
        return jnp.concatenate(
            [small_vm[b, :, lanes].astype(F32)[row : row + 1] for b in range(n_mem)], axis=1
        )

    def full_row(row):
        return jnp.concatenate(
            [small_vm[b].astype(F32)[row : row + 1] for b in range(n_mem)], axis=1
        )

    bias_q, bias_v = half_row(0), half_row(1)
    depth = x_vm.shape[1]

    def weight(ref):
        return ref[...].reshape(-1, ref.shape[-1])

    def project(span):
        x_tile = x_vm[span, :]
        q_vm[span, :] = ((mm(x_tile, weight(w_vm.at[0])) + bias_q) * 0.125).astype(BF16)
        k_vm[span, :] = mm(x_tile, weight(w_vm.at[1])).astype(BF16)
        v_vm[span, :] = (mm(x_tile, weight(w_vm.at[2])) + bias_v).astype(BF16)

    tiles(x_vm.shape[0], project)
    for copy in keeps[:3]:
        copy.start()
    pairs = q_vm.shape[1] // (2 * HD)
    for pair in range(pairs):
        self_attend(place, pair, q_vm, k_vm, v_vm, sa_vm, lse_vm, v_t, o_t)
        if pair in (0, pairs // 2):
            first_arrival(min(pair, 1))
    for copy in keeps[3:5]:
        copy.start()
    for gather in gathers[1:]:
        gather.finish()
    for copy in (loads[2], loads[3], loads[5]):
        copy.start()
    for copy in (loads[2], loads[3], loads[5]):
        copy.wait()

    def other_part(span):
        part_vm[span, :] = mm(
            sa_vm[pl.ds(pl.multiple_of(span.start + own, BLK), BLK), :], weight(so_vm)
        ).astype(BF16)

    tiles(own, other_part)
    swap_part.start()

    def own_part(span):
        unit_vm[span, :] = mm(sa_vm[span, :], weight(so_vm)) + x_vm[span, :].astype(F32)

    tiles(own, own_part)
    for u in range(2, units):
        first_arrival(u)
    bias_out = full_row(2)
    gain, shift = full_row(n_bias), full_row(6)
    swap_part.wait()

    def normalise(span):
        values = unit_vm[span, :] + twin_vm[span, :].astype(F32) + bias_out
        centre = values - jnp.mean(values, axis=-1, keepdims=True)
        scale = lax.rsqrt(jnp.mean(centre * centre, axis=-1, keepdims=True) + 1e-05)
        unit = centre * scale
        unit_vm[span, :] = unit
        scale_vm[span, :] = jnp.broadcast_to(scale, (BLK, scale_vm.shape[1]))
        h1_vm[span, :] = (unit * gain + shift).astype(BF16)

    tiles(own, normalise)
    swap_h1.start()
    for copy in keeps[6:8]:
        copy.start()
    bias_cq = half_row(3)

    def queries(span):
        cq_vm[span, :] = ((mm(h1_vm[span, :], weight(cq_w)) + bias_cq) * 0.125).astype(BF16)

    tiles(own, queries)
    swap_h1.wait()
    keeps[5].start()

    def other_queries(span):
        queries(pl.ds(pl.multiple_of(span.start + own, BLK), BLK))

    tiles(own, other_queries)
    keeps[8].start()

    map_copy.wait()
    near_map, far_map = map_ref[...], map_in[...]
    both_maps = jnp.where(home, near_map, far_map)
    mine = jnp.where(place.parity == 0, both_maps[:1], both_maps[1:])
    group = lax.div(mine, jnp.full_like(mine, units))
    index_out[...] = (group ^ (2 * place.core + place.parity)) * units + lax.rem(
        mine, jnp.full_like(mine, units)
    )

    bias_cv = half_row(4)

    def memory(block, u):
        rows_here = enc_vm[block, u]
        k_all[block * units + u] = mm(rows_here, weight(kv_w.at[0])).astype(BF16)
        v_all[block * units + u] = (mm(rows_here, weight(kv_w.at[1])) + bias_cv).astype(BF16)

    for u in range(units):
        second_arrival(u)
        memory(0, u)
    enc_keeps[0].start()
    enc_keeps[1].start()
    for block, copies in ((2, enc_twins), (1, None), (3, enc_ends)):
        for u in range(units):
            if copies is not None:
                copies[u].wait_recv()
            memory(block, u)
    enc_keeps[2].start()
    enc_keeps[3].start()
    for copy in keeps[9:]:
        copy.start()
    spread.wait_send()
    for copy in twin:
        copy.wait_send()
    small_line.wait_send()
    for item in encs:
        item.wait_send()
    for copy in enc_twins + enc_ends:
        copy.wait_send()
    for copy in keeps + enc_keeps:
        copy.wait()


def front(n_mem, plane, places, hidden_in, enc, passage_map, small, params):
    kinds = tuple(columns for _, columns in params)
    views = [half_views(shard, columns, n_mem, plane) for shard, columns in params]
    seg, width = hidden_in.shape[1:]
    rows, own = 4 * seg, 2 * seg
    part = width // 2
    pairs = part // (2 * HD)
    passages = 4 * enc.shape[0]
    shapes = (
        [((rows, width), BF16), ((4,) + enc.shape, BF16), ((1, passage_map.shape[1]), jnp.int32)]
        + [((n_mem,) + small.shape, BF16)]
        + [(full, BF16) for _, full in views]
    )
    kept = [
        ((rows, part), BF16),
        ((rows, part), BF16),
        ((rows, part), BF16),
        ((rows, part), BF16),
        ((pairs, 2, rows), F32),
        ((rows, width), BF16),
        ((own, width), F32),
        ((own, 2 * HD), F32),
        ((rows, part), BF16),
        ((passages, PLEN, part), BF16),
        ((passages, PLEN, part), BF16),
    ]
    scratch = [
        ((rows, width), BF16),
        (views[0][1], BF16),
        (views[1][1][1:], BF16),
        (views[2][1][1:], BF16),
        ((n_mem,) + small.shape, BF16),
    ] + kept + [
        ((2 * HD, rows), BF16),
        ((2 * HD, rows), F32),
        ((own, width), BF16),
        ((own, width), BF16),
        ((2,) + views[2][1][1:], BF16),
        ((4,) + enc.shape, BF16),
        (passage_map.shape, jnp.int32),
    ]
    scratch[2] = (views[1][1], BF16)
    outs = pl.pallas_call(
        functools.partial(front_kernel, n_mem, plane, kinds, places),
        in_specs=[VMEM] * (4 + len(params)),
        out_specs=[ANY, ANY, VMEM] + [ANY] * (len(shapes) + len(kept) - 3),
        out_shape=[jax.ShapeDtypeStruct(*item) for item in shapes + kept],
        scratch_shapes=[pltpu.VMEM(*item) for item in scratch]
        + [pltpu.SemaphoreType.DMA((90 + GATHER_SEMS * len(params),))],
        compiler_params=pltpu.CompilerParams(
            collective_id=0, has_side_effects=True, vmem_limit_bytes=60 * 2**20
        ),
        cost_estimate=pl.CostEstimate(
            flops=rows * width * part * 10, bytes_accessed=40 * 2**20, transcendentals=rows * rows * 8
        ),
        name="front",
    )(hidden_in, enc, passage_map, small, *[view for view, _ in views])
    count = 4 + len(params)
    return outs[:4], outs[4:count], outs[count:]


class PlaneSum:
    def __init__(self, place, sems, grad, own, bufs, rows, lanes=None):
        self.own = own
        self.from_near, self.via, self.add = bufs
        quarter = place.quarter
        first, count = rows
        half = count // 2
        self.lead, self.n_mem = own.shape[:2]
        lanes = pl.ds(*(lanes or (0, grad.shape[-1])))

        def piece(t, lo, size):
            return grad.at[:, :, flip(quarter, t), pl.ds(first + lo, size), lanes]

        loads = sems.take(3)
        self.loads = [pltpu.make_async_copy(piece(0, 0, count), own, loads[0])]
        send, recv = sems.take(6), sems.take(6)
        self.onward, self.direct, self.summed = [], [], []
        for t in (1, 2):
            lo = (t - 1) * half
            self.onward.append(
                remote(piece(3, lo, half), self.via.at[t - 1], send[t - 1], recv[t - 1], place.near(t))
            )
            self.direct.append(
                remote(
                    piece(t, lo, half),
                    self.from_near.at[t - 1, :, :, pl.ds(lo, half)],
                    send[t + 1],
                    recv[t + 1],
                    place.near(t),
                )
            )
            other = half - lo
            self.loads.append(
                pltpu.make_async_copy(piece(t, other, half), self.add.at[t - 1], loads[t])
            )
            self.summed.append(
                remote(
                    self.add.at[t - 1],
                    self.from_near.at[t - 1, :, :, pl.ds(other, half)],
                    send[t + 3],
                    recv[t + 3],
                    place.near(t),
                )
            )

    def start(self):
        for copy in self.onward + self.loads + self.direct:
            copy.start()

    def each(self, step):
        def run(i, carry):
            step(lax.div(i, jnp.int32(self.n_mem)), lax.rem(i, jnp.int32(self.n_mem)))
            return carry

        lax.fori_loop(0, self.lead * self.n_mem, run, 0)

    def middle(self):
        for copy in self.loads:
            copy.wait()
        for t in (1, 2):
            self.onward[2 - t].wait_recv()

            def add(l, m, t=t):
                total = self.add[t - 1, l, m].astype(F32) + self.via[2 - t, l, m].astype(F32)
                self.add[t - 1, l, m] = total.astype(BF16)

            self.each(add)
            self.summed[t - 1].start()

    def end(self):
        for copy in self.direct + self.summed:
            copy.wait_recv()

        def add(l, m):
            total = self.own[l, m].astype(F32)
            for t in range(2):
                total += self.from_near[t, l, m].astype(F32)
            self.own[l, m] = total.astype(BF16)

        self.each(add)

    def wait_send(self):
        for copy in self.onward + self.direct + self.summed:
            copy.wait_send()


class Settle:
    def __init__(self, place, sems, own, out, bufs, columns, n_mem, rows, lane=0):
        self.place, self.n_mem, self.columns, self.rows = place, n_mem, columns, rows
        self.lane = lane
        self.own, self.out = own, out
        self.line_in, self.far_in, self.slots = bufs
        quarter, mem, core = place.quarter, place.mem, place.core
        slots = self.slots

        def slot(t):
            return slots.at[flip(quarter, t), core]

        self.line = Line(
            place, sems, lambda s: own.at[:, flip(mem, s)], lambda s: self.line_in.at[s - 1], n_mem
        )
        others = place.planes - 1
        far_send, far_recv = sems.take(others), sems.take(others)
        self.far = [
            remote(slot(0), self.far_in.at[r - 1], far_send[r - 1], far_recv[r - 1], place.far(r))
            for r in range(1, place.planes)
        ]
        self.share = Share(place, sems, slot(0), slot)
        twin_send, twin_recv = sems.take(place.plane), sems.take(place.plane)
        self.twin = [
            remote(slot(t), slot(t), twin_send[t], twin_recv[t], place.twin())
            for t in range(place.plane)
        ]

    def start(self):
        self.line.start()

    def middle(self):
        for s in range(1, self.n_mem):
            self.line.wait_recv(s)
        quarter, core, mem = self.place.quarter, self.place.core, self.place.mem
        lead = self.own.shape[0]
        for l in range(lead):
            total = self.own[l, mem].astype(F32)
            for s in range(self.n_mem - 1):
                total += self.line_in[s, l].astype(F32)
            self.slots[quarter, core, l] = total.astype(BF16)
        if self.far:
            for copy in self.far:
                copy.start()
            for copy in self.far:
                copy.wait()
            for l in range(lead):
                total = self.slots[quarter, core, l].astype(F32)
                for r in range(len(self.far)):
                    total += self.far_in[r, l].astype(F32)
                self.slots[quarter, core, l] = total.astype(BF16)
        self.share.start()
        self.twin[0].start()

    def forward(self):
        self.share.forward()
        self.twin[1].start()
        self.twin[2].start()

    def end(self):
        self.share.wait()
        self.twin[3].start()
        for copy in self.twin:
            copy.wait()
        self.line.wait_send()
        lead = self.own.shape[0]
        wide = self.slots.shape[-1]
        first, count = self.rows
        for q in range(self.place.plane):
            for c in range(2):
                for l in range(lead):
                    if self.columns:
                        unit = self.out.shape[-1] // (2 * self.n_mem)
                        for b in range(wide // unit):
                            start = unit * (2 * (self.lane // unit + b) + c)
                            self.out[l, q, first : first + count, start : start + unit] = self.slots[
                                q, c, l, :, b * unit : (b + 1) * unit
                            ]
                    else:
                        self.out[c, q, first : first + count] = self.slots[q, c, l]


PLANE_SUM_SEMS = 15


def settle_sems(n_mem, plane, planes):
    return 2 * (n_mem - 1) + 2 * (planes - 1) + 8 + 2 * plane


def plane_sum_scratch(grad_shape, n_mem, count, cols=None):
    lead, cols = grad_shape[0], cols or grad_shape[-1]
    return [
        pltpu.VMEM((2, lead, n_mem, count, cols), BF16),
        pltpu.VMEM((2, lead, n_mem, count // 2, cols), BF16),
        pltpu.VMEM((2, lead, n_mem, count // 2, cols), BF16),
    ]


def settle_scratch(grad_shape, n_mem, plane, planes, count, cols=None):
    lead, cols = grad_shape[0], cols or grad_shape[-1]
    return [
        pltpu.VMEM((n_mem - 1, lead, count, cols), BF16),
        pltpu.VMEM((max(planes - 1, 1), lead, count, cols), BF16),
        pltpu.VMEM((plane, 2, lead, count, cols), BF16),
    ]


def sum_shape(grad_shape):
    lead, n_mem, _, rows, cols = grad_shape
    return jax.ShapeDtypeStruct((lead, n_mem, rows, cols), BF16)


def reduce_out(grad_shape, columns, plane):
    lead, _, _, rows, cols = grad_shape
    shape = (lead, plane, rows, 2 * cols) if columns else (2, plane, rows, cols)
    return jax.ShapeDtypeStruct(shape, BF16)


def reduce_peers(n_mem, plane, planes):
    return (
        [(1, 0)]
        + [(0, s) for s in range(1, n_mem)]
        + plane_peers(plane)
        + [(2 * plane * r, 0) for r in range(1, planes)]
    )


def whole(shape):
    return pl.BlockSpec(shape, lambda *grid: (0,) * len(shape))


class Fetch:
    def __init__(self, sems, src, dst):
        self.copy = pltpu.make_async_copy(src, dst, sems.take(1)[0])
        self.dst = dst
        self.here = False

    def start(self):
        self.copy.start()

    def get(self):
        if not self.here:
            self.copy.wait()
            self.here = True
        return self.dst


def unit_norm(values):
    centre = values - jnp.mean(values, axis=-1, keepdims=True)
    scale = lax.rsqrt(jnp.mean(centre * centre, axis=-1, keepdims=True) + 1e-05)
    return centre * scale, scale


def unit_norm_back(grad, unit, scale, gain):
    inner = grad * gain
    return (
        inner
        - jnp.mean(inner, axis=-1, keepdims=True)
        - unit * jnp.mean(inner * unit, axis=-1, keepdims=True)
    ) * scale


def feed_kernel(n_mem, plane, cot_ref, rows_ref, bias_ref, *refs):
    refs = Walk(refs)
    fetched = refs.take(4)
    out_part = refs.one()
    final_out, dca_ref, dz2_ref, sums_ref, bias_sum, own_out, dw_in, dw_co = refs.take(8)
    kept = refs.take(4)
    out_w = refs.one()
    cot_vm, h2_vm, unit_vm, scale_vm, act_vm, slope_vm, p_vm, part_vm, twin_vm = refs.take(9)
    final_vm, df_vm, dco_vm, dw_out = refs.take(4)
    bufs = refs.take(3)
    sems = Sems(refs.one())
    place = Place(plane)
    ca, unit1, w_co, w_in = [Fetch(sems, src, dst) for src, dst in zip(fetched, kept)]
    mem, quarter = place.mem, place.quarter
    pieces = [Fetch(sems, out_part.at[0, mem], out_w.at[0, mem])]
    shares = []
    for d in range(1, n_mem):
        source = lax.rem(mem + jnp.int32(n_mem - d), jnp.int32(n_mem))

        def place_of(t, source=source):
            return out_w.at[:, source, flip(quarter, t)]

        pieces.append(Fetch(sems, out_part.at[:, source, quarter], place_of(0)))
        shares.append(Share(place, sems, place_of(0), place_of))
    rows = h2_vm.shape[0]
    own = rows // 2
    seg = own // 2
    hidden = act_vm.shape[1]
    block = hidden // n_mem
    out_sum = PlaneSum(place, sems, dw_out, own_out, bufs, (0, dw_out.shape[3]))
    spread_cot = Spread(
        place,
        sems,
        lambda k: cot_ref.at[flip(place.parity, k)],
        lambda k: cot_vm.at[pl.ds(seg * k, seg)],
    )
    spread_final = Spread(
        place,
        sems,
        lambda k: final_vm.at[pl.ds(seg * k, seg)],
        lambda k: final_out.at[place.parity],
    )

    def swap(src, dst):
        send, recv = sems.take(2)
        return remote(src, dst, send, recv, place.twin())

    def half_lanes(ref, i):
        wide = ref.shape[1] // 2
        return ref.at[:, pl.ds(i * wide, wide)]

    swap_co = swap(part_vm, twin_vm)
    swap_h2 = swap(h2_vm.at[pl.ds(0, own)], h2_vm.at[pl.ds(own, own)])
    swap_ffn = [swap(half_lanes(part_vm, i), half_lanes(twin_vm, i)) for i in range(2)]
    swap_df = swap(df_vm.at[pl.ds(0, own)], df_vm.at[pl.ds(own, own)])
    swap_dh2 = [swap(half_lanes(part_vm, i), half_lanes(twin_vm, i)) for i in range(2)]
    swap_dco = swap(dco_vm.at[pl.ds(0, own)], dco_vm.at[pl.ds(own, own)])

    for item in [ca, w_co] + pieces + [unit1, w_in]:
        item.start()
    place.meet(column_peers(n_mem) + plane_peers(plane))
    spread_cot.start()
    for item in pieces:
        item.get()
    for share in shares:
        share.start()
    row = {name: rows_ref[i : i + 1, :] for i, name in enumerate(("g0", "b6", "b5", "g1", "b7", "b9", "g2", "b8"))}
    sums_ref[...] = jnp.zeros_like(sums_ref)
    bias_sum[...] = jnp.zeros_like(bias_sum)

    def after(span):
        return pl.ds(pl.multiple_of(span.start + own, BLK), BLK)

    ca, w_co = ca.get(), w_co.get()

    def co_other(span):
        part_vm[span, :] = mm(ca[after(span), :], w_co[...]).astype(BF16)

    tiles(own, co_other)
    swap_co.start()
    unit1 = unit1.get()

    def co_own(span):
        p_vm[span, :] = unit1[span, :] * row["g0"] + row["b6"] + mm(ca[span, :], w_co[...])

    tiles(own, co_own)
    swap_co.wait()

    def second_norm(span):
        values = p_vm[span, :] + twin_vm[span, :].astype(F32) + row["b5"]
        unit, scale = unit_norm(values)
        unit_vm[span, :] = unit
        scale_vm[span, :] = jnp.broadcast_to(scale, (BLK, scale_vm.shape[1]))
        h2_vm[span, :] = (unit * row["g1"] + row["b7"]).astype(BF16)

    tiles(own, second_norm)
    swap_h2.start()
    w_in = w_in.get()

    def forward(span):
        def part(i, carry):
            lanes = pl.ds(pl.multiple_of(i * block, block), block)
            pre = mm(h2_vm[span, :], w_in[:, lanes]) + bias_ref[:, lanes]
            cdf = 0.5 * (1.0 + lax.erf(pre * 0.7071067811865476))
            act_vm[span, lanes] = (pre * cdf).astype(BF16)
            density = jnp.exp(-0.5 * pre * pre) * 0.3989422804014327
            slope_vm[span, lanes] = (cdf + pre * density).astype(BF16)
            return carry

        lax.fori_loop(0, n_mem, part, 0)

    ours, others = pl.ds(0, own), pl.ds(own, own)
    width = h2_vm.shape[1]
    column = width // 2
    forward(ours)
    for share in shares:
        share.forward()
    swap_h2.wait()
    forward(others)
    for share in shares:
        share.wait()
    for i in range(2):
        lanes = slice(i * column, (i + 1) * column)
        weights = out_w[0, :, :, :, lanes].reshape(hidden, column)
        part_vm[:, lanes] = mm(act_vm[others, :], weights).astype(BF16)
        swap_ffn[i].start()
    p_vm[...] = mm(act_vm[ours, :], out_w[0].reshape(hidden, width))
    for k in range(2):
        spread_cot.wait_recv(k)
    for copy in swap_ffn:
        copy.wait()

    def third_norm(span):
        values = (
            unit_vm[span, :] * row["g1"]
            + row["b7"]
            + p_vm[span, :]
            + twin_vm[span, :].astype(F32)
            + row["b9"]
        )
        unit, scale = unit_norm(values)
        final_vm[span, :] = (unit * row["g2"] + row["b8"]).astype(BF16)
        grad = cot_vm[span, :].astype(F32)
        out = unit_norm_back(grad, unit, scale, row["g2"])
        dz2_ref[span, :] = out
        low = out.astype(BF16)
        df_vm[span, :] = low
        sums_ref[0:1, :] += jnp.sum(grad * unit, axis=0, keepdims=True)
        sums_ref[1:2, :] += jnp.sum(grad, axis=0, keepdims=True)
        sums_ref[2:3, :] += jnp.sum(low.astype(F32), axis=0, keepdims=True)

    tiles(own, third_norm)
    swap_df.start()
    spread_final.start()
    swap_df.wait()

    def out_weights(m, carry):
        lanes = pl.ds(pl.multiple_of(m * block, block), block)
        dw_out[0, m] = mm(act_vm[:, lanes].T, df_vm[...]).astype(BF16).reshape(dw_out.shape[2:])
        return carry

    lax.fori_loop(0, n_mem, out_weights, 0)
    out_sum.start()

    def hidden_grad(i, carry):
        lanes = pl.ds(pl.multiple_of(i * block, block), block)
        weights = out_w[0, i].reshape(block, width)
        grad = mm(df_vm[...], weights, NT) * slope_vm[:, lanes].astype(F32)
        low = grad.astype(BF16)
        slope_vm[:, lanes] = low
        bias_sum[:, lanes] = jnp.sum(low.astype(F32), axis=0, keepdims=True)
        return carry

    lax.fori_loop(0, n_mem, hidden_grad, 0)
    narrow = width // 4
    for i in range(2):
        for j in (2 * i, 2 * i + 1):
            lanes = slice(j * narrow, (j + 1) * narrow)
            grad = mm(slope_vm[...], w_in[lanes, :], NT)
            part_vm[:, lanes] = grad[own:].astype(BF16)
            dz2_ref[:, lanes] += grad[:own]
        swap_dh2[i].start()
    out_sum.middle()
    for copy in swap_dh2:
        copy.wait()

    def second_back(span):
        grad = dz2_ref[span, :] + twin_vm[span, :].astype(F32)
        unit = unit_vm[span, :]
        out = unit_norm_back(grad, unit, scale_vm[span, :1], row["g1"])
        dz2_ref[span, :] = out
        low = out.astype(BF16)
        dco_vm[span, :] = low
        sums_ref[3:4, :] += jnp.sum(grad * unit, axis=0, keepdims=True)
        sums_ref[4:5, :] += jnp.sum(grad, axis=0, keepdims=True)
        sums_ref[5:6, :] += jnp.sum(low.astype(F32), axis=0, keepdims=True)

    tiles(own, second_back)
    swap_dco.start()
    depth = h2_vm.shape[1] // n_mem

    def in_weights(m, carry):
        lanes = pl.ds(pl.multiple_of(m * depth, depth), depth)
        dw_in[0, m] = mm(h2_vm[:, lanes].T, slope_vm[...]).astype(BF16).reshape(dw_in.shape[2:])
        return carry

    lax.fori_loop(0, n_mem, in_weights, 0)
    swap_dco.wait()

    dca_ref[...] = mm(dco_vm[...], w_co[...], NT).astype(BF16)
    heads = ca.shape[1] // n_mem

    def co_weights(m, carry):
        lanes = pl.ds(pl.multiple_of(m * heads, heads), heads)
        dw_co[0, m] = mm(ca[:, lanes].T, dco_vm[...]).astype(BF16).reshape(dw_co.shape[2:])
        return carry

    lax.fori_loop(0, n_mem, co_weights, 0)
    out_sum.end()
    out_sum.wait_send()
    spread_cot.wait_send()
    for k in range(2):
        spread_final.wait_recv(k)
    spread_final.wait_send()


def feed(n_mem, plane, cotangent, vectors, bias, ca, unit1, w_co, w_in, w_out):
    rows, part = ca.shape
    width, hidden = w_in.shape
    own = rows // 2

    def grad_shape(depth, cols):
        return (1, n_mem, plane, depth // (n_mem * plane), cols)

    out_shape, in_shape = grad_shape(hidden, width), grad_shape(width, hidden)
    shapes = [
        jax.ShapeDtypeStruct((2, own // 2, width), BF16),
        jax.ShapeDtypeStruct((rows, part), BF16),
        jax.ShapeDtypeStruct((own, width), F32),
        jax.ShapeDtypeStruct((8, width), F32),
        jax.ShapeDtypeStruct((1, hidden), F32),
        sum_shape(out_shape),
        jax.ShapeDtypeStruct(in_shape, BF16),
        jax.ShapeDtypeStruct(grad_shape(part, width), BF16),
    ]
    fetched = [ca, unit1, w_co, w_in, w_out]
    scratch = [pltpu.VMEM(item.shape, item.dtype) for item in fetched] + [
        pltpu.VMEM((own, width), BF16),
        pltpu.VMEM((rows, width), BF16),
        pltpu.VMEM((own, width), F32),
        pltpu.VMEM((own, 2 * HD), F32),
        pltpu.VMEM((rows, hidden), BF16),
        pltpu.VMEM((rows, hidden), BF16),
        pltpu.VMEM((own, width), F32),
        pltpu.VMEM((own, width), BF16),
        pltpu.VMEM((own, width), BF16),
        pltpu.VMEM((own, width), BF16),
        pltpu.VMEM((rows, width), BF16),
        pltpu.VMEM((rows, width), BF16),
        pltpu.VMEM(out_shape, BF16),
    ]
    scratch += plane_sum_scratch(out_shape, n_mem, out_shape[3])
    scratch += [pltpu.SemaphoreType.DMA((PLANE_SUM_SEMS + 60,))]
    return pl.pallas_call(
        functools.partial(feed_kernel, n_mem, plane),
        in_specs=[VMEM] * 3 + [ANY] * len(fetched),
        out_specs=[ANY] + [VMEM] * (len(shapes) - 1),
        out_shape=shapes,
        scratch_shapes=scratch,
        compiler_params=pltpu.CompilerParams(
            vmem_limit_bytes=60 * 2**20, collective_id=1, has_side_effects=True
        ),
        cost_estimate=pl.CostEstimate(
            flops=rows * width * hidden * 12, bytes_accessed=40 * 2**20, transcendentals=rows * hidden * 2
        ),
        name="feed",
    )(cotangent, vectors, bias, *fetched)


def middle_kernel(n_mem, plane, planes, settled, slot_ref, member_ref, index_ref, *refs):
    refs = Walk(refs)
    dq_ref, dk_ref, dv_ref, wc_ref, scale_ref, gain_ref = refs.take(6)
    fetched = refs.take(6)
    ready = refs.take(len(settled))
    dsa_ref, dz1_ref, sums_ref, enc_out, own_cross, own_so = refs.take(6)
    outs = refs.take(len(settled))
    kept = refs.take(6)
    wk_t, wv_t, named_ref = refs.take(3)
    theirs, mine, twin_in, pair_in, dw_cross, dw_so, part_vm, twin_vm, dso_vm = refs.take(9)
    cross_bufs, so_bufs = refs.take(3), refs.take(3)
    settle_bufs = [refs.take(3) for _ in settled]
    sems = Sems(refs.one())
    place = Place(plane, planes)
    fetches = [Fetch(sems, src, dst) for src, dst in zip(fetched, kept)]
    h1_ref, enc_ref, dz2_ref, unit_ref, so_ref, sa_ref = kept
    settles = [
        Settle(
            place, sems, ready[i], outs[i], settle_bufs[i], columns, n_mem, (0, ready[i].shape[2])
        )
        for i, columns in enumerate(settled)
    ]
    cross_sum = PlaneSum(place, sems, dw_cross, own_cross, cross_bufs, (0, dw_cross.shape[3]))
    so_sum = PlaneSum(place, sems, dw_so, own_so, so_bufs, (0, dw_so.shape[3]))
    passages = mine.shape[0]
    units = passages // 2
    twin_sems = sems.take(2 * passages)
    twins = [
        remote(theirs.at[u], twin_in.at[u], twin_sems[2 * u], twin_sems[2 * u + 1], place.twin())
        for u in range(passages)
    ]
    pair_sems = sems.take(2 * units)
    pairs = [
        remote(
            mine.at[units + u], pair_in.at[u], pair_sems[2 * u], pair_sems[2 * u + 1], place.pair()
        )
        for u in range(units)
    ]
    homes = [
        Spread(place, sems, lambda k, u=u: mine.at[u], lambda k, u=u: enc_out.at[u], kinds=(0,))
        for u in range(units)
    ]
    swap_sems = sems.take(4)
    own = dz2_ref.shape[0]
    swap_part = remote(part_vm, twin_vm, swap_sems[0], swap_sems[1], place.twin())
    swap_dso = remote(
        dso_vm.at[pl.ds(0, own)], dso_vm.at[pl.ds(own, own)], swap_sems[2], swap_sems[3], place.twin()
    )

    for item in fetches:
        item.start()
    wk_t[...] = wc_ref[1].T
    wv_t[...] = wc_ref[2].T
    place.meet(
        column_peers(n_mem) + plane_peers(plane) + [(2 * plane * r, 0) for r in range(1, planes)]
    )
    for item in settles:
        item.start()

    def passage_grad(u):
        slot = slot_ref[u]
        value = mm(dk_ref[slot], wk_t[...]) + mm(dv_ref[slot], wv_t[...])
        return (value * member_ref[u]).astype(BF16)

    def add_twin(u):
        twins[u].wait_recv()

        def add(i, carry):
            span = pl.ds(pl.multiple_of(i * 64, 64), 64)
            total = mine[u, span, :].astype(F32) + twin_in[u, span, :].astype(F32)
            mine[u, span, :] = total.astype(BF16)
            return carry

        lax.fori_loop(0, PLEN // 64, add, 0)

    def send_home(u):
        add_twin(u)
        pairs[u].wait_recv()

        def add(i, carry):
            span = pl.ds(pl.multiple_of(i * 64, 64), 64)
            total = mine[u, span, :].astype(F32) + pair_in[u, span, :].astype(F32)
            mine[u, span, :] = total.astype(BF16)
            return carry

        lax.fori_loop(0, PLEN // 64, add, 0)
        homes[u].start()

    for group in (range(units, passages), range(units)):
        for u in group:
            theirs[u] = passage_grad(passages + u)
            twins[u].start()
        for u in group:
            mine[u] = passage_grad(u)
        if group.start:
            for u in group:
                add_twin(u)
                pairs[u - units].start()

    for item in fetches:
        item.get()
    for j in range(index_ref.shape[0]):
        named_ref[j * PLEN : (j + 1) * PLEN, :] = enc_ref[index_ref[j]]

    part = dw_cross.shape[-1]
    depth = h1_ref.shape[1] // n_mem

    def stacked(ref):
        return ref[...].reshape(-1, ref.shape[-1])

    def cross_weights(m, carry):
        lanes = pl.ds(pl.multiple_of(m * depth, depth), depth)
        split = dw_cross.shape[2:]
        dw_cross[0, m] = (
            (mm(h1_ref[:, lanes].T, dq_ref[...]) * 0.125).astype(BF16).reshape(split)
        )
        named_t = named_ref[:, lanes].T
        dw_cross[1, m] = mm(named_t, stacked(dk_ref)).astype(BF16).reshape(split)
        dw_cross[2, m] = mm(named_t, stacked(dv_ref)).astype(BF16).reshape(split)
        return carry

    lax.fori_loop(0, n_mem // 2, cross_weights, 0)
    send_home(0)
    lax.fori_loop(n_mem // 2, n_mem, cross_weights, 0)
    cross_sum.start()

    part_vm[...] = (mm(dq_ref[own:, :], wc_ref[0], NT) * 0.125).astype(BF16)
    swap_part.start()
    dz1_ref[...] = dz2_ref[...] + mm(dq_ref[:own, :], wc_ref[0], NT) * 0.125
    sums_ref[...] = jnp.zeros_like(sums_ref)
    sums_ref[3:4, :part] = 0.125 * jnp.sum(dq_ref[...].astype(F32), axis=0, keepdims=True)
    sums_ref[4:5, :part] = jnp.sum(stacked(dv_ref).astype(F32), axis=0, keepdims=True)
    send_home(1)
    swap_part.wait()
    gain = gain_ref[...]

    def norm(span):
        grad = dz1_ref[span, :] + twin_vm[span, :].astype(F32)
        unit = unit_ref[span, :]
        inner = grad * gain
        out = (
            inner
            - jnp.mean(inner, axis=-1, keepdims=True)
            - unit * jnp.mean(inner * unit, axis=-1, keepdims=True)
        ) * scale_ref[span, :1]
        dz1_ref[span, :] = out
        low = out.astype(BF16)
        dso_vm[span, :] = low
        sums_ref[0:1, :] += jnp.sum(grad * unit, axis=0, keepdims=True)
        sums_ref[1:2, :] += jnp.sum(grad, axis=0, keepdims=True)
        sums_ref[2:3, :] += jnp.sum(low.astype(F32), axis=0, keepdims=True)

    tiles(own, norm)
    swap_dso.start()
    cross_sum.middle()

    dsa_ref[:own, :] = mm(dso_vm[:own, :], so_ref[...], NT).astype(BF16)
    for u in range(2, units):
        send_home(u)
    swap_dso.wait()
    dsa_ref[own:, :] = mm(dso_vm[own:, :], so_ref[...], NT).astype(BF16)
    block = sa_ref.shape[1] // n_mem

    def so_weights(m, carry):
        lanes = pl.ds(pl.multiple_of(m * block, block), block)
        dw_so[0, m] = (
            mm(sa_ref[:, lanes].T, dso_vm[...]).astype(BF16).reshape(dw_so.shape[2:])
        )
        return carry

    lax.fori_loop(0, n_mem, so_weights, 0)
    so_sum.start()
    for item in settles:
        item.middle()
    cross_sum.end()
    for item in settles:
        item.forward()
    so_sum.middle()
    for item in settles:
        item.end()
    so_sum.end()
    cross_sum.wait_send()
    so_sum.wait_send()
    for copy in twins + pairs:
        copy.wait_send()
    for item in homes:
        item.wait_recv(0)
        item.wait_send()


def middle(
    n_mem, plane, planes, slot, member, index, dq, dk, dv, wc, so, sa, h1, enc, dz2, unit, scale, gain, ready
):
    rows, part = dq.shape
    width = h1.shape[1]
    own = rows // 2
    passages = slot.shape[0] // 2
    settled = tuple(columns for _, columns in ready)
    settled_shapes = [item.shape[:2] + (plane,) + item.shape[2:] for item, _ in ready]
    cross_shape = (3, n_mem, plane, width // (n_mem * plane), part)
    so_shape = (1, n_mem, plane, part // (n_mem * plane), width)
    shapes = [
        jax.ShapeDtypeStruct((rows, part), BF16),
        jax.ShapeDtypeStruct((own, width), F32),
        jax.ShapeDtypeStruct((8, width), F32),
        jax.ShapeDtypeStruct((passages // 2, PLEN, width), BF16),
        sum_shape(cross_shape),
        sum_shape(so_shape),
    ] + [reduce_out(shape, columns, plane) for shape, columns in zip(settled_shapes, settled)]
    fetched = [h1, enc, dz2, unit, so, sa]
    scratch = [pltpu.VMEM(item.shape, item.dtype) for item in fetched] + [
        pltpu.VMEM((part, width), BF16),
        pltpu.VMEM((part, width), BF16),
        pltpu.VMEM(dk.shape[:1] + (width,), BF16),
        pltpu.VMEM((passages, PLEN, width), BF16),
        pltpu.VMEM((passages, PLEN, width), BF16),
        pltpu.VMEM((passages, PLEN, width), BF16),
        pltpu.VMEM((passages // 2, PLEN, width), BF16),
        pltpu.VMEM(cross_shape, BF16),
        pltpu.VMEM(so_shape, BF16),
        pltpu.VMEM((own, width), BF16),
        pltpu.VMEM((own, width), BF16),
        pltpu.VMEM((rows, width), BF16),
    ]
    scratch += plane_sum_scratch(cross_shape, n_mem, cross_shape[3])
    scratch += plane_sum_scratch(so_shape, n_mem, so_shape[3])
    for shape in settled_shapes:
        scratch += settle_scratch(shape, n_mem, plane, planes, shape[3])
    count = (
        len(ready) * settle_sems(n_mem, plane, planes) + 2 * PLANE_SUM_SEMS + 2 * passages
        + passages + 4 * passages // 2 + 4 + 6
    )
    smem = pl.BlockSpec(memory_space=pltpu.SMEM)
    outs = pl.pallas_call(
        functools.partial(middle_kernel, n_mem, plane, planes, settled),
        in_specs=[smem, smem, smem] + [VMEM] * 6 + [ANY] * 6 + [VMEM] * len(ready),
        out_specs=[VMEM] * 3 + [ANY] + [VMEM] * (2 + len(ready)),
        out_shape=shapes,
        scratch_shapes=scratch + [pltpu.SemaphoreType.DMA((count,))],
        compiler_params=pltpu.CompilerParams(
            vmem_limit_bytes=60 * 2**20, collective_id=3, has_side_effects=True
        ),
        cost_estimate=pl.CostEstimate(
            flops=rows * part * width * 30, bytes_accessed=40 * 2**20, transcendentals=0
        ),
        name="middle",
    )(
        slot,
        member,
        index,
        dq,
        dk.reshape(-1, PLEN, part),
        dv.reshape(-1, PLEN, part),
        wc,
        scale,
        gain,
        *fetched,
        *[item for item, _ in ready],
    )
    return outs[:4], outs[4:6], outs[6:]


def self_attend_back(place, pair, q_vm, k_vm, v_vm, o_vm, do_vm, lse_vm, outs, scratch):
    dq_vm, dk_vm, dv_vm = outs
    q_a, do_a, k_t, q_h, do_h, p_vm, ds_vm = scratch
    base = 2 * place.core + place.parity
    count = q_vm.shape[0] // BLK
    lanes = pl.ds(pl.multiple_of(pair * 2 * HD, 2 * HD), 2 * HD)

    def rows(i):
        return pl.ds(pl.multiple_of(flip(base, i) * BLK, BLK), BLK)

    for i in range(count):
        span = slice(i * BLK, (i + 1) * BLK)
        q_a[span, :] = q_vm[rows(i), lanes]
        do_a[span, :] = do_vm[rows(i), lanes]
        k_t[:, span] = k_vm[rows(i), lanes].T
        q_t = q_a[span, :].T
        do_t = do_a[span, :].T
        prod = (do_a[span, :].astype(F32) * o_vm[rows(i), lanes].astype(F32)).T
        for head in range(2):
            delta = jnp.sum(prod[head * HD : (head + 1) * HD, :], axis=0, keepdims=True)
            q_h[head, :, span] = head_rows(q_t, head, lse_vm[pair, head : head + 1, span])
            do_h[head, :, span] = head_rows(do_t, head, delta)
    key_pos = lax.broadcasted_iota(jnp.int32, (BLK, BLK), 0)
    query_pos = lax.broadcasted_iota(jnp.int32, (BLK, BLK), 1)
    units = [(j, i, head) for j in range(count) for head in range(2) for i in range(j, count)]

    def products(unit):
        j, i, head = unit
        span = slice(i * BLK, (i + 1) * BLK)
        return (
            mm(ones_in(k_vm[rows(j), lanes], head), q_h[head, :, span]),
            mm(ones_in(v_vm[rows(j), lanes], head), do_h[head, :, span]),
        )

    ready = products(units[0])
    halves = {}
    for n, (j, i, head) in enumerate(units):
        coming = products(units[n + 1]) if n + 1 < len(units) else None
        scores, dprobs = ready
        probs = jnp.exp(scores)
        if i == j:
            probs = jnp.where(key_pos <= query_pos, probs, 0.0)
        keys, span = slice(j * BLK, (j + 1) * BLK), slice(i * BLK, (i + 1) * BLK)
        p_vm[head, keys, span] = probs.astype(BF16)
        ds_vm[head, keys, span] = (probs * dprobs).astype(BF16)
        if i == count - 1:
            late = slice(j * BLK, count * BLK)
            halves[head] = (
                mm(p_vm[head, keys, late], do_a[late, :]),
                mm(ds_vm[head, keys, late], q_a[late, :]),
            )
            if head == 1:
                dv_vm[rows(j), lanes] = pick_heads(halves[0][0], halves[1][0]).astype(BF16)
                dk_vm[rows(j), lanes] = pick_heads(halves[0][1], halves[1][1]).astype(BF16)
        ready = coming
    for i in range(count):
        span, keys = slice(i * BLK, (i + 1) * BLK), slice(0, (i + 1) * BLK)
        dq_t = jnp.concatenate(
            [
                mm(k_t[head * HD : (head + 1) * HD, keys], ds_vm[head, keys, span])
                for head in range(2)
            ],
            axis=0,
        )
        dq_vm[rows(i), lanes] = dq_t.T.astype(BF16) * BF16(0.125)


def last_kernel(n_mem, plane, planes, settled, chunks, *refs):
    refs = Walk(refs)
    q_ref, k_ref, v_ref, o_ref, do_ref, lse_ref, feed_ref, hidden_ref, middle_ref = refs.take(9)
    fetched = refs.take(3)
    ready = refs.take(len(settled))
    small_out, dx_out, self_out = refs.take(3)
    outs = refs.take(len(settled))
    x_ref, w_ref, dz1_ref = kept = refs.take(3)
    dq_vm, dk_vm, dv_vm = refs.take(3)
    attend_scratch = refs.take(7)
    x_t, dw_vm = refs.take(2)
    part_vm, twin_vm, dx_vm = refs.take(3)
    chunk_own = [refs.one() for _ in range(chunks)]
    chunk_bufs = [refs.take(3) for _ in range(chunks)]
    chunk_settle = [refs.take(3) for _ in range(chunks)]
    settle_bufs = [refs.take(3) for _ in settled]
    small_near, small_line, small_twin, small_far, small_sum, sem_ref = refs.take(6)
    sems = Sems(sem_ref)
    place = Place(plane, planes)
    fetches = [Fetch(sems, src, dst) for src, dst in zip(fetched, kept)]
    settles = [
        Settle(
            place, sems, ready[i], outs[i], settle_bufs[i], columns, n_mem, (0, ready[i].shape[2])
        )
        for i, columns in enumerate(settled)
    ]
    rows, part = q_ref.shape
    lanes = part // chunks
    depth = dw_vm.shape[3]
    sums = [
        PlaneSum(
            place, sems, dw_vm, chunk_own[c], chunk_bufs[c], (0, depth), (c * lanes, lanes)
        )
        for c in range(chunks)
    ]
    ends = [
        Settle(
            place, sems, chunk_own[c], self_out, chunk_settle[c], True, n_mem, (0, depth), c * lanes
        )
        for c in range(chunks)
    ]
    near_sems = sems.take(6)
    near = [
        remote(
            small_sum, small_near.at[t - 1], near_sems[2 * t - 2], near_sems[2 * t - 1], place.near(t)
        )
        for t in range(1, plane)
    ]
    line = Line(
        place, sems, lambda s: small_sum.at[flip(place.mem, s)], lambda s: small_line.at[s - 1], n_mem
    )
    twin_sems = sems.take(2)
    twin = remote(small_sum.at[place.mem], small_twin, twin_sems[0], twin_sems[1], place.twin())
    far_sems = sems.take(2 * (planes - 1))
    far = [
        remote(
            small_sum.at[place.mem],
            small_far.at[r - 1],
            far_sems[2 * r - 2],
            far_sems[2 * r - 1],
            place.far(r),
        )
        for r in range(1, planes)
    ]
    seg = dx_out.shape[1]
    own = 2 * seg
    spread = Spread(
        place,
        sems,
        lambda k: dx_vm.at[pl.ds(seg * k, seg)],
        lambda k: dx_out.at[place.parity],
    )
    swap_sems = sems.take(2)
    swap_part = remote(part_vm, twin_vm, swap_sems[0], swap_sems[1], place.twin())

    for item in fetches:
        item.start()
    place.meet(
        column_peers(n_mem) + plane_peers(plane) + [(2 * plane * r, 0) for r in range(1, planes)]
    )
    for item in settles:
        item.start()
    block = x_ref.shape[1] // n_mem

    def input_part(span):
        return (
            mm(dq_vm[span, :], w_ref[0], NT)
            + mm(dk_vm[span, :], w_ref[1], NT)
            + mm(dv_vm[span, :], w_ref[2], NT)
        )

    pairs = part // (2 * HD)
    late = []
    for c in range(chunks):
        for pair in range(c * pairs // chunks, (c + 1) * pairs // chunks):
            self_attend_back(
                place,
                pair,
                q_ref,
                k_ref,
                v_ref,
                o_ref,
                do_ref,
                lse_ref,
                (dq_vm, dk_vm, dv_vm),
                attend_scratch,
            )
        if c == 0:
            for item in fetches:
                item.get()
            for m in range(n_mem):
                x_t[m] = x_ref[:, m * block : (m + 1) * block].T
        span = slice(c * lanes, (c + 1) * lanes)

        def weights(m, carry, span=span):
            for i, grad in enumerate((dq_vm, dk_vm, dv_vm)):
                dw_vm[i, m, :, :, span] = (
                    mm(x_t[m], grad[:, span]).astype(BF16).reshape(plane, depth, lanes)
                )
            return carry

        if c < chunks - 2:
            lax.fori_loop(0, n_mem, weights, 0)
            sums[c].start()
        if c == 1:
            sums[0].middle()
        if c == 2:
            for item in settles:
                item.middle()
            sums[0].end()
            ends[0].start()
            sums[1].middle()
        late.append(weights)
    part_vm[...] = input_part(slice(own, 2 * own)).astype(BF16)
    swap_part.start()
    lax.fori_loop(0, n_mem, late[-2], 0)
    sums[-2].start()
    swap_part.wait()
    total = dz1_ref[...] + input_part(slice(0, own)) + twin_vm[...].astype(F32)
    dx_vm[...] = total.astype(BF16)
    spread.start()
    lax.fori_loop(0, n_mem, late[-1], 0)
    sums[-1].start()
    sums[1].end()
    ends[1].start()
    for item in settles:
        item.forward()
    sums[-2].middle()

    small_sum[...] = jnp.zeros_like(small_sum)
    wide = small_sum.shape[2]
    unit = wide // 2
    first = place.core == 0
    for row, ref, at in (
        (2, middle_ref, 2),
        (5, feed_ref, 5),
        (6, middle_ref, 1),
        (7, feed_ref, 4),
        (8, feed_ref, 1),
        (9, feed_ref, 2),
        (10, middle_ref, 0),
        (11, feed_ref, 3),
        (12, feed_ref, 0),
    ):
        for b in range(n_mem):
            small_sum[b, row : row + 1, :] = ref[at : at + 1, b * wide : (b + 1) * wide]
    for row, value in (
        (0, jnp.sum(dq_vm[...].astype(F32), axis=0, keepdims=True)),
        (1, jnp.sum(dv_vm[...].astype(F32), axis=0, keepdims=True)),
        (3, middle_ref[3:4, :part]),
        (4, middle_ref[4:5, :part]),
    ):
        for b in range(n_mem):
            side = value[:, b * unit : (b + 1) * unit]
            none = jnp.zeros_like(side)
            small_sum[b, row : row + 1, :unit] = jnp.where(first, side, none)
            small_sum[b, row : row + 1, unit:] = jnp.where(first, none, side)
    count = hidden_ref.shape[1] // (n_mem * wide)
    for b in range(n_mem):
        for i in range(count):
            at = (b * count + i) * wide
            side = hidden_ref[:, at : at + wide]
            none = jnp.zeros_like(side)
            row = 13 + i
            small_sum[b, row : row + 1, :] = jnp.where(first, side, none)
            small_sum[b, row + count : row + count + 1, :] = jnp.where(first, none, side)
    for copy in near:
        copy.start()
    sums[-1].middle()
    sums[-2].end()
    ends[-2].start()
    ends[0].middle()
    for copy in near:
        copy.wait()
    total = small_sum[...]
    for t in range(plane - 1):
        total += small_near[t]
    small_sum[...] = total
    line.start()
    sums[-1].end()
    ends[-1].start()
    ends[1].middle()
    ends[0].forward()
    for item in settles:
        item.end()
    ends[-2].middle()
    ends[1].forward()
    for s in range(1, n_mem):
        line.wait_recv(s)
    line.wait_send()
    value = small_sum[place.mem]
    for s in range(n_mem - 1):
        value += small_line[s]
    small_sum[place.mem] = value
    twin.start()
    ends[-1].middle()
    ends[-2].forward()
    for item in ends[:-2]:
        item.end()
    twin.wait()
    value = small_sum[place.mem] + small_twin[...]
    if far:
        small_sum[place.mem] = value
        for copy in far:
            copy.start()
        for copy in far:
            copy.wait()
        for r in range(planes - 1):
            value += small_far[r]
    small_out[...] = value
    ends[-1].forward()
    ends[-2].end()
    ends[-1].end()
    for item in sums:
        item.wait_send()
    for k in range(2):
        spread.wait_recv(k)
    spread.wait_send()


def last(n_mem, plane, planes, q, k, v, o, do, lse, x, w, dz1, sums, small_shape, ready):
    rows, part = q.shape
    chunks = part // (2 * HD)
    width = x.shape[1]
    own = rows // 2
    settled = tuple(columns for _, columns in ready)
    settled_shapes = [item.shape[:2] + (plane,) + item.shape[2:] for item, _ in ready]
    grad_shape = (3, n_mem, plane, width // (n_mem * plane), part)
    depth, lanes = grad_shape[3], part // chunks
    small_part = small_shape[1:]
    shapes = [
        jax.ShapeDtypeStruct(small_part, F32),
        jax.ShapeDtypeStruct((2, own // 2, width), BF16),
        reduce_out(grad_shape, True, plane),
    ] + [reduce_out(shape, columns, plane) for shape, columns in zip(settled_shapes, settled)]
    fetched = [x, w, dz1]
    scratch = (
        [pltpu.VMEM(item.shape, item.dtype) for item in fetched]
        + [pltpu.VMEM((rows, part), BF16)] * 3
        + [
            pltpu.VMEM((rows, 2 * HD), BF16),
            pltpu.VMEM((rows, 2 * HD), BF16),
            pltpu.VMEM((2 * HD, rows), BF16),
            pltpu.VMEM((2, 2 * HD, rows), BF16),
            pltpu.VMEM((2, 2 * HD, rows), BF16),
            pltpu.VMEM((2, rows, rows), BF16),
            pltpu.VMEM((2, rows, rows), BF16),
            pltpu.VMEM((n_mem, width // n_mem, rows), BF16),
            pltpu.VMEM(grad_shape, BF16),
        ]
        + [pltpu.VMEM((own, width), BF16)] * 3
        + [pltpu.VMEM((3, n_mem, depth, lanes), BF16)] * chunks
    )
    for _ in range(chunks):
        scratch += plane_sum_scratch(grad_shape, n_mem, depth, lanes)
    for _ in range(chunks):
        scratch += settle_scratch(grad_shape, n_mem, plane, planes, depth, lanes)
    for shape in settled_shapes:
        scratch += settle_scratch(shape, n_mem, plane, planes, shape[3])
    scratch += [
        pltpu.VMEM((plane - 1,) + small_shape, F32),
        pltpu.VMEM((n_mem - 1,) + small_part, F32),
        pltpu.VMEM(small_part, F32),
        pltpu.VMEM((max(planes - 1, 1),) + small_part, F32),
        pltpu.VMEM(small_shape, F32),
        pltpu.SemaphoreType.DMA(
            (
                (len(ready) + chunks) * settle_sems(n_mem, plane, planes)
                + chunks * PLANE_SUM_SEMS
                + 24
                + 2 * planes,
            )
        ),
    ]
    outs = pl.pallas_call(
        functools.partial(last_kernel, n_mem, plane, planes, settled, chunks),
        in_specs=[VMEM] * 9 + [ANY] * 3 + [VMEM] * len(ready),
        out_specs=[VMEM, ANY, VMEM] + [VMEM] * len(ready),
        out_shape=shapes,
        scratch_shapes=scratch,
        compiler_params=pltpu.CompilerParams(
            vmem_limit_bytes=60 * 2**20, collective_id=4, has_side_effects=True
        ),
        cost_estimate=pl.CostEstimate(
            flops=rows * rows * width * 40, bytes_accessed=40 * 2**20, transcendentals=rows * rows * 8
        ),
        name="last",
    )(q, k, v, o, do, lse, *sums, *fetched, *[item for item, _ in ready])
    return outs[0], outs[1], outs[2:]


def cross_forward_kernel(n_mem, plane, kinds, index_ref, q_ref, k_ref, v_ref, *refs):
    refs = Walk(refs)
    count_w = len(kinds)
    shards = refs.take(count_w)
    o_ref, lse_ref = refs.take(2)
    halves = refs.take(count_w)
    v_t, o_t, sem_ref = refs.take(3)
    sems = Sems(sem_ref)
    place = Place(plane)
    step = pl.program_id(0) * pl.num_programs(1) + pl.program_id(1)
    last = pl.num_programs(0) * pl.num_programs(1) - 1
    gathers = [
        Gather(place, sems, shard, half, columns, n_mem, i != 1)
        for i, (shard, half, columns) in enumerate(zip(shards, halves, kinds))
    ]
    @pl.when(step == 0)
    def _():
        for gather in gathers:
            gather.own.start()
        place.meet(column_peers(n_mem) + plane_peers(plane))
        for gather in gathers:
            gather.begin()

    rows = q_ref.shape[0]
    count = index_ref.shape[0]

    @pl.when(pl.program_id(1) == 0)
    def _():
        for j in range(count):
            v_t[:, j * BLK : (j + 1) * BLK] = v_ref[index_ref[j]].T

    units = []
    for i in range(rows // BLK):
        q_t = q_ref[i * BLK : (i + 1) * BLK, :].T
        for head in range(2):
            q_head = head_rows(q_t, head)

            def score(j, q_head=q_head):
                return mm(k_ref[index_ref[j]], q_head)

            def value(j, head=head):
                return v_t[head * HD : (head + 1) * HD, j * BLK : (j + 1) * BLK]

            units.append(
                (
                    [functools.partial(score, j) for j in range(count)],
                    [functools.partial(value, j) for j in range(count)],
                    (i, head),
                )
            )

    def finish(tag, mixed, lse):
        i, head = tag
        span = slice(i * BLK, (i + 1) * BLK)
        o_t[head * HD : (head + 1) * HD, span] = mixed
        lse_ref[0, head : head + 1, span] = lse

    whole_one, line_one, small_one = gathers
    plan = {
        4: [(whole_one.share, 1), (small_one.share, 1)],
        6: [(line_one.share, 1)],
        10: [(whole_one.share, 2), (small_one.share, 2)],
        12: [(line_one.share, 2), (whole_one.forward, 1), (small_one.forward, 1)],
        17: [(whole_one.share, 3), (small_one.share, 3)],
        19: [(line_one.share, 3), (whole_one.forward, 2), (small_one.forward, 2)],
        24: [(whole_one.forward, 3), (small_one.forward, 3)],
    }

    def serve(n):
        for when, calls in plan.items():
            if when % len(units) == n:

                @pl.when(step == when // len(units))
                def _():
                    for call, hops in calls:
                        call(hops)

    softmax_units(units, finish, serve)
    o_ref[...] = o_t[...].T.astype(BF16)

    @pl.when(step == last)
    def _():
        for gather in gathers:
            gather.finish()


def cross_forward(n_mem, plane, index, q, k, v, params):
    rows, width = q.shape
    pairs = width // (2 * HD)
    keys = index.shape[0] * PLEN
    block = 2 * BLK
    question = pl.BlockSpec((block, 2 * HD), lambda h, i: (i, h))
    memory = pl.BlockSpec(k.shape[:2] + (2 * HD,), lambda h, i: (0, 0, h))
    kinds = tuple(columns for _, columns in params)
    views = [half_views(shard, columns, n_mem, plane) for shard, columns in params]
    outs = pl.pallas_call(
        functools.partial(cross_forward_kernel, n_mem, plane, kinds),
        grid=(pairs, rows // block),
        in_specs=[pl.BlockSpec(memory_space=pltpu.SMEM), question, memory, memory]
        + [whole(view.shape) for view, _ in views],
        out_specs=[question, pl.BlockSpec((1, 2, block), lambda h, i: (h, 0, i))]
        + [ANY] * len(params),
        out_shape=[
            jax.ShapeDtypeStruct((rows, width), BF16),
            jax.ShapeDtypeStruct((pairs, 2, rows), F32),
        ]
        + [jax.ShapeDtypeStruct(full, BF16) for _, full in views],
        scratch_shapes=[
            pltpu.VMEM((2 * HD, keys), BF16),
            pltpu.VMEM((2 * HD, block), F32),
            pltpu.SemaphoreType.DMA((4 + GATHER_SEMS * len(params),)),
        ],
        compiler_params=pltpu.CompilerParams(
            vmem_limit_bytes=60 * 2**20, collective_id=2, has_side_effects=True
        ),
        cost_estimate=pl.CostEstimate(
            flops=rows * keys * width * 16,
            bytes_accessed=rows * width * 4 + k.size * 4,
            transcendentals=rows * keys * pairs * 2,
        ),
        name="cross_forward",
    )(index, q, k, v, *[view for view, _ in views])
    return outs[:2], outs[2:]


def cross_backward_kernel(
    n_mem, plane, planes, chunks, settled, index_ref, q_ref, k_ref, v_ref, o_ref, do_ref, lse_ref, *refs
):
    refs = Walk(refs)
    kinds = {which: columns for which, columns, _ in chunks}
    grads = refs.take(len(kinds))
    ready = refs.take(len(settled))
    dq_ref, dk_ref, dv_ref = refs.take(3)
    outs = refs.take(len(kinds))
    ready_outs = refs.take(len(settled))
    q_h, do_h, dq_t, p_vm, ds_vm = refs.take(5)
    sems = Sems(refs.refs[-1])
    place = Place(plane, planes)
    sums, settles = [], []
    for which, columns, rows_of in chunks:
        own = refs.one()
        sums.append(PlaneSum(place, sems, grads[which], own, refs.take(3), rows_of))
        settles.append(
            Settle(place, sems, own, outs[which], refs.take(3), columns, n_mem, rows_of)
        )
    first = [
        Settle(
            place, sems, ready[i], ready_outs[i], refs.take(3), columns, n_mem, (0, ready[i].shape[2])
        )
        for i, columns in enumerate(settled)
    ]
    passage = pl.program_id(1)
    step = pl.program_id(0) * pl.num_programs(1) + passage
    steps = pl.num_programs(0) * pl.num_programs(1)
    rows = q_ref.shape[0]
    count = rows // BLK

    @pl.when(step == 0)
    def _():
        place.meet(
            column_peers(n_mem) + plane_peers(plane) + [(2 * plane * r, 0) for r in range(1, planes)]
        )
        for item in first:
            item.start()

    def at(when, *calls):
        @pl.when(step == when)
        def _():
            for call in calls:
                call()

    for i, (plane_sum, settle) in enumerate(zip(sums, settles)):
        at(3 * i, plane_sum.start)
        at(3 * i + 2, plane_sum.middle)
        at(3 * i + 4, plane_sum.end, settle.start)
        at(3 * i + 7, settle.middle)
        at(3 * i + 8, settle.forward)
    for item in first:
        at(6, item.middle)
        at(7, item.forward)

    @pl.when(passage == 0)
    def _():
        for i in range(count):
            span = slice(i * BLK, (i + 1) * BLK)
            q_t = q_ref[span, :].T
            grads_t = do_ref[span, :].T
            prod = (do_ref[span, :].astype(F32) * o_ref[span, :].astype(F32)).T
            for head in range(2):
                delta = jnp.sum(prod[head * HD : (head + 1) * HD, :], axis=0, keepdims=True)
                q_h[head, :, span] = head_rows(q_t, head, lse_ref[0, head : head + 1, span])
                do_h[head, :, span] = head_rows(grads_t, head, delta)
        dq_t[...] = jnp.zeros_like(dq_t)

    keys = dk_ref.shape[0] // BLK
    slots = [index_ref[passage * keys + j] for j in range(keys)]
    k_t = jnp.concatenate([k_ref[slot].T for slot in slots], axis=1)
    units = [(head, j, i) for head in range(2) for j in range(keys) for i in range(count)]

    def products(unit):
        head, j, i = unit
        span = slice(i * BLK, (i + 1) * BLK)
        return (
            mm(ones_in(k_ref[slots[j]], head), q_h[head, :, span]),
            mm(ones_in(v_ref[slots[j]], head), do_h[head, :, span]),
        )

    coming = products(units[0])
    halves = []
    for n, (head, j, i) in enumerate(units):
        scores, dprobs = coming
        if n + 1 < len(units):
            coming = products(units[n + 1])
        tile, span = slice(j * BLK, (j + 1) * BLK), slice(i * BLK, (i + 1) * BLK)
        probs = jnp.exp(scores)
        p_vm[head, tile, span] = probs.astype(BF16)
        ds_vm[head, tile, span] = (probs * dprobs).astype(BF16)
        if (j, i) == (keys - 1, count - 1):
            half = slice(head * HD, (head + 1) * HD)
            halves.append((mm(p_vm[head], do_ref[...]), mm(ds_vm[head], q_ref[...])))
            dq_t[half, :] += mm(k_t[half, :], ds_vm[head])
    dv_ref[...] = pick_heads(halves[0][0], halves[1][0]).astype(BF16)
    dk_ref[...] = pick_heads(halves[0][1], halves[1][1]).astype(BF16)

    @pl.when(passage == pl.num_programs(1) - 1)
    def _():
        dq_ref[...] = dq_t[...].T.astype(BF16)

    @pl.when(step == steps - 1)
    def _():
        for settle in first + settles:
            settle.end()
        for item in sums:
            item.wait_send()


def cross_backward(n_mem, plane, planes, index, q, k, v, o, do, lse, grads, ready):
    rows, width = q.shape
    pairs = width // (2 * HD)
    block = 2 * PLEN
    keys = index.shape[0] * PLEN
    passages = keys // block
    question = pl.BlockSpec((rows, 2 * HD), lambda h, u: (0, h))
    memory = pl.BlockSpec(k.shape[:2] + (2 * HD,), lambda h, u: (0, 0, h))
    grads_of = pl.BlockSpec((block, 2 * HD), lambda h, u: (u, h))
    shapes, chunks, scratch = [], [], []
    for which, (grad, columns, pieces) in enumerate(grads):
        lead, _, _, depth, cols = grad.shape
        count = depth // pieces
        shapes.append(reduce_out(grad.shape, columns, plane))
        for i in range(pieces):
            chunks.append((which, columns, (i * count, count)))
            scratch.append(pltpu.VMEM((lead, n_mem, count, cols), BF16))
            scratch += plane_sum_scratch(grad.shape, n_mem, count)
            scratch += settle_scratch(grad.shape, n_mem, plane, planes, count)
    settled = tuple(columns for _, columns in ready)
    for item, columns in ready:
        shape = item.shape[:2] + (plane,) + item.shape[2:]
        shapes.append(reduce_out(shape, columns, plane))
        scratch += settle_scratch(shape, n_mem, plane, planes, shape[3])
    outs = pl.pallas_call(
        functools.partial(cross_backward_kernel, n_mem, plane, planes, tuple(chunks), settled),
        grid=(pairs, passages),
        in_specs=[
            pl.BlockSpec(memory_space=pltpu.SMEM),
            question,
            memory,
            memory,
            question,
            question,
            pl.BlockSpec((1, 2, rows), lambda h, u: (h, 0, 0)),
        ]
        + [ANY] * len(grads)
        + [whole(item.shape) for item, _ in ready],
        out_specs=[question, grads_of, grads_of]
        + [whole(item.shape) for item in shapes],
        out_shape=[
            jax.ShapeDtypeStruct((rows, width), BF16),
            jax.ShapeDtypeStruct((keys, width), BF16),
            jax.ShapeDtypeStruct((keys, width), BF16),
        ]
        + shapes,
        scratch_shapes=[
            pltpu.VMEM((2, 2 * HD, rows), BF16),
            pltpu.VMEM((2, 2 * HD, rows), BF16),
            pltpu.VMEM((2 * HD, rows), F32),
            pltpu.VMEM((2, block, rows), BF16),
            pltpu.VMEM((2, block, rows), BF16),
        ]
        + scratch
        + [
            pltpu.SemaphoreType.DMA(
                (
                    len(chunks) * PLANE_SUM_SEMS
                    + (len(chunks) + len(ready)) * settle_sems(n_mem, plane, planes),
                )
            )
        ],
        compiler_params=pltpu.CompilerParams(
            vmem_limit_bytes=56 * 2**20, collective_id=5, has_side_effects=True
        ),
        cost_estimate=pl.CostEstimate(
            flops=rows * keys * width * 40,
            bytes_accessed=rows * width * 10 + k.size * 8,
            transcendentals=rows * keys * pairs * 2,
        ),
        name="cross_backward",
    )(index, q, k, v, o, do, lse, *[item[0] for item in grads], *[item for item, _ in ready])
    return outs[:3], outs[3:]


def widen_kernel(*refs):
    count = len(refs) // 2
    for src, dst in zip(refs[:count], refs[count:]):
        dst[...] = src[...].astype(F32)


def widen(pairs):
    steps = 8
    flats = [value.reshape(-1, like.shape[-1]) for value, like in pairs]
    blocks = [
        pl.BlockSpec((item.shape[0] // steps, item.shape[1]), lambda i: (i, 0)) for item in flats
    ]
    outs = pl.pallas_call(
        widen_kernel,
        grid=(steps,),
        in_specs=blocks,
        out_specs=blocks,
        out_shape=[jax.ShapeDtypeStruct(item.shape, F32) for item in flats],
        compiler_params=pltpu.CompilerParams(vmem_limit_bytes=60 * 2**20),
        cost_estimate=pl.CostEstimate(
            flops=0, bytes_accessed=6 * sum(item.size for item in flats), transcendentals=0
        ),
        name="widen",
    )(*flats)
    return [out.reshape(like.shape) for out, (_, like) in zip(outs, pairs)]


def body(
    hidden_in,
    encoder_rows,
    passage_map,
    self_qkv,
    self_out,
    cross_qkv,
    cross_out,
    ffn_in,
    ffn_out,
    ffn_in_bias,
    biases,
    gains,
    cotangent,
):
    n_pb = lax.axis_size("pb")
    n_mem = lax.axis_size("mem")
    columns = n_pb // 2
    plane = min(columns, 4)
    pb = lax.axis_index("pb")
    core = pb % 2
    width = hidden_in.shape[2]
    planes = columns // plane

    enc_local = encoder_rows.reshape(-1, PLEN, width)
    n_bias, n_gain = biases.shape[0], gains.shape[0]
    small = jnp.concatenate([biases, gains, ffn_in_bias.reshape(-1, biases.shape[1])], axis=0)
    n_small = small.shape[0]
    small_rows = -(-n_small // 16) * 16
    small = jnp.pad(small, ((0, small_rows - n_small), (0, 0)))
    rows_out, halves, kept = front(
        n_mem,
        plane,
        (n_bias, n_gain),
        hidden_in,
        enc_local,
        passage_map,
        small,
        [(self_qkv, True), (self_out, False), (cross_qkv, True)],
    )
    x_full, enc_full, index, small = rows_out
    sq, sk, sv, sa, self_lse, h1_full, unit1, scale1, cq, ck, cv = kept
    index = index.reshape(-1)

    def flat(half):
        lead, _, _, _, cols = half.shape
        return half.reshape(lead, -1, cols)

    w_self, w_cross = flat(halves[0]), flat(halves[2])
    w_self_out = flat(halves[1])[0]
    small = small.astype(F32)
    vectors = small[:, : n_bias + n_gain].transpose(1, 0, 2).reshape(n_bias + n_gain, width)
    bias, gain = vectors[:n_bias], vectors[n_bias:]
    ffn_bias = small[:, n_bias + n_gain : n_small].reshape(-1)

    def half_of(vector):
        parts = vector.reshape(n_mem, 2, -1)
        return jnp.where(core == 0, parts[:, 0], parts[:, 1]).reshape(-1)

    order = jnp.arange(encoder_rows.shape[1] * n_mem, dtype=jnp.int32)
    hits = index[None, :] == order[:, None]
    member = jnp.any(hits, axis=1).astype(F32)
    slot = jnp.sum(jnp.where(hits, jnp.arange(index.shape[0], dtype=jnp.int32)[None], 0), axis=1)
    (ca, cross_lse), halves = cross_forward(
        n_mem,
        plane,
        index,
        cq,
        ck,
        cv,
        [(ffn_in[None], True), (ffn_out, False), (cross_out, False)],
    )
    w_ffn_in, w_ffn_out, w_cross_out = flat(halves[0])[0], halves[1], flat(halves[2])[0]

    rows_of = jnp.stack(
        [gain[0], bias[6], bias[5], gain[1], bias[7], bias[9], gain[2], bias[8]]
    )
    layer_out, dca, dz2, feed_sums, hidden_sums, own_ffn_out, dw_ffn_in, dw_cross_out = feed(
        n_mem,
        plane,
        cotangent,
        rows_of,
        half_of(ffn_bias)[None],
        ca,
        unit1,
        w_cross_out,
        w_ffn_in,
        w_ffn_out,
    )
    (dcq, dck, dcv), ffn_sums = cross_backward(
        n_mem,
        plane,
        planes,
        index,
        cq,
        ck,
        cv,
        ca,
        dca,
        cross_lse,
        [(dw_ffn_in, True, 2), (dw_cross_out, False, 1)],
        [(own_ffn_out, False)],
    )
    (dsa, dz1, middle_sums, enc_sum), (own_cross, own_so), _ = middle(
        n_mem,
        plane,
        planes,
        slot,
        member,
        index,
        dcq,
        dck,
        dcv,
        w_cross,
        w_self_out,
        sa,
        h1_full,
        enc_full.reshape(-1, PLEN, width),
        dz2,
        unit1,
        scale1,
        gain[0][None],
        [],
    )

    vec, dx, sums = last(
        n_mem,
        plane,
        planes,
        sq,
        sk,
        sv,
        sa,
        dsa,
        self_lse,
        x_full,
        w_self,
        dz1,
        [feed_sums, hidden_sums, middle_sums],
        small.shape,
        [(own_so, False), (own_cross, True)],
    )
    (
        grad_in,
        grad_encoder,
        out_self_qkv,
        out_self_out,
        out_cross_qkv,
        out_cross_out,
        out_ffn_in,
        out_ffn_out,
    ) = widen(
        [
            (dx, hidden_in),
            (enc_sum, encoder_rows),
            (sums[0], self_qkv),
            (sums[1], self_out),
            (sums[2], cross_qkv),
            (ffn_sums[1], cross_out),
            (ffn_sums[0], ffn_in),
            (ffn_sums[2], ffn_out),
        ]
    )
    out_ffn_bias = vec[n_bias + n_gain : n_small].reshape(-1)
    return (
        layer_out,
        grad_in,
        grad_encoder,
        out_self_qkv,
        out_self_out,
        out_cross_qkv,
        out_cross_out,
        out_ffn_in,
        out_ffn_out,
        out_ffn_bias,
        vec[:n_bias],
        vec[n_bias : n_bias + n_gain],
    )


def solution(mesh):
    placed = (
        P("pb", "mem", None),
        P("pb", "mem", None, None),
        P("pb", None),
        P(None, "mem", None),
        P("mem", None),
        P(None, "mem", None),
        P("mem", None),
        P("mem", None),
        P("mem", None),
        P("mem"),
        P(None, "mem"),
        P(None, "mem"),
        P("pb", "mem", None),
    )
    return jax.shard_map(
        body,
        mesh=mesh,
        in_specs=placed,
        out_specs=(
            P("pb", "mem", None),
            P("pb", "mem", None),
            P("pb", "mem", None, None),
            P(None, "mem", None),
            P("mem", None),
            P(None, "mem", None),
            P("mem", None),
            P("mem", None),
            P("mem", None),
            P("mem"),
            P(None, "mem"),
            P(None, "mem"),
        ),
        check_vma=False,
    )
```

time: 2940 us -> 550 us (0.19)
  waiting for transfers between devices: 1570 us -> 0 us
  matrix products: 584 us -> 0 us
  Pallas kernels: 0 us -> 531 us
  blocking collectives: 381 us -> 0 us
  other arithmetic: 178 us -> 3.38 us
  local copies, waits for them, and re-layouts: 178 us -> 5.6 us
    reduce_scatter x11 -> x0, waiting for transfers between devices: 910 us -> none  [the longest x1 147 us: body(): lax.psum_scatter(grad_w_ffn_out.astype(jnp.bfloat16), 'mem', scatter_dime...]
    all_gather x10 -> x0, waiting for transfers between devices: 656 us -> none  [the longest x1 121 us: body(): lax.all_gather(ffn_out, 'mem', axis=0, tiled=True)]
    dot_general x77 -> x0, matrix products: 584 us -> none  [the longest x8 96.4 us: block_scores(): jnp.einsum('bqhe,khe->bhqk', query_part, key_part, preferred_element_type...]
    pallas_call x0 -> x7, Pallas kernels: none -> 531 us  [the longest x1 117 us: front(): pl.pallas_call(functools.partial(front_kernel, n_mem, plane, kinds, place...]
    psum x1 -> x0, blocking collectives: 330 us -> none  [body(): lax.psum((local_sums[0], local_sums[1], local_sums[2], local_sums[3], loc...]
    convert_element_type x14 -> x2, other arithmetic: 101 us -> 1.37 us  [the longest x1 0.85 us: body(): small = small.astype(F32)]
    reduce_sum x23 -> x1, other arithmetic: 67 us -> 0.59 us  [body(): jnp.sum(jnp.where(hits, jnp.arange(index.shape[0], dtype=jnp.int32)[None]...]
    all_gather x3 -> x0, blocking collectives: 39.2 us -> none  [the longest x1 15 us: body(): lax.all_gather(biases, 'mem', axis=1, tiled=True)]
  transfers between devices with their start and end apart: 22 -> 0, of which waited for: 20 -> 0; matrix products, arithmetic and copies ran while one was open for 14% -> 0% of each run, Pallas kernels for 0% -> 0%
where the time goes in v1:
time: 550 us; the launch traced here: 541 us
  Pallas kernels  531 us (97%)
  local copies, waits for them, and re-layouts  5.6 us (1%)
    pallas_call x1, Pallas kernels, front(): pl.pallas_call(functools.partial(front_kernel, n_mem, plane, kinds, place...  117 us
    pallas_call x1, Pallas kernels, last(): pl.pallas_call(functools.partial(last_kernel, n_mem, plane, planes, settl...  92.5 us
    pallas_call x1, Pallas kernels, cross_backward(): pl.pallas_call(functools.partial(cross_backward_kernel, n_mem, plane, pla...  89.7 us
    pallas_call x1, Pallas kernels, feed(): pl.pallas_call(functools.partial(feed_kernel, n_mem, plane), in_specs=[VM...  86.5 us
    pallas_call x1, Pallas kernels, middle(): pl.pallas_call(functools.partial(middle_kernel, n_mem, plane, planes, set...  72.4 us
    pallas_call x1, Pallas kernels, cross_forward(): pl.pallas_call(functools.partial(cross_forward_kernel, n_mem, plane, kind...  60.8 us
    pallas_call x1, Pallas kernels, widen(): pl.pallas_call(widen_kernel, grid=(steps,), in_specs=blocks, out_specs=bl...  12.5 us

profile of v1, /device:TPU:0, one launch (start us, length us, event | category | flops | bytes accessed | tf_op | source)
XLA Modules:
  0.0 541.4 jit_solution(14599201333540224221)
XLA Ops:
  0.6 0.7 reshape.133
  1.3 1.3 fusion.4.small_ref
  2.7 116.8 %front.1 = (bf16[1024,1024]{1,0:T(8,128)(2,1)}, bf16[4,3,256,1024]{3,2,1,0:T(8,128)(2,1)}, s32[1,8]{1,0:T(1,128)}, bf16[4,32,256]{2,1,0:T(8,128)(2,1)}, bf16[3,4...) custom-call(bf16[2,256,1024]{2,1,0:T(8,128)(2,1)} %x_ref.1, ...), custom_call_target="tpu_custom_call" | custom-call | flops 5368709120 | bytes 41943040 | tf_op jit(solution)/shard_map/front/pallas_call | solution.py:776
  119.5 0.9 convert_element_type.8
  120.4 0.0 copy-start.2
  120.4 0.7 stack.3.rows_ref
  121.1 0.8 slice.114
  121.9 0.6 copy.31
  122.5 60.8 %cross_forward.1 = (bf16[1024,512]{1,0:T(8,128)(2,1)}, f32[4,2,1024]{2,1,0:T(2,128)}, bf16[1,4,4,64,2048]{4,3,2,1,0:T(8,128)(2,1)}, bf16[1,4,4,128,1024]{4,3,2,1,0:T(8,128)(2,1)}, bf16[1,4,4,32,1024]{4,3,2,1,0:T(8,128)(2,1)}) custom-call(s32[8]{0:T(128)} %bitcast.83, bf16[1024,512]{1,0:T(8,128)(2,1)} %get-tuple-element.70.q_ref, ...), custom_call_target="tpu_custom_call" | custom-call | flops 17179869184 | bytes 8388608 | tf_op jit(solution)/shard_map/cross_forward/pallas_call | solution.py:2057
  183.4 0.0 copy-done.2
  183.4 86.5 %feed.1 = (bf16[2,256,1024]{2,1,0:T(8,128)(2,1)}, bf16[1024,512]{1,0:T(8,128)(2,1)}, f32[512,1024]{1,0:T(8,128)}, f32[8,1024]{1,0:T(8,128)}, f32[1,2048]{1,0:T(1...) custom-call(bf16[2,256,1024]{2,1,0:T(8,128)(2,1)} %cot_ref.1, ...), custom_call_target="tpu_custom_call" | custom-call | flops 25769803776 | bytes 41943040 | tf_op jit(solution)/shard_map/feed/pallas_call | solution.py:1306
  269.9 0.0 copy-start.3
  269.9 89.7 %cross_backward.1 = (bf16[1024,512]{1,0:T(8,128)(2,1)}, bf16[2048,512]{1,0:T(8,128)(2,1)}, bf16[2048,512]{1,0:T(8,128)(2,1)}, bf16[1,4,64,4096]{3,2,1,0:T(8,128)...) custom-call(s32[8]{0:T(128)} %bitcast.84, bf16[1024,512]{1,0:T(8,128)(2,1)} %get-tuple-element.70.q_ref, ...), custom_call_target="tpu_custom_call" | custom-call | flops 42949672960 | bytes 17825792 | tf_op jit(solution)/shard_map/cross_backward/pallas_call | solution.py:2222
  359.5 0.0 copy-done.3
  359.5 0.1 fusion.6
  359.6 0.5 convert_element_type.9.member_ref
  360.1 0.6 select_reduce_fusion.slot_ref
  360.7 72.4 %middle.1 = (bf16[1024,512]{1,0:T(8,128)(2,1)}, f32[512,1024]{1,0:T(8,128)}, f32[8,1024]{1,0:T(8,128)}, bf16[3,256,1024]{2,1,0:T(8,128)(2,1)}, bf16[3,4,64,512]{...) custom-call(s32[12]{0:T(128)} %select_reduce_fusion.slot_ref, f32[12]{0:T(128)} %convert_element_type.9.member_ref, ...), custom_call_target="tpu_custom_call" | custom-call | flops 16106127360 | bytes 41943040 | tf_op jit(solution)/shard_map/middle/pallas_call | solution.py:1555
  433.1 92.5 %last.1 = (f32[32,256]{1,0:T(8,128)}, bf16[2,256,1024]{2,1,0:T(8,128)(2,1)}, bf16[3,4,64,1024]{3,2,1,0:T(8,128)(2,1)}, bf16[2,4,32,1024]{3,2,1,0:T(8,128)(2,1)}, bf16[3,4,64,1024]{3,2,1,0:T(8,128)(2,1)}) custom-call(bf16[1024,512]{1,0:T(8,128)(2,1)} %get-tuple-element.79.refs_0_, bf16[1024,512]{1,0:T(8,128)(2,1)} %get-tuple-element.80.refs_1_, ...), custom_call_target="tpu_custom_call" | custom-call | flops 42949672960 | bytes 41943040 | tf_op jit(solution)/shard_map/last/pallas_call | solution.py:1945
  525.7 0.0 copy-start.1
  525.7 0.0 copy-start
  525.7 12.5 %widen.1 = (f32[512,1024]{1,0:T(8,128)}, f32[768,1024]{1,0:T(8,128)}, f32[768,1024]{1,0:T(8,128)}, f32[256,1024]{1,0:T(8,128)}, f32[768,1024]{1,0:T(8,128)}, /*i...) custom-call(bf16[512,1024]{1,0:T(8,128)(2,1)} %bitcast.50, bf16[768,1024]{1,0:T(8,128)(2,1)} %bitcast.47, ...), custom_call_target="tpu_custom_call" | custom-call | bytes 33030144 | tf_op jit(solution)/shard_map/widen/pallas_call | solution.py:2285
  538.2 0.0 copy-done.1
  538.2 0.6 slice.103
  538.8 0.6 copy.32
  539.4 0.6 slice.104
  540.0 0.0 copy-done
  540.0 1.0 copy.38
  (6 shorter events, 0.1 us)
Async XLA Ops:
  120.4 63.0 %copy-start.2 = (f32[1,4,256]{2,0,1:T(1,128)}, f32[1,4,256]{2,0,1:T(1,128)S(1)}, u32[]{:S(2)}) copy-start(f32[1,4,256]{2,0,1:T(1,128)S(1)} %get-tuple-element.131) | copy-start | bytes 12292
  269.9 89.7 %copy-start.3 = (s32[1,8]{1,0:T(1,128)S(1)}, s32[1,8]{1,0:T(1,128)}, u32[]{:S(2)}) copy-start(s32[1,8]{1,0:T(1,128)} %get-tuple-element.69) | copy-start | bytes 100
  525.7 12.5 %copy-start.1 = (f32[32,256]{1,0:T(8,128)S(1)}, f32[32,256]{1,0:T(8,128)}, u32[]{:S(2)}) copy-start(f32[32,256]{1,0:T(8,128)} %get-tuple-element.123) | copy-start | bytes 98308
  525.7 14.3 %copy-start = (bf16[2,256,1024]{2,1,0:T(8,128)(2,1)S(1)}, bf16[2,256,1024]{2,1,0:T(8,128)(2,1)}, u32[]{:S(2)}) copy-start(bf16[2,256,1024]{2,1,0:T(8,128)(2,1)} %get-tuple-element.146) | copy-start | bytes 3145732

commit v2 on v1

--- a/solution.py
+++ b/solution.py
@@ -560,12 +560,14 @@
         twin[k].start()
     for gather in gathers:
         gather.share(3)
-    for u in range(units):
+    def send_passage(u):
         encs[u].start()
 
         @pl.when(home)
         def _():
             enc_pairs[u].start()
+
+    send_passage(0)
 
     def first_arrival(u):
         encs[u].wait_recv(0)
@@ -587,11 +589,14 @@
 
         enc_ends[u].start()
 
-    for hops in (2, 3):
-        gathers[0].forward(hops)
+    gathers[0].forward(2)
+    gathers[0].forward(3)
+    send_passage(1)
     for hops in (1, 2, 3):
         for gather in gathers[1:]:
             gather.forward(hops)
+    for u in range(2, units):
+        send_passage(u)
     for copy in twin:
         copy.wait_recv()
     small_own.wait()
@@ -1040,14 +1045,14 @@
     ) * scale
 
 
-def feed_kernel(n_mem, plane, cot_ref, rows_ref, bias_ref, *refs):
+def feed_kernel(n_mem, plane, cot_vm, rows_ref, bias_ref, *refs):
     refs = Walk(refs)
     fetched = refs.take(4)
     out_part = refs.one()
     final_out, dca_ref, dz2_ref, sums_ref, bias_sum, own_out, dw_in, dw_co = refs.take(8)
     kept = refs.take(4)
     out_w = refs.one()
-    cot_vm, h2_vm, unit_vm, scale_vm, act_vm, slope_vm, p_vm, part_vm, twin_vm = refs.take(9)
+    h2_vm, unit_vm, scale_vm, act_vm, slope_vm, p_vm, part_vm, twin_vm = refs.take(8)
     final_vm, df_vm, dco_vm, dw_out = refs.take(4)
     bufs = refs.take(3)
     sems = Sems(refs.one())
@@ -1070,12 +1075,6 @@
     hidden = act_vm.shape[1]
     block = hidden // n_mem
     out_sum = PlaneSum(place, sems, dw_out, own_out, bufs, (0, dw_out.shape[3]))
-    spread_cot = Spread(
-        place,
-        sems,
-        lambda k: cot_ref.at[flip(place.parity, k)],
-        lambda k: cot_vm.at[pl.ds(seg * k, seg)],
-    )
     spread_final = Spread(
         place,
         sems,
@@ -1101,7 +1100,6 @@
     for item in [ca, w_co] + pieces + [unit1, w_in]:
         item.start()
     place.meet(column_peers(n_mem) + plane_peers(plane))
-    spread_cot.start()
     for item in pieces:
         item.get()
     for share in shares:
@@ -1167,8 +1165,6 @@
         part_vm[:, lanes] = mm(act_vm[others, :], weights).astype(BF16)
         swap_ffn[i].start()
     p_vm[...] = mm(act_vm[ours, :], out_w[0].reshape(hidden, width))
-    for k in range(2):
-        spread_cot.wait_recv(k)
     for copy in swap_ffn:
         copy.wait()
 
@@ -1260,7 +1256,6 @@
     lax.fori_loop(0, n_mem, co_weights, 0)
     out_sum.end()
     out_sum.wait_send()
-    spread_cot.wait_send()
     for k in range(2):
         spread_final.wait_recv(k)
     spread_final.wait_send()
@@ -1287,7 +1282,6 @@
     ]
     fetched = [ca, unit1, w_co, w_in, w_out]
     scratch = [pltpu.VMEM(item.shape, item.dtype) for item in fetched] + [
-        pltpu.VMEM((own, width), BF16),
         pltpu.VMEM((rows, width), BF16),
         pltpu.VMEM((own, width), F32),
         pltpu.VMEM((own, 2 * HD), F32),
@@ -1959,17 +1953,24 @@
     return outs[0], outs[1], outs[2:]
 
 
-def cross_forward_kernel(n_mem, plane, kinds, index_ref, q_ref, k_ref, v_ref, *refs):
+def cross_forward_kernel(n_mem, plane, kinds, index_ref, q_ref, k_ref, v_ref, cot_ref, *refs):
     refs = Walk(refs)
     count_w = len(kinds)
     shards = refs.take(count_w)
-    o_ref, lse_ref = refs.take(2)
+    o_ref, lse_ref, cot_out = refs.take(3)
     halves = refs.take(count_w)
     v_t, o_t, sem_ref = refs.take(3)
     sems = Sems(sem_ref)
     place = Place(plane)
     step = pl.program_id(0) * pl.num_programs(1) + pl.program_id(1)
     last = pl.num_programs(0) * pl.num_programs(1) - 1
+    seg = cot_ref.shape[1]
+    spread = Spread(
+        place,
+        sems,
+        lambda k: cot_ref.at[flip(place.parity, k)],
+        lambda k: cot_out.at[pl.ds(seg * k, seg)],
+    )
     gathers = [
         Gather(place, sems, shard, half, columns, n_mem, i != 1)
         for i, (shard, half, columns) in enumerate(zip(shards, halves, kinds))
@@ -2016,15 +2017,16 @@
         o_t[head * HD : (head + 1) * HD, span] = mixed
         lse_ref[0, head : head + 1, span] = lse
 
-    whole_one, line_one, small_one = gathers
+    whole_one, line_one = gathers
     plan = {
-        4: [(whole_one.share, 1), (small_one.share, 1)],
-        6: [(line_one.share, 1)],
-        10: [(whole_one.share, 2), (small_one.share, 2)],
-        12: [(line_one.share, 2), (whole_one.forward, 1), (small_one.forward, 1)],
-        17: [(whole_one.share, 3), (small_one.share, 3)],
-        19: [(line_one.share, 3), (whole_one.forward, 2), (small_one.forward, 2)],
-        24: [(whole_one.forward, 3), (small_one.forward, 3)],
+        4: [lambda: whole_one.share(1)],
+        6: [lambda: line_one.share(1)],
+        10: [lambda: whole_one.share(2), lambda: whole_one.forward(1)],
+        12: [lambda: line_one.share(2)],
+        14: [spread.start],
+        17: [lambda: whole_one.share(3), lambda: whole_one.forward(2)],
+        19: [lambda: line_one.share(3)],
+        23: [lambda: whole_one.forward(3)],
     }
 
     def serve(n):
@@ -2033,8 +2035,8 @@
 
                 @pl.when(step == when // len(units))
                 def _():
-                    for call, hops in calls:
-                        call(hops)
+                    for call in calls:
+                        call()
 
     softmax_units(units, finish, serve)
     o_ref[...] = o_t[...].T.astype(BF16)
@@ -2043,9 +2045,12 @@
     def _():
         for gather in gathers:
             gather.finish()
-
-
-def cross_forward(n_mem, plane, index, q, k, v, params):
+        for k in range(2):
+            spread.wait_recv(k)
+        spread.wait_send()
+
+
+def cross_forward(n_mem, plane, index, q, k, v, cotangent, params):
     rows, width = q.shape
     pairs = width // (2 * HD)
     keys = index.shape[0] * PLEN
@@ -2057,13 +2062,20 @@
     outs = pl.pallas_call(
         functools.partial(cross_forward_kernel, n_mem, plane, kinds),
         grid=(pairs, rows // block),
-        in_specs=[pl.BlockSpec(memory_space=pltpu.SMEM), question, memory, memory]
+        in_specs=[
+            pl.BlockSpec(memory_space=pltpu.SMEM),
+            question,
+            memory,
+            memory,
+            whole(cotangent.shape),
+        ]
         + [whole(view.shape) for view, _ in views],
-        out_specs=[question, pl.BlockSpec((1, 2, block), lambda h, i: (h, 0, i))]
+        out_specs=[question, pl.BlockSpec((1, 2, block), lambda h, i: (h, 0, i)), ANY]
         + [ANY] * len(params),
         out_shape=[
             jax.ShapeDtypeStruct((rows, width), BF16),
             jax.ShapeDtypeStruct((pairs, 2, rows), F32),
+            jax.ShapeDtypeStruct((2 * cotangent.shape[1], cotangent.shape[2]), BF16),
         ]
         + [jax.ShapeDtypeStruct(full, BF16) for _, full in views],
         scratch_shapes=[
@@ -2080,8 +2092,8 @@
             transcendentals=rows * keys * pairs * 2,
         ),
         name="cross_forward",
-    )(index, q, k, v, *[view for view, _ in views])
-    return outs[:2], outs[2:]
+    )(index, q, k, v, cotangent, *[view for view, _ in views])
+    return outs[:3], outs[3:]
 
 
 def cross_backward_kernel(
@@ -2335,7 +2347,7 @@
         enc_local,
         passage_map,
         small,
-        [(self_qkv, True), (self_out, False), (cross_qkv, True)],
+        [(self_qkv, True), (self_out, False), (cross_qkv, True), (cross_out, False)],
     )
     x_full, enc_full, index, small = rows_out
     sq, sk, sv, sa, self_lse, h1_full, unit1, scale1, cq, ck, cv = kept
@@ -2346,7 +2358,7 @@
         return half.reshape(lead, -1, cols)
 
     w_self, w_cross = flat(halves[0]), flat(halves[2])
-    w_self_out = flat(halves[1])[0]
+    w_self_out, w_cross_out = flat(halves[1])[0], flat(halves[3])[0]
     small = small.astype(F32)
     vectors = small[:, : n_bias + n_gain].transpose(1, 0, 2).reshape(n_bias + n_gain, width)
     bias, gain = vectors[:n_bias], vectors[n_bias:]
@@ -2360,16 +2372,17 @@
     hits = index[None, :] == order[:, None]
     member = jnp.any(hits, axis=1).astype(F32)
     slot = jnp.sum(jnp.where(hits, jnp.arange(index.shape[0], dtype=jnp.int32)[None], 0), axis=1)
-    (ca, cross_lse), halves = cross_forward(
+    (ca, cross_lse, grad_own), halves = cross_forward(
         n_mem,
         plane,
         index,
         cq,
         ck,
         cv,
-        [(ffn_in[None], True), (ffn_out, False), (cross_out, False)],
-    )
-    w_ffn_in, w_ffn_out, w_cross_out = flat(halves[0])[0], halves[1], flat(halves[2])[0]
+        cotangent,
+        [(ffn_in[None], True), (ffn_out, False)],
+    )
+    w_ffn_in, w_ffn_out = flat(halves[0])[0], halves[1]
 
     rows_of = jnp.stack(
         [gain[0], bias[6], bias[5], gain[1], bias[7], bias[9], gain[2], bias[8]]
@@ -2377,7 +2390,7 @@
     layer_out, dca, dz2, feed_sums, hidden_sums, own_ffn_out, dw_ffn_in, dw_cross_out = feed(
         n_mem,
         plane,
-        cotangent,
+        grad_own,
         rows_of,
         half_of(ffn_bias)[None],
         ca,

time: 550 us -> 561 us (1.020)
  Pallas kernels: 531 us -> 542 us
    pallas_call x1, Pallas kernels: 60.8 us -> 67.4 us  [cross_forward(): pl.pallas_call(functools.partial(cross_forward_kernel, n_mem, plane, kind...]
where the time goes in v2:
time: 561 us; the launch traced here: 552 us
  Pallas kernels  542 us (97%)
    pallas_call x1, Pallas kernels, front(): pl.pallas_call(functools.partial(front_kernel, n_mem, plane, kinds, place...  121 us
    pallas_call x1, Pallas kernels, last(): pl.pallas_call(functools.partial(last_kernel, n_mem, plane, planes, settl...  92.1 us
    pallas_call x1, Pallas kernels, cross_backward(): pl.pallas_call(functools.partial(cross_backward_kernel, n_mem, plane, pla...  89 us
    pallas_call x1, Pallas kernels, feed(): pl.pallas_call(functools.partial(feed_kernel, n_mem, plane), in_specs=[VM...  86.7 us
    pallas_call x1, Pallas kernels, middle(): pl.pallas_call(functools.partial(middle_kernel, n_mem, plane, planes, set...  73.2 us
    pallas_call x1, Pallas kernels, cross_forward(): pl.pallas_call(functools.partial(cross_forward_kernel, n_mem, plane, kind...  67.4 us
    pallas_call x1, Pallas kernels, widen(): pl.pallas_call(widen_kernel, grid=(steps,), in_specs=blocks, out_specs=bl...  12.5 us

profile of v2, /device:TPU:0, one launch (start us, length us, event | category | flops | bytes accessed | tf_op | source)
XLA Modules:
  0.0 552.3 jit_solution(6585951186982581684)
XLA Ops:
  0.6 0.7 reshape.133
  1.3 1.3 fusion.4.small_ref
  2.7 121.4 %front.1 = (bf16[1024,1024]{1,0:T(8,128)(2,1)}, bf16[4,3,256,1024]{3,2,1,0:T(8,128)(2,1)}, s32[1,8]{1,0:T(1,128)}, bf16[4,32,256]{2,1,0:T(8,128)(2,1)}, bf16[3,4...) custom-call(bf16[2,256,1024]{2,1,0:T(8,128)(2,1)} %x_ref.1, ...), custom_call_target="tpu_custom_call" | custom-call | flops 5368709120 | bytes 41943040 | tf_op jit(solution)/shard_map/front/pallas_call | solution.py:781
  124.1 0.9 convert_element_type.8
  125.0 0.0 copy-start.2
  125.0 0.7 stack.3.rows_ref
  125.6 0.8 slice.114
  126.5 0.6 copy.31
  127.1 67.4 %cross_forward.1 = (bf16[1024,512]{1,0:T(8,128)(2,1)}, f32[4,2,1024]{2,1,0:T(2,128)}, bf16[512,1024]{1,0:T(8,128)(2,1)}, bf16[1,4,4,64,2048]{4,3,2,1,0:T(8,128)(2,1)}, bf16[1,4,4,128,1024]{4,3,2,1,0:T(8,128)(2,1)}) custom-call(s32[8]{0:T(128)} %bitcast.83, bf16[1024,512]{1,0:T(8,128)(2,1)} %get-tuple-element.70.q_ref, ...), custom_call_target="tpu_custom_call" | custom-call | flops 17179869184 | bytes 8388608 | tf_op jit(solution)/shard_map/cross_forward/pallas_call | solution.py:2062
  194.5 0.0 copy-done.2
  194.5 86.7 %feed.1 = (bf16[2,256,1024]{2,1,0:T(8,128)(2,1)}, bf16[1024,512]{1,0:T(8,128)(2,1)}, f32[512,1024]{1,0:T(8,128)}, f32[8,1024]{1,0:T(8,128)}, f32[1,2048]{1,0:T(1...) custom-call(bf16[512,1024]{1,0:T(8,128)(2,1)} %get-tuple-element.73., ...), custom_call_target="tpu_custom_call" | custom-call | flops 25769803776 | bytes 41943040 | tf_op jit(solution)/shard_map/feed/pallas_call | solution.py:1300
  281.2 0.0 copy-start.3
  281.2 89.0 %cross_backward.1 = (bf16[1024,512]{1,0:T(8,128)(2,1)}, bf16[2048,512]{1,0:T(8,128)(2,1)}, bf16[2048,512]{1,0:T(8,128)(2,1)}, bf16[1,4,64,4096]{3,2,1,0:T(8,128)...) custom-call(s32[8]{0:T(128)} %bitcast.84, bf16[1024,512]{1,0:T(8,128)(2,1)} %get-tuple-element.70.q_ref, ...), custom_call_target="tpu_custom_call" | custom-call | flops 42949672960 | bytes 17825792 | tf_op jit(solution)/shard_map/cross_backward/pallas_call | solution.py:2234
  370.3 0.0 copy-done.3
  370.3 0.1 fusion.6
  370.4 0.5 convert_element_type.9.member_ref
  370.9 0.6 select_reduce_fusion.slot_ref
  371.5 73.2 %middle.1 = (bf16[1024,512]{1,0:T(8,128)(2,1)}, f32[512,1024]{1,0:T(8,128)}, f32[8,1024]{1,0:T(8,128)}, bf16[3,256,1024]{2,1,0:T(8,128)(2,1)}, bf16[3,4,64,512]{...) custom-call(s32[12]{0:T(128)} %select_reduce_fusion.slot_ref, f32[12]{0:T(128)} %convert_element_type.9.member_ref, ...), custom_call_target="tpu_custom_call" | custom-call | flops 16106127360 | bytes 41943040 | tf_op jit(solution)/shard_map/middle/pallas_call | solution.py:1549
  444.7 92.1 %last.1 = (f32[32,256]{1,0:T(8,128)}, bf16[2,256,1024]{2,1,0:T(8,128)(2,1)}, bf16[3,4,64,1024]{3,2,1,0:T(8,128)(2,1)}, bf16[2,4,32,1024]{3,2,1,0:T(8,128)(2,1)}, bf16[3,4,64,1024]{3,2,1,0:T(8,128)(2,1)}) custom-call(bf16[1024,512]{1,0:T(8,128)(2,1)} %get-tuple-element.81.refs_0_, bf16[1024,512]{1,0:T(8,128)(2,1)} %get-tuple-element.82.refs_1_, ...), custom_call_target="tpu_custom_call" | custom-call | flops 42949672960 | bytes 41943040 | tf_op jit(solution)/shard_map/last/pallas_call | solution.py:1939
  536.8 0.0 copy-start.1
  536.8 0.0 copy-start
  536.8 12.5 %widen.1 = (f32[512,1024]{1,0:T(8,128)}, f32[768,1024]{1,0:T(8,128)}, f32[768,1024]{1,0:T(8,128)}, f32[256,1024]{1,0:T(8,128)}, f32[768,1024]{1,0:T(8,128)}, /*i...) custom-call(bf16[512,1024]{1,0:T(8,128)(2,1)} %bitcast.50, bf16[768,1024]{1,0:T(8,128)(2,1)} %bitcast.47, ...), custom_call_target="tpu_custom_call" | custom-call | bytes 33030144 | tf_op jit(solution)/shard_map/widen/pallas_call | solution.py:2297
  549.3 0.0 copy-done.1
  549.3 0.6 slice.103
  549.9 0.6 copy.32
  550.5 0.6 slice.104
  551.1 0.0 copy-done
  551.1 1.0 copy.38
  (6 shorter events, 0.1 us)
Async XLA Ops:
  125.0 69.5 %copy-start.2 = (f32[1,4,256]{2,0,1:T(1,128)}, f32[1,4,256]{2,0,1:T(1,128)S(1)}, u32[]{:S(2)}) copy-start(f32[1,4,256]{2,0,1:T(1,128)S(1)} %get-tuple-element.133) | copy-start | bytes 12292
  281.2 89.1 %copy-start.3 = (s32[1,8]{1,0:T(1,128)S(1)}, s32[1,8]{1,0:T(1,128)}, u32[]{:S(2)}) copy-start(s32[1,8]{1,0:T(1,128)} %get-tuple-element.69) | copy-start | bytes 100
  536.8 12.5 %copy-start.1 = (f32[32,256]{1,0:T(8,128)S(1)}, f32[32,256]{1,0:T(8,128)}, u32[]{:S(2)}) copy-start(f32[32,256]{1,0:T(8,128)} %get-tuple-element.125) | copy-start | bytes 98308
  536.8 14.3 %copy-start = (bf16[2,256,1024]{2,1,0:T(8,128)(2,1)S(1)}, bf16[2,256,1024]{2,1,0:T(8,128)(2,1)}, u32[]{:S(2)}) copy-start(bf16[2,256,1024]{2,1,0:T(8,128)(2,1)} %get-tuple-element.148) | copy-start | bytes 3145732

commit v3 on v1

--- a/solution.py
+++ b/solution.py
@@ -319,14 +319,16 @@
 
 
 class Gather:
-    def __init__(self, place, sems, shard, full, columns, n_mem, in_plane=True):
+    def __init__(self, place, sems, shard, full, columns, n_mem, in_plane=None):
         mem, quarter = place.mem, place.quarter
         self.n_mem = n_mem
-        self.in_plane = in_plane
+        self.in_plane = tuple(range(1, n_mem)) if in_plane is None else in_plane
         self.own = Own(place, sems, shard, full, columns, n_mem)
         self.chain = Chain(place, sems, lambda i: full.at[:, i, quarter], n_mem)
         self.shares = {}
-        for d in range(1, n_mem if in_plane else 1):
+        for d in range(1, n_mem):
+            if d not in self.in_plane and n_mem - d not in self.in_plane:
+                continue
             source = lax.rem(mem + jnp.int32(n_mem - d), jnp.int32(n_mem))
 
             def block(t, source=source):
@@ -339,7 +341,9 @@
         self.chain.start()
 
     def share(self, hops):
-        self.chain.relay(hops, lambda d: self.shares[d].start() if self.in_plane else None)
+        self.chain.relay(
+            hops, lambda d: self.shares[d].start() if hops in self.in_plane else None
+        )
 
     def forward(self, hops):
         for way, d in ((1, hops), (-1, self.n_mem - hops)):
@@ -350,8 +354,12 @@
 
     def finish(self):
         self.chain.wait_send()
-        for share in self.shares.values():
-            share.wait()
+        for hops in self.in_plane:
+            for way, d in ((1, hops), (-1, self.n_mem - hops)):
+
+                @pl.when(self.chain.comes(way, hops))
+                def _():
+                    self.shares[d].wait()
 
 
 GATHER_SEMS = 44
@@ -1044,32 +1052,52 @@
     refs = Walk(refs)
     fetched = refs.take(4)
     out_part = refs.one()
-    final_out, dca_ref, dz2_ref, sums_ref, bias_sum, own_out, dw_in, dw_co = refs.take(8)
+    final_out, dca_ref, dz2_ref, sums_ref, bias_sum, own_out, dw_in, dw_co, dw_out = refs.take(9)
     kept = refs.take(4)
     out_w = refs.one()
     cot_vm, h2_vm, unit_vm, scale_vm, act_vm, slope_vm, p_vm, part_vm, twin_vm = refs.take(9)
-    final_vm, df_vm, dco_vm, dw_out = refs.take(4)
+    final_vm, df_vm, dco_vm = refs.take(3)
     bufs = refs.take(3)
     sems = Sems(refs.one())
     place = Place(plane)
     ca, unit1, w_co, w_in = [Fetch(sems, src, dst) for src, dst in zip(fetched, kept)]
     mem, quarter = place.mem, place.quarter
-    pieces = [Fetch(sems, out_part.at[0, mem], out_w.at[0, mem])]
-    shares = []
+    own_piece = Fetch(sems, out_part.at[0, mem], out_w.at[0, mem])
+    pieces = []
     for d in range(1, n_mem):
         source = lax.rem(mem + jnp.int32(n_mem - d), jnp.int32(n_mem))
 
         def place_of(t, source=source):
             return out_w.at[:, source, flip(quarter, t)]
 
-        pieces.append(Fetch(sems, out_part.at[:, source, quarter], place_of(0)))
-        shares.append(Share(place, sems, place_of(0), place_of))
+        (sem,) = sems.take(1)
+        pieces.append(
+            (
+                mem < d if d == 1 else mem >= (d if d == n_mem - 1 else 0),
+                pltpu.make_async_copy(out_part.at[0, source], out_w.at[0, source], sem),
+                pltpu.make_async_copy(out_part.at[:, source, quarter], place_of(0), sem),
+                Share(place, sems, place_of(0), place_of),
+            )
+        )
+
+    def each_piece(whole_step, part_step):
+        for part, whole_copy, part_copy, share in pieces:
+            if whole_step is not None:
+
+                @pl.when(jnp.logical_not(part))
+                def _():
+                    whole_step(whole_copy)
+
+            @pl.when(part)
+            def _():
+                part_step(part_copy, share)
+
     rows = h2_vm.shape[0]
     own = rows // 2
     seg = own // 2
     hidden = act_vm.shape[1]
     block = hidden // n_mem
-    out_sum = PlaneSum(place, sems, dw_out, own_out, bufs, (0, dw_out.shape[3]))
+    out_sum = PlaneSum(place, sems, dw_out, own_out, bufs, (0, own_out.shape[2]))
     spread_cot = Spread(
         place,
         sems,
@@ -1098,14 +1126,19 @@
     swap_dh2 = [swap(half_lanes(part_vm, i), half_lanes(twin_vm, i)) for i in range(2)]
     swap_dco = swap(dco_vm.at[pl.ds(0, own)], dco_vm.at[pl.ds(own, own)])
 
-    for item in [ca, w_co] + pieces + [unit1, w_in]:
+    for item in (ca, w_co, own_piece):
+        item.start()
+    each_piece(lambda copy: copy.start(), lambda copy, share: copy.start())
+    for item in (unit1, w_in):
         item.start()
     place.meet(column_peers(n_mem) + plane_peers(plane))
     spread_cot.start()
-    for item in pieces:
-        item.get()
-    for share in shares:
+
+    def share_start(copy, share):
+        copy.wait()
         share.start()
+
+    each_piece(None, share_start)
     row = {name: rows_ref[i : i + 1, :] for i, name in enumerate(("g0", "b6", "b5", "g1", "b7", "b9", "g2", "b8"))}
     sums_ref[...] = jnp.zeros_like(sums_ref)
     bias_sum[...] = jnp.zeros_like(bias_sum)
@@ -1154,13 +1187,12 @@
     ours, others = pl.ds(0, own), pl.ds(own, own)
     width = h2_vm.shape[1]
     column = width // 2
+    each_piece(None, lambda copy, share: share.forward())
     forward(ours)
-    for share in shares:
-        share.forward()
     swap_h2.wait()
     forward(others)
-    for share in shares:
-        share.wait()
+    own_piece.get()
+    each_piece(lambda copy: copy.wait(), lambda copy, share: share.wait())
     for i in range(2):
         lanes = slice(i * column, (i + 1) * column)
         weights = out_w[0, :, :, :, lanes].reshape(hidden, column)
@@ -1281,9 +1313,10 @@
         jax.ShapeDtypeStruct((own, width), F32),
         jax.ShapeDtypeStruct((8, width), F32),
         jax.ShapeDtypeStruct((1, hidden), F32),
-        sum_shape(out_shape),
+        jax.ShapeDtypeStruct((1, n_mem, out_shape[3] // 2, width), BF16),
         jax.ShapeDtypeStruct(in_shape, BF16),
         jax.ShapeDtypeStruct(grad_shape(part, width), BF16),
+        jax.ShapeDtypeStruct(out_shape, BF16),
     ]
     fetched = [ca, unit1, w_co, w_in, w_out]
     scratch = [pltpu.VMEM(item.shape, item.dtype) for item in fetched] + [
@@ -1299,9 +1332,8 @@
         pltpu.VMEM((own, width), BF16),
         pltpu.VMEM((rows, width), BF16),
         pltpu.VMEM((rows, width), BF16),
-        pltpu.VMEM(out_shape, BF16),
     ]
-    scratch += plane_sum_scratch(out_shape, n_mem, out_shape[3])
+    scratch += plane_sum_scratch(out_shape, n_mem, out_shape[3] // 2)
     scratch += [pltpu.SemaphoreType.DMA((PLANE_SUM_SEMS + 60,))]
     return pl.pallas_call(
         functools.partial(feed_kernel, n_mem, plane),
@@ -1971,7 +2003,7 @@
     step = pl.program_id(0) * pl.num_programs(1) + pl.program_id(1)
     last = pl.num_programs(0) * pl.num_programs(1) - 1
     gathers = [
-        Gather(place, sems, shard, half, columns, n_mem, i != 1)
+        Gather(place, sems, shard, half, columns, n_mem, (1,) if i == 1 else None)
         for i, (shard, half, columns) in enumerate(zip(shards, halves, kinds))
     ]
     @pl.when(step == 0)
@@ -2016,15 +2048,16 @@
         o_t[head * HD : (head + 1) * HD, span] = mixed
         lse_ref[0, head : head + 1, span] = lse
 
-    whole_one, line_one, small_one = gathers
+    whole_one, line_one = gathers
     plan = {
-        4: [(whole_one.share, 1), (small_one.share, 1)],
+        4: [(whole_one.share, 1)],
         6: [(line_one.share, 1)],
-        10: [(whole_one.share, 2), (small_one.share, 2)],
-        12: [(line_one.share, 2), (whole_one.forward, 1), (small_one.forward, 1)],
-        17: [(whole_one.share, 3), (small_one.share, 3)],
-        19: [(line_one.share, 3), (whole_one.forward, 2), (small_one.forward, 2)],
-        24: [(whole_one.forward, 3), (small_one.forward, 3)],
+        10: [(whole_one.share, 2)],
+        12: [(line_one.share, 2), (whole_one.forward, 1)],
+        14: [(line_one.forward, 1)],
+        17: [(whole_one.share, 3)],
+        19: [(line_one.share, 3), (whole_one.forward, 2)],
+        24: [(whole_one.forward, 3)],
     }
 
     def serve(n):
@@ -2093,7 +2126,6 @@
     ready = refs.take(len(settled))
     dq_ref, dk_ref, dv_ref = refs.take(3)
     outs = refs.take(len(kinds))
-    ready_outs = refs.take(len(settled))
     q_h, do_h, dq_t, p_vm, ds_vm = refs.take(5)
     sems = Sems(refs.refs[-1])
     place = Place(plane, planes)
@@ -2106,9 +2138,9 @@
         )
     first = [
         Settle(
-            place, sems, ready[i], ready_outs[i], refs.take(3), columns, n_mem, (0, ready[i].shape[2])
-        )
-        for i, columns in enumerate(settled)
+            place, sems, ready[i], outs[which], refs.take(3), columns, n_mem, (0, ready[i].shape[2])
+        )
+        for i, (which, columns) in enumerate(settled)
     ]
     passage = pl.program_id(1)
     step = pl.program_id(0) * pl.num_programs(1) + passage
@@ -2130,12 +2162,14 @@
             for call in calls:
                 call()
 
+    plan = ((0, 2, 4, 7, 8), (2, 4, 6, 9, 10), (5, 7, 9, 12, 13), (8, 10, 11, 13, 14))
     for i, (plane_sum, settle) in enumerate(zip(sums, settles)):
-        at(3 * i, plane_sum.start)
-        at(3 * i + 2, plane_sum.middle)
-        at(3 * i + 4, plane_sum.end, settle.start)
-        at(3 * i + 7, settle.middle)
-        at(3 * i + 8, settle.forward)
+        start, middle, end, line, near = plan[i]
+        at(start, plane_sum.start)
+        at(middle, plane_sum.middle)
+        at(end, plane_sum.end, settle.start)
+        at(line, settle.middle)
+        at(near, settle.forward)
     for item in first:
         at(6, item.middle)
         at(7, item.forward)
@@ -2205,19 +2239,18 @@
     memory = pl.BlockSpec(k.shape[:2] + (2 * HD,), lambda h, u: (0, 0, h))
     grads_of = pl.BlockSpec((block, 2 * HD), lambda h, u: (u, h))
     shapes, chunks, scratch = [], [], []
-    for which, (grad, columns, pieces) in enumerate(grads):
+    for which, (grad, columns, pieces, begin) in enumerate(grads):
         lead, _, _, depth, cols = grad.shape
         count = depth // pieces
         shapes.append(reduce_out(grad.shape, columns, plane))
-        for i in range(pieces):
+        for i in range(begin, pieces):
             chunks.append((which, columns, (i * count, count)))
             scratch.append(pltpu.VMEM((lead, n_mem, count, cols), BF16))
             scratch += plane_sum_scratch(grad.shape, n_mem, count)
             scratch += settle_scratch(grad.shape, n_mem, plane, planes, count)
-    settled = tuple(columns for _, columns in ready)
-    for item, columns in ready:
+    settled = tuple((which, grads[which][1]) for _, which in ready)
+    for item, _ in ready:
         shape = item.shape[:2] + (plane,) + item.shape[2:]
-        shapes.append(reduce_out(shape, columns, plane))
         scratch += settle_scratch(shape, n_mem, plane, planes, shape[3])
     outs = pl.pallas_call(
         functools.partial(cross_backward_kernel, n_mem, plane, planes, tuple(chunks), settled),
@@ -2335,7 +2368,7 @@
         enc_local,
         passage_map,
         small,
-        [(self_qkv, True), (self_out, False), (cross_qkv, True)],
+        [(self_qkv, True), (self_out, False), (cross_qkv, True), (cross_out, False)],
     )
     x_full, enc_full, index, small = rows_out
     sq, sk, sv, sa, self_lse, h1_full, unit1, scale1, cq, ck, cv = kept
@@ -2346,7 +2379,7 @@
         return half.reshape(lead, -1, cols)
 
     w_self, w_cross = flat(halves[0]), flat(halves[2])
-    w_self_out = flat(halves[1])[0]
+    w_self_out, w_cross_out = flat(halves[1])[0], flat(halves[3])[0]
     small = small.astype(F32)
     vectors = small[:, : n_bias + n_gain].transpose(1, 0, 2).reshape(n_bias + n_gain, width)
     bias, gain = vectors[:n_bias], vectors[n_bias:]
@@ -2367,14 +2400,14 @@
         cq,
         ck,
         cv,
-        [(ffn_in[None], True), (ffn_out, False), (cross_out, False)],
-    )
-    w_ffn_in, w_ffn_out, w_cross_out = flat(halves[0])[0], halves[1], flat(halves[2])[0]
+        [(ffn_in[None], True), (ffn_out, False)],
+    )
+    w_ffn_in, w_ffn_out = flat(halves[0])[0], halves[1]
 
     rows_of = jnp.stack(
         [gain[0], bias[6], bias[5], gain[1], bias[7], bias[9], gain[2], bias[8]]
     )
-    layer_out, dca, dz2, feed_sums, hidden_sums, own_ffn_out, dw_ffn_in, dw_cross_out = feed(
+    layer_out, dca, dz2, feed_sums, hidden_sums, own_ffn_out, dw_ffn_in, dw_cross_out, dw_ffn_out = feed(
         n_mem,
         plane,
         cotangent,
@@ -2397,8 +2430,8 @@
         ca,
         dca,
         cross_lse,
-        [(dw_ffn_in, True, 2), (dw_cross_out, False, 1)],
-        [(own_ffn_out, False)],
+        [(dw_ffn_out, False, 2, 1), (dw_ffn_in, True, 2, 0), (dw_cross_out, False, 1, 0)],
+        [(own_ffn_out, 0)],
     )
     (dsa, dz1, middle_sums, enc_sum), (own_cross, own_so), _ = middle(
         n_mem,
@@ -2455,9 +2488,9 @@
             (sums[0], self_qkv),
             (sums[1], self_out),
             (sums[2], cross_qkv),
-            (ffn_sums[1], cross_out),
-            (ffn_sums[0], ffn_in),
-            (ffn_sums[2], ffn_out),
+            (ffn_sums[2], cross_out),
+            (ffn_sums[1], ffn_in),
+            (ffn_sums[0], ffn_out),
         ]
     )
     out_ffn_bias = vec[n_bias + n_gain : n_small].reshape(-1)

time: 550 us -> 553 us (level)
    pallas_call x1, Pallas kernels: 89.7 us -> 107 us  [cross_backward(): pl.pallas_call(functools.partial(cross_backward_kernel, n_mem, plane, pla...]
    pallas_call x1, Pallas kernels: 86.5 us -> 72.9 us  [feed(): pl.pallas_call(functools.partial(feed_kernel, n_mem, plane), in_specs=[VM...]
where the time goes in v3:
time: 553 us; the launch traced here: 544 us
  Pallas kernels  534 us (97%)
  local copies, waits for them, and re-layouts  5.6 us (1%)
    pallas_call x1, Pallas kernels, front(): pl.pallas_call(functools.partial(front_kernel, n_mem, plane, kinds, place...  121 us
    pallas_call x1, Pallas kernels, cross_backward(): pl.pallas_call(functools.partial(cross_backward_kernel, n_mem, plane, pla...  107 us
    pallas_call x1, Pallas kernels, last(): pl.pallas_call(functools.partial(last_kernel, n_mem, plane, planes, settl...  92.4 us
    pallas_call x1, Pallas kernels, feed(): pl.pallas_call(functools.partial(feed_kernel, n_mem, plane), in_specs=[VM...  72.9 us
    pallas_call x1, Pallas kernels, middle(): pl.pallas_call(functools.partial(middle_kernel, n_mem, plane, planes, set...  71.6 us
    pallas_call x1, Pallas kernels, cross_forward(): pl.pallas_call(functools.partial(cross_forward_kernel, n_mem, plane, kind...  56.2 us
    pallas_call x1, Pallas kernels, widen(): pl.pallas_call(widen_kernel, grid=(steps,), in_specs=blocks, out_specs=bl...  12.5 us

profile of v3, /device:TPU:0, one launch (start us, length us, event | category | flops | bytes accessed | tf_op | source)
XLA Modules:
  0.0 543.9 jit_solution(2793428969756113884)
XLA Ops:
  0.6 0.7 reshape.133
  1.3 1.3 fusion.4.small_ref
  2.7 121.4 %front.1 = (bf16[1024,1024]{1,0:T(8,128)(2,1)}, bf16[4,3,256,1024]{3,2,1,0:T(8,128)(2,1)}, s32[1,8]{1,0:T(1,128)}, bf16[4,32,256]{2,1,0:T(8,128)(2,1)}, bf16[3,4...) custom-call(bf16[2,256,1024]{2,1,0:T(8,128)(2,1)} %x_ref.1, ...), custom_call_target="tpu_custom_call" | custom-call | flops 5368709120 | bytes 41943040 | tf_op jit(solution)/shard_map/front/pallas_call | solution.py:784
  124.1 0.9 convert_element_type.8
  125.0 0.0 copy-start.2
  125.0 0.7 stack.3.rows_ref
  125.6 0.8 slice.114
  126.5 0.6 copy.31
  127.1 56.2 %cross_forward.1 = (bf16[1024,512]{1,0:T(8,128)(2,1)}, f32[4,2,1024]{2,1,0:T(2,128)}, bf16[1,4,4,64,2048]{4,3,2,1,0:T(8,128)(2,1)}, bf16[1,4,4,128,1024]{4,3,2,1,0:T(8,128)(2,1)}) custom-call(s32[8]{0:T(128)} %bitcast.83, bf16[1024,512]{1,0:T(8,128)(2,1)} %get-tuple-element.71.q_ref, bf16[12,256,512]{2,1,0:T(8,128)(2,1)} %get-tuple-element.72.k_ref, ...), custom_call_target="tpu_custom_call" | custom-call | flops 17179869184 | bytes 8388608 | tf_op jit(solution)/shard_map/cross_forward/pallas_call | solution.py:2090
  183.3 0.0 copy-done.2
  183.3 72.9 %feed.1 = (bf16[2,256,1024]{2,1,0:T(8,128)(2,1)}, bf16[1024,512]{1,0:T(8,128)(2,1)}, f32[512,1024]{1,0:T(8,128)}, f32[8,1024]{1,0:T(8,128)}, f32[1,2048]{1,0:T(1...) custom-call(bf16[2,256,1024]{2,1,0:T(8,128)(2,1)} %cot_ref.1, ...), custom_call_target="tpu_custom_call" | custom-call | flops 25769803776 | bytes 41943040 | tf_op jit(solution)/shard_map/feed/pallas_call | solution.py:1338
  256.2 0.0 copy-start.3
  256.2 106.7 %cross_backward.1 = (bf16[1024,512]{1,0:T(8,128)(2,1)}, bf16[2048,512]{1,0:T(8,128)(2,1)}, bf16[2048,512]{1,0:T(8,128)(2,1)}, bf16[2,4,128,1024]{3,2,1,0:T(8,128...) custom-call(s32[8]{0:T(128)} %bitcast.84, bf16[1024,512]{1,0:T(8,128)(2,1)} %get-tuple-element.71.q_ref, ...), custom_call_target="tpu_custom_call" | custom-call | flops 42949672960 | bytes 17825792 | tf_op jit(solution)/shard_map/cross_backward/pallas_call | solution.py:2255
  362.9 0.0 copy-done.3
  362.9 0.1 fusion.6
  363.0 0.5 convert_element_type.9.member_ref
  363.5 0.6 select_reduce_fusion.slot_ref
  364.1 71.6 %middle.1 = (bf16[1024,512]{1,0:T(8,128)(2,1)}, f32[512,1024]{1,0:T(8,128)}, f32[8,1024]{1,0:T(8,128)}, bf16[3,256,1024]{2,1,0:T(8,128)(2,1)}, bf16[3,4,64,512]{...) custom-call(s32[12]{0:T(128)} %select_reduce_fusion.slot_ref, f32[12]{0:T(128)} %convert_element_type.9.member_ref, ...), custom_call_target="tpu_custom_call" | custom-call | flops 16106127360 | bytes 41943040 | tf_op jit(solution)/shard_map/middle/pallas_call | solution.py:1587
  435.8 92.4 %last.1 = (f32[32,256]{1,0:T(8,128)}, bf16[2,256,1024]{2,1,0:T(8,128)(2,1)}, bf16[3,4,64,1024]{3,2,1,0:T(8,128)(2,1)}, bf16[2,4,32,1024]{3,2,1,0:T(8,128)(2,1)}, bf16[3,4,64,1024]{3,2,1,0:T(8,128)(2,1)}) custom-call(bf16[1024,512]{1,0:T(8,128)(2,1)} %get-tuple-element.80.refs_0_, bf16[1024,512]{1,0:T(8,128)(2,1)} %get-tuple-element.81.refs_1_, ...), custom_call_target="tpu_custom_call" | custom-call | flops 42949672960 | bytes 41943040 | tf_op jit(solution)/shard_map/last/pallas_call | solution.py:1977
  528.1 0.0 copy-start.1
  528.1 0.0 copy-start
  528.2 12.5 %widen.1 = (f32[512,1024]{1,0:T(8,128)}, f32[768,1024]{1,0:T(8,128)}, f32[768,1024]{1,0:T(8,128)}, f32[256,1024]{1,0:T(8,128)}, f32[768,1024]{1,0:T(8,128)}, /*i...) custom-call(bf16[512,1024]{1,0:T(8,128)(2,1)} %bitcast.50, bf16[768,1024]{1,0:T(8,128)(2,1)} %bitcast.47, ...), custom_call_target="tpu_custom_call" | custom-call | bytes 33030144 | tf_op jit(solution)/shard_map/widen/pallas_call | solution.py:2318
  540.7 0.0 copy-done.1
  540.7 0.6 slice.103
  541.3 0.6 copy.32
  541.9 0.6 slice.104
  542.5 0.0 copy-done
  542.5 1.0 copy.38
  (6 shorter events, 0.1 us)
Async XLA Ops:
  125.0 58.3 %copy-start.2 = (f32[1,4,256]{2,0,1:T(1,128)}, f32[1,4,256]{2,0,1:T(1,128)S(1)}, u32[]{:S(2)}) copy-start(f32[1,4,256]{2,0,1:T(1,128)S(1)} %get-tuple-element.133) | copy-start | bytes 12292
  256.2 106.7 %copy-start.3 = (s32[1,8]{1,0:T(1,128)S(1)}, s32[1,8]{1,0:T(1,128)}, u32[]{:S(2)}) copy-start(s32[1,8]{1,0:T(1,128)} %get-tuple-element.70) | copy-start | bytes 100
  528.1 12.5 %copy-start.1 = (f32[32,256]{1,0:T(8,128)S(1)}, f32[32,256]{1,0:T(8,128)}, u32[]{:S(2)}) copy-start(f32[32,256]{1,0:T(8,128)} %get-tuple-element.125) | copy-start | bytes 98308
  528.1 14.3 %copy-start = (bf16[2,256,1024]{2,1,0:T(8,128)(2,1)S(1)}, bf16[2,256,1024]{2,1,0:T(8,128)(2,1)}, u32[]{:S(2)}) copy-start(bf16[2,256,1024]{2,1,0:T(8,128)(2,1)} %get-tuple-element.148) | copy-start | bytes 3145732

commit v4 on v3

--- a/solution.py
+++ b/solution.py
@@ -1052,11 +1052,11 @@
     refs = Walk(refs)
     fetched = refs.take(4)
     out_part = refs.one()
-    final_out, dca_ref, dz2_ref, sums_ref, bias_sum, own_out, dw_in, dw_co, dw_out = refs.take(9)
+    final_out, dca_ref, dz2_ref, sums_ref, bias_sum, own_out, dw_in, dw_co = refs.take(8)
     kept = refs.take(4)
     out_w = refs.one()
     cot_vm, h2_vm, unit_vm, scale_vm, act_vm, slope_vm, p_vm, part_vm, twin_vm = refs.take(9)
-    final_vm, df_vm, dco_vm = refs.take(3)
+    final_vm, df_vm, dco_vm, dw_out = refs.take(4)
     bufs = refs.take(3)
     sems = Sems(refs.one())
     place = Place(plane)
@@ -1313,10 +1313,9 @@
         jax.ShapeDtypeStruct((own, width), F32),
         jax.ShapeDtypeStruct((8, width), F32),
         jax.ShapeDtypeStruct((1, hidden), F32),
-        jax.ShapeDtypeStruct((1, n_mem, out_shape[3] // 2, width), BF16),
+        sum_shape(out_shape),
         jax.ShapeDtypeStruct(in_shape, BF16),
         jax.ShapeDtypeStruct(grad_shape(part, width), BF16),
-        jax.ShapeDtypeStruct(out_shape, BF16),
     ]
     fetched = [ca, unit1, w_co, w_in, w_out]
     scratch = [pltpu.VMEM(item.shape, item.dtype) for item in fetched] + [
@@ -1332,8 +1331,9 @@
         pltpu.VMEM((own, width), BF16),
         pltpu.VMEM((rows, width), BF16),
         pltpu.VMEM((rows, width), BF16),
+        pltpu.VMEM(out_shape, BF16),
     ]
-    scratch += plane_sum_scratch(out_shape, n_mem, out_shape[3] // 2)
+    scratch += plane_sum_scratch(out_shape, n_mem, out_shape[3])
     scratch += [pltpu.SemaphoreType.DMA((PLANE_SUM_SEMS + 60,))]
     return pl.pallas_call(
         functools.partial(feed_kernel, n_mem, plane),
@@ -2126,6 +2126,7 @@
     ready = refs.take(len(settled))
     dq_ref, dk_ref, dv_ref = refs.take(3)
     outs = refs.take(len(kinds))
+    ready_outs = refs.take(len(settled))
     q_h, do_h, dq_t, p_vm, ds_vm = refs.take(5)
     sems = Sems(refs.refs[-1])
     place = Place(plane, planes)
@@ -2138,9 +2139,9 @@
         )
     first = [
         Settle(
-            place, sems, ready[i], outs[which], refs.take(3), columns, n_mem, (0, ready[i].shape[2])
-        )
-        for i, (which, columns) in enumerate(settled)
+            place, sems, ready[i], ready_outs[i], refs.take(3), columns, n_mem, (0, ready[i].shape[2])
+        )
+        for i, columns in enumerate(settled)
     ]
     passage = pl.program_id(1)
     step = pl.program_id(0) * pl.num_programs(1) + passage
@@ -2162,7 +2163,7 @@
             for call in calls:
                 call()
 
-    plan = ((0, 2, 4, 7, 8), (2, 4, 6, 9, 10), (5, 7, 9, 12, 13), (8, 10, 11, 13, 14))
+    plan = ((0, 2, 5, 9, 10), (4, 6, 9, 13, 14), (8, 9, 11, 14, 15))
     for i, (plane_sum, settle) in enumerate(zip(sums, settles)):
         start, middle, end, line, near = plan[i]
         at(start, plane_sum.start)
@@ -2171,8 +2172,8 @@
         at(line, settle.middle)
         at(near, settle.forward)
     for item in first:
-        at(6, item.middle)
-        at(7, item.forward)
+        at(7, item.middle)
+        at(9, item.forward)
 
     @pl.when(passage == 0)
     def _():
@@ -2239,18 +2240,19 @@
     memory = pl.BlockSpec(k.shape[:2] + (2 * HD,), lambda h, u: (0, 0, h))
     grads_of = pl.BlockSpec((block, 2 * HD), lambda h, u: (u, h))
     shapes, chunks, scratch = [], [], []
-    for which, (grad, columns, pieces, begin) in enumerate(grads):
+    for which, (grad, columns, pieces) in enumerate(grads):
         lead, _, _, depth, cols = grad.shape
         count = depth // pieces
         shapes.append(reduce_out(grad.shape, columns, plane))
-        for i in range(begin, pieces):
+        for i in range(pieces):
             chunks.append((which, columns, (i * count, count)))
             scratch.append(pltpu.VMEM((lead, n_mem, count, cols), BF16))
             scratch += plane_sum_scratch(grad.shape, n_mem, count)
             scratch += settle_scratch(grad.shape, n_mem, plane, planes, count)
-    settled = tuple((which, grads[which][1]) for _, which in ready)
-    for item, _ in ready:
+    settled = tuple(columns for _, columns in ready)
+    for item, columns in ready:
         shape = item.shape[:2] + (plane,) + item.shape[2:]
+        shapes.append(reduce_out(shape, columns, plane))
         scratch += settle_scratch(shape, n_mem, plane, planes, shape[3])
     outs = pl.pallas_call(
         functools.partial(cross_backward_kernel, n_mem, plane, planes, tuple(chunks), settled),
@@ -2407,7 +2409,7 @@
     rows_of = jnp.stack(
         [gain[0], bias[6], bias[5], gain[1], bias[7], bias[9], gain[2], bias[8]]
     )
-    layer_out, dca, dz2, feed_sums, hidden_sums, own_ffn_out, dw_ffn_in, dw_cross_out, dw_ffn_out = feed(
+    layer_out, dca, dz2, feed_sums, hidden_sums, own_ffn_out, dw_ffn_in, dw_cross_out = feed(
         n_mem,
         plane,
         cotangent,
@@ -2430,8 +2432,8 @@
         ca,
         dca,
         cross_lse,
-        [(dw_ffn_out, False, 2, 1), (dw_ffn_in, True, 2, 0), (dw_cross_out, False, 1, 0)],
-        [(own_ffn_out, 0)],
+        [(dw_ffn_in, True, 2), (dw_cross_out, False, 1)],
+        [(own_ffn_out, False)],
     )
     (dsa, dz1, middle_sums, enc_sum), (own_cross, own_so), _ = middle(
         n_mem,
@@ -2488,9 +2490,9 @@
             (sums[0], self_qkv),
             (sums[1], self_out),
             (sums[2], cross_qkv),
-            (ffn_sums[2], cross_out),
-            (ffn_sums[1], ffn_in),
-            (ffn_sums[0], ffn_out),
+            (ffn_sums[1], cross_out),
+            (ffn_sums[0], ffn_in),
+            (ffn_sums[2], ffn_out),
         ]
     )
     out_ffn_bias = vec[n_bias + n_gain : n_small].reshape(-1)

time: 553 us -> 542 us (0.980)
  Pallas kernels: 534 us -> 523 us
    pallas_call x1, Pallas kernels: 107 us -> 84.6 us  [cross_backward(): pl.pallas_call(functools.partial(cross_backward_kernel, n_mem, plane, pla...]
    pallas_call x1, Pallas kernels: 72.9 us -> 84.9 us  [feed(): pl.pallas_call(functools.partial(feed_kernel, n_mem, plane), in_specs=[VM...]
where the time goes in v4:
time: 542 us; the launch traced here: 533 us
  Pallas kernels  523 us (96%)
  local copies, waits for them, and re-layouts  5.6 us (1%)
    pallas_call x1, Pallas kernels, front(): pl.pallas_call(functools.partial(front_kernel, n_mem, plane, kinds, place...  121 us
    pallas_call x1, Pallas kernels, last(): pl.pallas_call(functools.partial(last_kernel, n_mem, plane, planes, settl...  91.9 us
    pallas_call x1, Pallas kernels, feed(): pl.pallas_call(functools.partial(feed_kernel, n_mem, plane), in_specs=[VM...  84.9 us
    pallas_call x1, Pallas kernels, cross_backward(): pl.pallas_call(functools.partial(cross_backward_kernel, n_mem, plane, pla...  84.6 us
    pallas_call x1, Pallas kernels, middle(): pl.pallas_call(functools.partial(middle_kernel, n_mem, plane, planes, set...  71.6 us
    pallas_call x1, Pallas kernels, cross_forward(): pl.pallas_call(functools.partial(cross_forward_kernel, n_mem, plane, kind...  56.2 us
    pallas_call x1, Pallas kernels, widen(): pl.pallas_call(widen_kernel, grid=(steps,), in_specs=blocks, out_specs=bl...  12.5 us

profile of v4, /device:TPU:0, one launch (start us, length us, event | category | flops | bytes accessed | tf_op | source)
XLA Modules:
  0.0 533.4 jit_solution(14714403913000034945)
XLA Ops:
  0.6 0.7 reshape.133
  1.3 1.3 fusion.4.small_ref
  2.7 121.4 %front.1 = (bf16[1024,1024]{1,0:T(8,128)(2,1)}, bf16[4,3,256,1024]{3,2,1,0:T(8,128)(2,1)}, s32[1,8]{1,0:T(1,128)}, bf16[4,32,256]{2,1,0:T(8,128)(2,1)}, bf16[3,4...) custom-call(bf16[2,256,1024]{2,1,0:T(8,128)(2,1)} %x_ref.1, ...), custom_call_target="tpu_custom_call" | custom-call | flops 5368709120 | bytes 41943040 | tf_op jit(solution)/shard_map/front/pallas_call | solution.py:784
  124.1 0.9 convert_element_type.8
  125.0 0.0 copy-start.2
  125.0 0.7 stack.3.rows_ref
  125.6 0.8 slice.114
  126.5 0.6 copy.31
  127.1 56.2 %cross_forward.1 = (bf16[1024,512]{1,0:T(8,128)(2,1)}, f32[4,2,1024]{2,1,0:T(2,128)}, bf16[1,4,4,64,2048]{4,3,2,1,0:T(8,128)(2,1)}, bf16[1,4,4,128,1024]{4,3,2,1,0:T(8,128)(2,1)}) custom-call(s32[8]{0:T(128)} %bitcast.83, bf16[1024,512]{1,0:T(8,128)(2,1)} %get-tuple-element.70.q_ref, bf16[12,256,512]{2,1,0:T(8,128)(2,1)} %get-tuple-element.71.k_ref, ...), custom_call_target="tpu_custom_call" | custom-call | flops 17179869184 | bytes 8388608 | tf_op jit(solution)/shard_map/cross_forward/pallas_call | solution.py:2090
  183.3 0.0 copy-done.2
  183.3 84.9 %feed.1 = (bf16[2,256,1024]{2,1,0:T(8,128)(2,1)}, bf16[1024,512]{1,0:T(8,128)(2,1)}, f32[512,1024]{1,0:T(8,128)}, f32[8,1024]{1,0:T(8,128)}, f32[1,2048]{1,0:T(1...) custom-call(bf16[2,256,1024]{2,1,0:T(8,128)(2,1)} %cot_ref.1, ...), custom_call_target="tpu_custom_call" | custom-call | flops 25769803776 | bytes 41943040 | tf_op jit(solution)/shard_map/feed/pallas_call | solution.py:1338
  268.3 0.0 copy-start.3
  268.3 84.6 %cross_backward.1 = (bf16[1024,512]{1,0:T(8,128)(2,1)}, bf16[2048,512]{1,0:T(8,128)(2,1)}, bf16[2048,512]{1,0:T(8,128)(2,1)}, bf16[1,4,64,4096]{3,2,1,0:T(8,128)...) custom-call(s32[8]{0:T(128)} %bitcast.84, bf16[1024,512]{1,0:T(8,128)(2,1)} %get-tuple-element.70.q_ref, ...), custom_call_target="tpu_custom_call" | custom-call | flops 42949672960 | bytes 17825792 | tf_op jit(solution)/shard_map/cross_backward/pallas_call | solution.py:2257
  352.9 0.0 copy-done.3
  352.9 0.1 fusion.6
  353.0 0.5 convert_element_type.9.member_ref
  353.5 0.6 select_reduce_fusion.slot_ref
  354.1 71.6 %middle.1 = (bf16[1024,512]{1,0:T(8,128)(2,1)}, f32[512,1024]{1,0:T(8,128)}, f32[8,1024]{1,0:T(8,128)}, bf16[3,256,1024]{2,1,0:T(8,128)(2,1)}, bf16[3,4,64,512]{...) custom-call(s32[12]{0:T(128)} %select_reduce_fusion.slot_ref, f32[12]{0:T(128)} %convert_element_type.9.member_ref, ...), custom_call_target="tpu_custom_call" | custom-call | flops 16106127360 | bytes 41943040 | tf_op jit(solution)/shard_map/middle/pallas_call | solution.py:1587
  425.7 91.9 %last.1 = (f32[32,256]{1,0:T(8,128)}, bf16[2,256,1024]{2,1,0:T(8,128)(2,1)}, bf16[3,4,64,1024]{3,2,1,0:T(8,128)(2,1)}, bf16[2,4,32,1024]{3,2,1,0:T(8,128)(2,1)}, bf16[3,4,64,1024]{3,2,1,0:T(8,128)(2,1)}) custom-call(bf16[1024,512]{1,0:T(8,128)(2,1)} %get-tuple-element.79.refs_0_, bf16[1024,512]{1,0:T(8,128)(2,1)} %get-tuple-element.80.refs_1_, ...), custom_call_target="tpu_custom_call" | custom-call | flops 42949672960 | bytes 41943040 | tf_op jit(solution)/shard_map/last/pallas_call | solution.py:1977
  517.6 0.0 copy-start.1
  517.6 0.0 copy-start
  517.6 12.5 %widen.1 = (f32[512,1024]{1,0:T(8,128)}, f32[768,1024]{1,0:T(8,128)}, f32[768,1024]{1,0:T(8,128)}, f32[256,1024]{1,0:T(8,128)}, f32[768,1024]{1,0:T(8,128)}, /*i...) custom-call(bf16[512,1024]{1,0:T(8,128)(2,1)} %bitcast.50, bf16[768,1024]{1,0:T(8,128)(2,1)} %bitcast.47, ...), custom_call_target="tpu_custom_call" | custom-call | bytes 33030144 | tf_op jit(solution)/shard_map/widen/pallas_call | solution.py:2320
  530.1 0.0 copy-done.1
  530.1 0.6 slice.103
  530.7 0.6 copy.32
  531.3 0.6 slice.104
  531.9 0.0 copy-done
  531.9 1.0 copy.38
  (6 shorter events, 0.1 us)
Async XLA Ops:
  125.0 58.3 %copy-start.2 = (f32[1,4,256]{2,0,1:T(1,128)}, f32[1,4,256]{2,0,1:T(1,128)S(1)}, u32[]{:S(2)}) copy-start(f32[1,4,256]{2,0,1:T(1,128)S(1)} %get-tuple-element.131) | copy-start | bytes 12292
  268.3 84.6 %copy-start.3 = (s32[1,8]{1,0:T(1,128)S(1)}, s32[1,8]{1,0:T(1,128)}, u32[]{:S(2)}) copy-start(s32[1,8]{1,0:T(1,128)} %get-tuple-element.69) | copy-start | bytes 100
  517.6 12.5 %copy-start.1 = (f32[32,256]{1,0:T(8,128)S(1)}, f32[32,256]{1,0:T(8,128)}, u32[]{:S(2)}) copy-start(f32[32,256]{1,0:T(8,128)} %get-tuple-element.123) | copy-start | bytes 98308
  517.6 14.3 %copy-start = (bf16[2,256,1024]{2,1,0:T(8,128)(2,1)S(1)}, bf16[2,256,1024]{2,1,0:T(8,128)(2,1)}, u32[]{:S(2)}) copy-start(bf16[2,256,1024]{2,1,0:T(8,128)(2,1)} %get-tuple-element.146) | copy-start | bytes 3145732

commit v5 on v3

--- a/solution.py
+++ b/solution.py
@@ -2162,7 +2162,7 @@
             for call in calls:
                 call()
 
-    plan = ((0, 2, 4, 7, 8), (2, 4, 6, 9, 10), (5, 7, 9, 12, 13), (8, 10, 11, 13, 14))
+    plan = ((0, 2, 5, 9, 10), (3, 5, 8, 12, 13), (6, 8, 11, 14, 15), (9, 10, 12, 15, 15))
     for i, (plane_sum, settle) in enumerate(zip(sums, settles)):
         start, middle, end, line, near = plan[i]
         at(start, plane_sum.start)
@@ -2172,7 +2172,7 @@
         at(near, settle.forward)
     for item in first:
         at(6, item.middle)
-        at(7, item.forward)
+        at(8, item.forward)
 
     @pl.when(passage == 0)
     def _():

time: 553 us -> 554 us (level)
  no operation moved by 1% of the time
where the time goes in v5:
time: 554 us; the launch traced here: 545 us
  Pallas kernels  535 us (97%)
  local copies, waits for them, and re-layouts  5.6 us (1%)
    pallas_call x1, Pallas kernels, front(): pl.pallas_call(functools.partial(front_kernel, n_mem, plane, kinds, place...  121 us
    pallas_call x1, Pallas kernels, cross_backward(): pl.pallas_call(functools.partial(cross_backward_kernel, n_mem, plane, pla...  103 us
    pallas_call x1, Pallas kernels, last(): pl.pallas_call(functools.partial(last_kernel, n_mem, plane, planes, settl...  92.8 us
    pallas_call x1, Pallas kernels, middle(): pl.pallas_call(functools.partial(middle_kernel, n_mem, plane, planes, set...  76.1 us
    pallas_call x1, Pallas kernels, feed(): pl.pallas_call(functools.partial(feed_kernel, n_mem, plane), in_specs=[VM...  72.9 us
    pallas_call x1, Pallas kernels, cross_forward(): pl.pallas_call(functools.partial(cross_forward_kernel, n_mem, plane, kind...  56.2 us
    pallas_call x1, Pallas kernels, widen(): pl.pallas_call(widen_kernel, grid=(steps,), in_specs=blocks, out_specs=bl...  12.5 us

profile of v5, /device:TPU:0, one launch (start us, length us, event | category | flops | bytes accessed | tf_op | source)
XLA Modules:
  0.0 545.3 jit_solution(12644766333730849657)
XLA Ops:
  0.6 0.7 reshape.133
  1.3 1.3 fusion.4.small_ref
  2.7 121.4 %front.1 = (bf16[1024,1024]{1,0:T(8,128)(2,1)}, bf16[4,3,256,1024]{3,2,1,0:T(8,128)(2,1)}, s32[1,8]{1,0:T(1,128)}, bf16[4,32,256]{2,1,0:T(8,128)(2,1)}, bf16[3,4...) custom-call(bf16[2,256,1024]{2,1,0:T(8,128)(2,1)} %x_ref.1, ...), custom_call_target="tpu_custom_call" | custom-call | flops 5368709120 | bytes 41943040 | tf_op jit(solution)/shard_map/front/pallas_call | solution.py:784
  124.1 0.9 convert_element_type.8
  125.0 0.0 copy-start.2
  125.0 0.7 stack.3.rows_ref
  125.6 0.8 slice.114
  126.5 0.6 copy.31
  127.1 56.2 %cross_forward.1 = (bf16[1024,512]{1,0:T(8,128)(2,1)}, f32[4,2,1024]{2,1,0:T(2,128)}, bf16[1,4,4,64,2048]{4,3,2,1,0:T(8,128)(2,1)}, bf16[1,4,4,128,1024]{4,3,2,1,0:T(8,128)(2,1)}) custom-call(s32[8]{0:T(128)} %bitcast.83, bf16[1024,512]{1,0:T(8,128)(2,1)} %get-tuple-element.71.q_ref, bf16[12,256,512]{2,1,0:T(8,128)(2,1)} %get-tuple-element.72.k_ref, ...), custom_call_target="tpu_custom_call" | custom-call | flops 17179869184 | bytes 8388608 | tf_op jit(solution)/shard_map/cross_forward/pallas_call | solution.py:2090
  183.3 0.0 copy-done.2
  183.3 72.9 %feed.1 = (bf16[2,256,1024]{2,1,0:T(8,128)(2,1)}, bf16[1024,512]{1,0:T(8,128)(2,1)}, f32[512,1024]{1,0:T(8,128)}, f32[8,1024]{1,0:T(8,128)}, f32[1,2048]{1,0:T(1...) custom-call(bf16[2,256,1024]{2,1,0:T(8,128)(2,1)} %cot_ref.1, ...), custom_call_target="tpu_custom_call" | custom-call | flops 25769803776 | bytes 41943040 | tf_op jit(solution)/shard_map/feed/pallas_call | solution.py:1338
  256.2 0.0 copy-start.3
  256.2 103.2 %cross_backward.1 = (bf16[1024,512]{1,0:T(8,128)(2,1)}, bf16[2048,512]{1,0:T(8,128)(2,1)}, bf16[2048,512]{1,0:T(8,128)(2,1)}, bf16[2,4,128,1024]{3,2,1,0:T(8,128...) custom-call(s32[8]{0:T(128)} %bitcast.84, bf16[1024,512]{1,0:T(8,128)(2,1)} %get-tuple-element.71.q_ref, ...), custom_call_target="tpu_custom_call" | custom-call | flops 42949672960 | bytes 17825792 | tf_op jit(solution)/shard_map/cross_backward/pallas_call | solution.py:2255
  359.4 0.0 copy-done.3
  359.4 0.1 fusion.6
  359.5 0.5 convert_element_type.9.member_ref
  360.0 0.6 select_reduce_fusion.slot_ref
  360.6 76.1 %middle.1 = (bf16[1024,512]{1,0:T(8,128)(2,1)}, f32[512,1024]{1,0:T(8,128)}, f32[8,1024]{1,0:T(8,128)}, bf16[3,256,1024]{2,1,0:T(8,128)(2,1)}, bf16[3,4,64,512]{...) custom-call(s32[12]{0:T(128)} %select_reduce_fusion.slot_ref, f32[12]{0:T(128)} %convert_element_type.9.member_ref, ...), custom_call_target="tpu_custom_call" | custom-call | flops 16106127360 | bytes 41943040 | tf_op jit(solution)/shard_map/middle/pallas_call | solution.py:1587
  436.8 92.8 %last.1 = (f32[32,256]{1,0:T(8,128)}, bf16[2,256,1024]{2,1,0:T(8,128)(2,1)}, bf16[3,4,64,1024]{3,2,1,0:T(8,128)(2,1)}, bf16[2,4,32,1024]{3,2,1,0:T(8,128)(2,1)}, bf16[3,4,64,1024]{3,2,1,0:T(8,128)(2,1)}) custom-call(bf16[1024,512]{1,0:T(8,128)(2,1)} %get-tuple-element.80.refs_0_, bf16[1024,512]{1,0:T(8,128)(2,1)} %get-tuple-element.81.refs_1_, ...), custom_call_target="tpu_custom_call" | custom-call | flops 42949672960 | bytes 41943040 | tf_op jit(solution)/shard_map/last/pallas_call | solution.py:1977
  529.5 0.0 copy-start.1
  529.6 0.0 copy-start
  529.6 12.5 %widen.1 = (f32[512,1024]{1,0:T(8,128)}, f32[768,1024]{1,0:T(8,128)}, f32[768,1024]{1,0:T(8,128)}, f32[256,1024]{1,0:T(8,128)}, f32[768,1024]{1,0:T(8,128)}, /*i...) custom-call(bf16[512,1024]{1,0:T(8,128)(2,1)} %bitcast.50, bf16[768,1024]{1,0:T(8,128)(2,1)} %bitcast.47, ...), custom_call_target="tpu_custom_call" | custom-call | bytes 33030144 | tf_op jit(solution)/shard_map/widen/pallas_call | solution.py:2318
  542.1 0.0 copy-done.1
  542.1 0.6 slice.103
  542.7 0.6 copy.32
  543.3 0.6 slice.104
  543.9 0.0 copy-done
  543.9 1.0 copy.38
  (6 shorter events, 0.1 us)
Async XLA Ops:
  125.0 58.3 %copy-start.2 = (f32[1,4,256]{2,0,1:T(1,128)}, f32[1,4,256]{2,0,1:T(1,128)S(1)}, u32[]{:S(2)}) copy-start(f32[1,4,256]{2,0,1:T(1,128)S(1)} %get-tuple-element.133) | copy-start | bytes 12292
  256.2 103.2 %copy-start.3 = (s32[1,8]{1,0:T(1,128)S(1)}, s32[1,8]{1,0:T(1,128)}, u32[]{:S(2)}) copy-start(s32[1,8]{1,0:T(1,128)} %get-tuple-element.70) | copy-start | bytes 100
  529.5 12.5 %copy-start.1 = (f32[32,256]{1,0:T(8,128)S(1)}, f32[32,256]{1,0:T(8,128)}, u32[]{:S(2)}) copy-start(f32[32,256]{1,0:T(8,128)} %get-tuple-element.125) | copy-start | bytes 98308
  529.6 14.3 %copy-start = (bf16[2,256,1024]{2,1,0:T(8,128)(2,1)S(1)}, bf16[2,256,1024]{2,1,0:T(8,128)(2,1)}, u32[]{:S(2)}) copy-start(bf16[2,256,1024]{2,1,0:T(8,128)(2,1)} %get-tuple-element.148) | copy-start | bytes 3145732

commit v6 on v4

--- a/solution.py
+++ b/solution.py
@@ -1254,7 +1254,8 @@
             part_vm[:, lanes] = grad[own:].astype(BF16)
             dz2_ref[:, lanes] += grad[:own]
         swap_dh2[i].start()
-    out_sum.middle()
+        if i == 0:
+            out_sum.middle()
     for copy in swap_dh2:
         copy.wait()
 

time: 542 us -> 542 us (level)
  no operation moved by 1% of the time
where the time goes in v6:
time: 542 us; the launch traced here: 533 us
  Pallas kernels  523 us (96%)
  local copies, waits for them, and re-layouts  5.6 us (1%)
    pallas_call x1, Pallas kernels, front(): pl.pallas_call(functools.partial(front_kernel, n_mem, plane, kinds, place...  121 us
    pallas_call x1, Pallas kernels, last(): pl.pallas_call(functools.partial(last_kernel, n_mem, plane, planes, settl...  91.9 us
    pallas_call x1, Pallas kernels, feed(): pl.pallas_call(functools.partial(feed_kernel, n_mem, plane), in_specs=[VM...  84.9 us
    pallas_call x1, Pallas kernels, cross_backward(): pl.pallas_call(functools.partial(cross_backward_kernel, n_mem, plane, pla...  84.6 us
    pallas_call x1, Pallas kernels, middle(): pl.pallas_call(functools.partial(middle_kernel, n_mem, plane, planes, set...  71.6 us
    pallas_call x1, Pallas kernels, cross_forward(): pl.pallas_call(functools.partial(cross_forward_kernel, n_mem, plane, kind...  56.2 us
    pallas_call x1, Pallas kernels, widen(): pl.pallas_call(widen_kernel, grid=(steps,), in_specs=blocks, out_specs=bl...  12.5 us

profile of v6, /device:TPU:0, one launch (start us, length us, event | category | flops | bytes accessed | tf_op | source)
XLA Modules:
  0.0 533.4 jit_solution(14075407906664702254)
XLA Ops:
  0.6 0.7 reshape.133
  1.3 1.3 fusion.4.small_ref
  2.7 121.4 %front.1 = (bf16[1024,1024]{1,0:T(8,128)(2,1)}, bf16[4,3,256,1024]{3,2,1,0:T(8,128)(2,1)}, s32[1,8]{1,0:T(1,128)}, bf16[4,32,256]{2,1,0:T(8,128)(2,1)}, bf16[3,4...) custom-call(bf16[2,256,1024]{2,1,0:T(8,128)(2,1)} %x_ref.1, ...), custom_call_target="tpu_custom_call" | custom-call | flops 5368709120 | bytes 41943040 | tf_op jit(solution)/shard_map/front/pallas_call | solution.py:784
  124.1 0.9 convert_element_type.8
  125.0 0.0 copy-start.2
  125.0 0.7 stack.3.rows_ref
  125.6 0.8 slice.114
  126.5 0.6 copy.31
  127.1 56.2 %cross_forward.1 = (bf16[1024,512]{1,0:T(8,128)(2,1)}, f32[4,2,1024]{2,1,0:T(2,128)}, bf16[1,4,4,64,2048]{4,3,2,1,0:T(8,128)(2,1)}, bf16[1,4,4,128,1024]{4,3,2,1,0:T(8,128)(2,1)}) custom-call(s32[8]{0:T(128)} %bitcast.83, bf16[1024,512]{1,0:T(8,128)(2,1)} %get-tuple-element.70.q_ref, bf16[12,256,512]{2,1,0:T(8,128)(2,1)} %get-tuple-element.71.k_ref, ...), custom_call_target="tpu_custom_call" | custom-call | flops 17179869184 | bytes 8388608 | tf_op jit(solution)/shard_map/cross_forward/pallas_call | solution.py:2091
  183.3 0.0 copy-done.2
  183.3 84.9 %feed.1 = (bf16[2,256,1024]{2,1,0:T(8,128)(2,1)}, bf16[1024,512]{1,0:T(8,128)(2,1)}, f32[512,1024]{1,0:T(8,128)}, f32[8,1024]{1,0:T(8,128)}, f32[1,2048]{1,0:T(1...) custom-call(bf16[2,256,1024]{2,1,0:T(8,128)(2,1)} %cot_ref.1, ...), custom_call_target="tpu_custom_call" | custom-call | flops 25769803776 | bytes 41943040 | tf_op jit(solution)/shard_map/feed/pallas_call | solution.py:1339
  268.3 0.0 copy-start.3
  268.3 84.6 %cross_backward.1 = (bf16[1024,512]{1,0:T(8,128)(2,1)}, bf16[2048,512]{1,0:T(8,128)(2,1)}, bf16[2048,512]{1,0:T(8,128)(2,1)}, bf16[1,4,64,4096]{3,2,1,0:T(8,128)...) custom-call(s32[8]{0:T(128)} %bitcast.84, bf16[1024,512]{1,0:T(8,128)(2,1)} %get-tuple-element.70.q_ref, ...), custom_call_target="tpu_custom_call" | custom-call | flops 42949672960 | bytes 17825792 | tf_op jit(solution)/shard_map/cross_backward/pallas_call | solution.py:2258
  352.9 0.0 copy-done.3
  352.9 0.1 fusion.6
  353.0 0.5 convert_element_type.9.member_ref
  353.5 0.6 select_reduce_fusion.slot_ref
  354.1 71.6 %middle.1 = (bf16[1024,512]{1,0:T(8,128)(2,1)}, f32[512,1024]{1,0:T(8,128)}, f32[8,1024]{1,0:T(8,128)}, bf16[3,256,1024]{2,1,0:T(8,128)(2,1)}, bf16[3,4,64,512]{...) custom-call(s32[12]{0:T(128)} %select_reduce_fusion.slot_ref, f32[12]{0:T(128)} %convert_element_type.9.member_ref, ...), custom_call_target="tpu_custom_call" | custom-call | flops 16106127360 | bytes 41943040 | tf_op jit(solution)/shard_map/middle/pallas_call | solution.py:1588
  425.7 91.9 %last.1 = (f32[32,256]{1,0:T(8,128)}, bf16[2,256,1024]{2,1,0:T(8,128)(2,1)}, bf16[3,4,64,1024]{3,2,1,0:T(8,128)(2,1)}, bf16[2,4,32,1024]{3,2,1,0:T(8,128)(2,1)}, bf16[3,4,64,1024]{3,2,1,0:T(8,128)(2,1)}) custom-call(bf16[1024,512]{1,0:T(8,128)(2,1)} %get-tuple-element.79.refs_0_, bf16[1024,512]{1,0:T(8,128)(2,1)} %get-tuple-element.80.refs_1_, ...), custom_call_target="tpu_custom_call" | custom-call | flops 42949672960 | bytes 41943040 | tf_op jit(solution)/shard_map/last/pallas_call | solution.py:1978
  517.6 0.0 copy-start.1
  517.6 0.0 copy-start
  517.6 12.5 %widen.1 = (f32[512,1024]{1,0:T(8,128)}, f32[768,1024]{1,0:T(8,128)}, f32[768,1024]{1,0:T(8,128)}, f32[256,1024]{1,0:T(8,128)}, f32[768,1024]{1,0:T(8,128)}, /*i...) custom-call(bf16[512,1024]{1,0:T(8,128)(2,1)} %bitcast.50, bf16[768,1024]{1,0:T(8,128)(2,1)} %bitcast.47, ...), custom_call_target="tpu_custom_call" | custom-call | bytes 33030144 | tf_op jit(solution)/shard_map/widen/pallas_call | solution.py:2321
  530.1 0.0 copy-done.1
  530.1 0.6 slice.103
  530.7 0.6 copy.32
  531.3 0.6 slice.104
  531.9 0.0 copy-done
  531.9 1.0 copy.38
  (6 shorter events, 0.1 us)
Async XLA Ops:
  125.0 58.3 %copy-start.2 = (f32[1,4,256]{2,0,1:T(1,128)}, f32[1,4,256]{2,0,1:T(1,128)S(1)}, u32[]{:S(2)}) copy-start(f32[1,4,256]{2,0,1:T(1,128)S(1)} %get-tuple-element.131) | copy-start | bytes 12292
  268.3 84.6 %copy-start.3 = (s32[1,8]{1,0:T(1,128)S(1)}, s32[1,8]{1,0:T(1,128)}, u32[]{:S(2)}) copy-start(s32[1,8]{1,0:T(1,128)} %get-tuple-element.69) | copy-start | bytes 100
  517.6 12.5 %copy-start.1 = (f32[32,256]{1,0:T(8,128)S(1)}, f32[32,256]{1,0:T(8,128)}, u32[]{:S(2)}) copy-start(f32[32,256]{1,0:T(8,128)} %get-tuple-element.123) | copy-start | bytes 98308
  517.6 14.3 %copy-start = (bf16[2,256,1024]{2,1,0:T(8,128)(2,1)S(1)}, bf16[2,256,1024]{2,1,0:T(8,128)(2,1)}, u32[]{:S(2)}) copy-start(bf16[2,256,1024]{2,1,0:T(8,128)(2,1)} %get-tuple-element.146) | copy-start | bytes 3145732
